TPU v7x, 128 devices: a whole 4x4x4 slice. The times are simulated.
128 devices in a mesh: dp: 16 (over y, x), tensor: 8 (over z, core).
Axes of the slice: x: 4, y: 4, z: 4, core: 2. Of those that a mesh axis runs over, the one named last changes fastest.
Arguments:
- tokens: bfloat16 [25216, 512], P(('dp', 'tensor')), may hold values from -6 to 6
- image_counts: int32 [16], P('dp'), may hold values from 1 to 8, 96 in all
- choices: int32 [25216, 2], P('dp'), may hold values from 0 to 31, all different within a row
- gain_attn: bfloat16 [512], P('dp'), may hold values from 0.25 to 1.75
- qkv_weight: bfloat16 [512, 1536], P('dp', 'tensor'), may hold values from -0.25 to 0.25
- out_weight: bfloat16 [512, 512], P('tensor', 'dp'), may hold values from -2 to 2
- gain_moe: bfloat16 [512], P('dp'), may hold values from 0.25 to 1.75
- router_weight: bfloat16 [512, 32], P('dp'), may hold values from -0.1875 to 0.1875
- expert_in: bfloat16 [32, 512, 2048], P(None, 'dp', 'tensor'), may hold values from -0.25 to 0.25
- expert_out: bfloat16 [32, 2048, 512], P(None, 'tensor', 'dp'), may hold values from -2 to 2
- cotangent: bfloat16 [25216, 512], P(('dp', 'tensor')), may hold values from -6 to 6
Outputs:
- output: bfloat16 [25216, 512], P(('dp', 'tensor'))
- tokens_grad: float32 [25216, 512], P(('dp', 'tensor'))
- gain_attn_grad: float32 [512], P('dp')
- qkv_weight_grad: float32 [512, 1536], P('dp', 'tensor')
- out_weight_grad: float32 [512, 512], P('tensor', 'dp')
- gain_moe_grad: float32 [512], P('dp')
- router_weight_grad: float32 [512, 32], P('dp')
- expert_in_grad: float32 [32, 512, 2048], P(None, 'dp', 'tensor')
- expert_out_grad: float32 [32, 2048, 512], P(None, 'tensor', 'dp')
Inputs may be any that keep to these rules, and one draw needn't show every extreme that they name: `image_counts`: each data group's images fill its first slots, and some group has all 8 filled. `choices`: a token's two experts differ.
All inputs are finite; a program needn't handle non-finite values.
Results may differ from a plain program's by a relative error of at most 0.02.
Values may be sent and summed in bfloat16 or wider, within the bound.
A program may use at most 128 MiB of HBM per device.

v0:
```python
import math

import jax
import jax.numpy as jnp
from jax import lax
from jax.sharding import PartitionSpec as P

DH = 64
L = 197
CAP = 123


norm_eps = 1e-05


def layer_norm(values, gain):
    center = values - jnp.mean(values, -1, keepdims=True)
    spread = jnp.mean(center * center, -1, keepdims=True)
    return center * lax.rsqrt(spread + norm_eps) * gain


def slot_numbers(choices, alive_rows, experts, capacity):
    expert_ids = jnp.arange(experts, dtype=jnp.int32)
    first_hits = ((choices[:, 0:1] == expert_ids) & alive_rows[:, None]).astype(jnp.int32)
    second_hits = ((choices[:, 1:2] == expert_ids) & alive_rows[:, None]).astype(jnp.int32)
    before_first = jnp.cumsum(first_hits, 0) - first_hits
    before_second = jnp.cumsum(second_hits, 0) - second_hits + jnp.sum(first_hits, 0)
    places = jnp.stack(
        [jnp.sum(before_first * first_hits, 1), jnp.sum(before_second * second_hits, 1)], 1
    )
    kept_pairs = alive_rows[:, None] & (places < capacity)
    slot_index = jnp.where(kept_pairs, places, capacity)
    return (kept_pairs, slot_index)


def contract_rows(left, right):
    return lax.dot_general(
        left, right, (((0,), (0,)), ((), ())), preferred_element_type=jnp.float32
    )


def contract_cols(left, right):
    return lax.dot_general(
        left, right, (((1,), (1,)), ((), ())), preferred_element_type=jnp.float32
    )


def body(
    tokens,
    image_counts,
    choices,
    gain_attn,
    qkv_weight,
    out_weight,
    gain_moe,
    router_weight,
    expert_in,
    expert_out,
    cotangent,
):
    highest = lax.Precision.HIGHEST
    own_rows = tokens.shape[0]
    width = tokens.shape[1]
    group_rows = choices.shape[0]
    slots_here = group_rows // L
    heads_here = qkv_weight.shape[1] // (3 * DH)
    experts = router_weight.shape[1]
    scale = 1.0 / math.sqrt(DH)
    start_row = lax.axis_index("tensor") * own_rows
    alive_group = jnp.arange(group_rows, dtype=jnp.int32) // L < image_counts[0]
    kept_pairs, slot_index = slot_numbers(choices, alive_group, experts, CAP)
    safe_slot = jnp.minimum(slot_index, CAP - 1)
    kept_float = kept_pairs.astype(jnp.float32)
    own_alive = lax.dynamic_slice_in_dim(alive_group, start_row, own_rows, 0).astype(jnp.float32)
    own_kept = lax.dynamic_slice_in_dim(kept_float, start_row, own_rows, 0)
    own_choices = lax.dynamic_slice_in_dim(choices, start_row, own_rows, 0)
    gain_one, qkv_full, out_full = (
        lax.all_gather(gain_attn, "dp", axis=0, tiled=True),
        lax.all_gather(qkv_weight, "dp", axis=0, tiled=True),
        lax.all_gather(out_weight, "dp", axis=1, tiled=True),
    )
    gain_two, router_full, first_full, second_full = (
        lax.all_gather(gain_moe, "dp", axis=0, tiled=True),
        lax.all_gather(router_weight, "dp", axis=0, tiled=True),
        lax.all_gather(expert_in, "dp", axis=1, tiled=True),
        lax.all_gather(expert_out, "dp", axis=2, tiled=True),
    )
    token_vals = tokens.astype(jnp.float32)
    normed_one = layer_norm(token_vals, gain_one.astype(jnp.float32)).astype(jnp.bfloat16)
    qkv_use, out_use = (qkv_full, out_full)
    attn_input = lax.all_gather(normed_one, "tensor", axis=0, tiled=True)
    attn_count = slots_here * L
    qkv_all = jnp.dot(attn_input, qkv_use, preferred_element_type=jnp.float32).astype(jnp.bfloat16)
    qkv_all = qkv_all.reshape(slots_here, L, heads_here, 3, DH)
    queries = qkv_all[:, :, :, 0]
    keys_all = qkv_all[:, :, :, 1]
    values_all = qkv_all[:, :, :, 2]
    scores = (
        jnp.einsum("aqhd,akhd->ahqk", queries, keys_all, preferred_element_type=jnp.float32) * scale
    )
    log_total = jax.nn.logsumexp(scores, -1, keepdims=True)
    probs_low = jnp.exp(scores - log_total).astype(jnp.bfloat16)
    mixed = jnp.einsum("ahqk,akhd->aqhd", probs_low, values_all, preferred_element_type=jnp.float32)
    mixed = mixed.reshape(attn_count, heads_here * DH).astype(jnp.bfloat16)
    projected = jnp.dot(mixed, out_use, preferred_element_type=jnp.float32)
    attn_rows = lax.psum_scatter(projected, "tensor", scatter_dimension=0, tiled=True)
    resid = token_vals + attn_rows
    gain_two_vals = gain_two.astype(jnp.float32)
    normed_two = layer_norm(resid, gain_two_vals).astype(jnp.bfloat16)
    router = jax.nn.softmax(
        jnp.dot(normed_two, router_full, preferred_element_type=jnp.float32), -1
    )
    gates_own = (jnp.take_along_axis(router, own_choices, 1) * own_kept).astype(jnp.bfloat16)
    moe_inputs, gates_all = (
        lax.all_gather(normed_two, "tensor", axis=0, tiled=True),
        lax.all_gather(gates_own, "tensor", axis=0, tiled=True),
    )
    spread_rows = jnp.broadcast_to(moe_inputs[:, None, :], (group_rows, 2, width))
    bucket = (
        jnp.zeros((experts, CAP, width), jnp.bfloat16)
        .at[choices, slot_index]
        .set(spread_rows, mode="drop")
    )
    inner = jnp.einsum("ecd,edf->ecf", bucket, first_full, preferred_element_type=jnp.float32)
    activ = jax.nn.gelu(inner, approximate=True).astype(jnp.bfloat16)
    result = jnp.einsum("ecf,efd->ecd", activ, second_full, preferred_element_type=jnp.float32)
    picked = result[choices, safe_slot]
    gate_vals = gates_all.astype(jnp.float32)
    combined = jnp.sum(gate_vals[:, :, None] * picked, 1)
    moe_rows = lax.psum_scatter(
        combined.astype(jnp.bfloat16), "tensor", scatter_dimension=0, tiled=True
    ).astype(jnp.float32)
    output = ((resid + moe_rows) * own_alive[:, None]).astype(jnp.bfloat16)
    gain_two, router_full, first_full, second_full = (
        lax.all_gather(gain_moe, "dp", axis=0, tiled=True),
        lax.all_gather(router_weight, "dp", axis=0, tiled=True),
        lax.all_gather(expert_in, "dp", axis=1, tiled=True),
        lax.all_gather(expert_out, "dp", axis=2, tiled=True),
    )
    gain_two_vals = gain_two.astype(jnp.float32)
    grad_masked = cotangent.astype(jnp.float32) * own_alive[:, None]
    grad_low = grad_masked.astype(jnp.bfloat16)
    grad_all = lax.all_gather(grad_low, "tensor", axis=0, tiled=True)
    grad_vals = grad_all.astype(jnp.float32)
    pair_grads = gate_vals[:, :, None] * grad_vals[:, None, :]
    result_grad = (
        jnp.zeros((experts, CAP, width), jnp.float32)
        .at[choices, slot_index]
        .set(pair_grads, mode="drop")
    )
    result_grad = result_grad.astype(jnp.bfloat16)
    gate_grads = jnp.sum(grad_vals[:, None, :] * picked, -1)
    second_grad = jnp.einsum("ecf,ecd->efd", activ, result_grad, preferred_element_type=jnp.float32)
    activ_grad = jnp.einsum(
        "ecd,efd->ecf", result_grad, second_full, preferred_element_type=jnp.float32
    )
    _, gelu_back = jax.vjp(lambda arg: jax.nn.gelu(arg, approximate=True), inner)
    inner_grad = gelu_back(activ_grad)[0].astype(jnp.bfloat16)
    first_grad = jnp.einsum("ecd,ecf->edf", bucket, inner_grad, preferred_element_type=jnp.float32)
    bucket_grad = jnp.einsum(
        "ecf,edf->ecd", inner_grad, first_full, preferred_element_type=jnp.float32
    )
    token_terms = jnp.sum(bucket_grad[choices, safe_slot] * kept_float[:, :, None], 1)
    normed_grad, gate_grad_own = (
        lax.psum_scatter(
            token_terms.astype(jnp.bfloat16), "tensor", scatter_dimension=0, tiled=True
        ).astype(jnp.float32),
        lax.psum_scatter(
            gate_grads.astype(jnp.bfloat16), "tensor", scatter_dimension=0, tiled=True
        ).astype(jnp.float32),
    )
    expert_ids = jnp.arange(experts, dtype=jnp.int32)
    one_hot = (own_choices[:, :, None] == expert_ids).astype(jnp.float32)
    router_grad = jnp.sum(one_hot * (gate_grad_own * own_kept)[:, :, None], 1)
    logit_grad = router * (router_grad - jnp.sum(router_grad * router, -1, keepdims=True))
    router_vals = router_full.astype(jnp.float32)
    normed_grad = normed_grad + jnp.dot(logit_grad, router_vals.T, precision=highest)
    router_weight_part = jnp.dot(normed_two.astype(jnp.float32).T, logit_grad, precision=highest)
    _, norm_two_back = jax.vjp(layer_norm, resid, gain_two_vals)
    resid_norm_grad, gain_two_part = norm_two_back(normed_grad)
    resid_grad = grad_masked + resid_norm_grad
    resid_low = resid_grad.astype(jnp.bfloat16)
    attn_grad = lax.all_gather(resid_low, "tensor", axis=0, tiled=True)
    out_grad = contract_rows(mixed, attn_grad)
    mixed_grad = contract_cols(attn_grad, out_use).astype(jnp.bfloat16)
    mixed_heads = mixed_grad.reshape(slots_here, L, heads_here, DH)
    probs_full = jnp.exp(
        jnp.einsum("aqhd,akhd->ahqk", queries, keys_all, preferred_element_type=jnp.float32) * scale
        - log_total
    )
    probs_grad = jnp.einsum(
        "aqhd,akhd->ahqk", mixed_heads, values_all, preferred_element_type=jnp.float32
    )
    score_grad = probs_full * (probs_grad - jnp.sum(probs_full * probs_grad, -1, keepdims=True))
    score_grad = score_grad.astype(jnp.bfloat16)
    query_grad = (
        jnp.einsum("ahqk,akhd->aqhd", score_grad, keys_all, preferred_element_type=jnp.float32)
        * scale
    )
    key_grad = (
        jnp.einsum("ahqk,aqhd->akhd", score_grad, queries, preferred_element_type=jnp.float32)
        * scale
    )
    value_grad = jnp.einsum(
        "ahqk,aqhd->akhd", probs_low, mixed_heads, preferred_element_type=jnp.float32
    )
    qkv_grad = (
        jnp.stack([query_grad, key_grad, value_grad], 3)
        .reshape(attn_count, heads_here * 3 * DH)
        .astype(jnp.bfloat16)
    )
    qkv_weight_part = contract_rows(attn_input, qkv_grad)
    normed_one_terms = contract_cols(qkv_grad, qkv_use)
    normed_one_grad = lax.psum_scatter(
        normed_one_terms.astype(jnp.bfloat16), "tensor", scatter_dimension=0, tiled=True
    ).astype(jnp.float32)
    _, norm_one_back = jax.vjp(layer_norm, token_vals, gain_one.astype(jnp.float32))
    token_norm_grad, gain_one_part = norm_one_back(normed_one_grad)
    tokens_grad = resid_grad + token_norm_grad
    qkv_sum, out_sum, first_sum, second_sum = (
        lax.psum_scatter(
            qkv_weight_part.astype(jnp.bfloat16), "dp", scatter_dimension=0, tiled=True
        ).astype(jnp.float32),
        lax.psum_scatter(
            out_grad.astype(jnp.bfloat16), "dp", scatter_dimension=1, tiled=True
        ).astype(jnp.float32),
        lax.psum_scatter(
            first_grad.astype(jnp.bfloat16), "dp", scatter_dimension=1, tiled=True
        ).astype(jnp.float32),
        lax.psum_scatter(
            second_grad.astype(jnp.bfloat16), "dp", scatter_dimension=2, tiled=True
        ).astype(jnp.float32),
    )
    gain_one_all, gain_two_all, router_all = lax.psum(
        (gain_one_part, gain_two_part, router_weight_part), ("dp", "tensor")
    )
    shard_rows = gain_attn.shape[0]
    shard_start = lax.axis_index("dp") * shard_rows
    gain_one_sum = lax.dynamic_slice_in_dim(gain_one_all, shard_start, shard_rows, 0)
    gain_two_sum = lax.dynamic_slice_in_dim(gain_two_all, shard_start, shard_rows, 0)
    router_sum = lax.dynamic_slice_in_dim(router_all, shard_start, shard_rows, 0)
    return (
        output,
        tokens_grad,
        gain_one_sum,
        qkv_sum,
        out_sum,
        gain_two_sum,
        router_sum,
        first_sum,
        second_sum,
    )


def solution(mesh):
    in_specs = (
        P(("dp", "tensor"), None),
        P("dp"),
        P("dp", None),
        P("dp"),
        P("dp", "tensor"),
        P("tensor", "dp"),
        P("dp"),
        P("dp", None),
        P(None, "dp", "tensor"),
        P(None, "tensor", "dp"),
        P(("dp", "tensor"), None),
    )
    out_specs = (
        P(("dp", "tensor"), None),
        P(("dp", "tensor"), None),
        P("dp"),
        P("dp", "tensor"),
        P("tensor", "dp"),
        P("dp"),
        P("dp", None),
        P(None, "dp", "tensor"),
        P(None, "tensor", "dp"),
    )
    return jax.shard_map(body, mesh=mesh, in_specs=in_specs, out_specs=out_specs, check_vma=False)
```

profile of v0, /device:TPU:1, one launch (start us, length us, event | category | flops | bytes accessed | tf_op | source)
XLA Modules:
  0.0 1081.2 jit_solution(127695450321536617)
XLA Ops:
  10.8 34.3 %all-reduce.15 = (bf16[512]{0:T(512)(128)(2,1)S(1)}, bf16[512]{0:T(512)(128)(2,1)S(1)}) all-reduce(bf16[512]{0:T(512)(128)(2,1)S(1)} %dynamic-update-slice, bf16[512]{0:T(512)(128)(2,1)S(1)} %dynamic-update-slice.1), channel_id=1, replica_groups=mesh['dp'=16,'tensor'=8] {'dp'}, use_global_device_ids=true, to_apply=%add.2 | all-reduce | flops 1024 | bytes 4096
  51.7 16.6 %all_gather.42 = bf16[512,192]{1,0:T(8,128)(2,1)S(1)} all-gather(bf16[32,192]{1,0:T(8,128)(2,1)} %param.15), channel_id=1, replica_groups=mesh['dp'=16,'tensor'=8] {'dp'}, dimensions={0}, use_global_device_ids=true | all-gather | bytes 208896 | tf_op jit(solution)/shard_map/all_gather | solution.py:79
  68.3 19.3 %all_gather.43 = bf16[64,512]{0,1:T(8,128)(2,1)} all-gather(bf16[64,32]{0,1:T(8,128)(2,1)} %param.16), channel_id=1, replica_groups=mesh['dp'=16,'tensor'=8] {'dp'}, dimensions={1}, use_global_device_ids=true | all-gather | bytes 69632 | tf_op jit(solution)/shard_map/all_gather | solution.py:80
  95.6 40.5 %fusion = f32[200,512]{1,0:T(8,128)S(1)} fusion(f32[1576,512]{1,0:T(8,128)} %fusion.78), kind=kCustom, calls=%all-reduce-scatter | all-reduce-scatter fusion | flops 819201 | bytes 3637760
  148.3 9.1 reduce-window.16
  159.0 9.1 reduce-window.14
  172.1 19.2 %all_gather.45 = bf16[512,32]{1,0:T(8,128)(2,1)} all-gather(bf16[32,32]{1,0:T(8,128)(2,1)S(1)} %copy-done.30), channel_id=1, replica_groups=mesh['dp'=16,'tensor'=8] {'dp'}, dimensions={0}, use_global_device_ids=true | all-gather | bytes 34816 | tf_op jit(solution)/shard_map/all_gather | solution.py:84
  204.1 17.1 %all-gather.1 = bf16[8,197,2]{1,2,0:T(2,128)(2,1)S(1)} all-gather(bf16[1,197,2]{1,2,0:T(2,128)(2,1)S(1)} %fusion.67), channel_id=1, replica_groups=mesh['dp'=16,'tensor'=8] {'tensor'}, dimensions={0}, use_global_device_ids=true | all-gather | bytes 7092 | tf_op jit(solution)/shard_map/all_gather | solution.py:116
  225.7 12.9 %broadcast_in_dim.28 = bf16[1576,2,512]{2,1,0:T(2,128)(2,1)} broadcast(bf16[1576,512]{1,0:T(8,128)(2,1)} %reshape.476), dimensions={0,2} | broadcast | bytes 4841472 | tf_op jit(solution)/shard_map/broadcast_in_dim | solution.py:118
  246.2 20.8 %scatter_custom_fusion = bf16[3936,512]{1,0:T(8,128)(2,1)} fusion(s32[3152]{0:T(1024)} %reshape.448, bf16[3152,512]{1,0:T(8,128)(2,1)} %reshape.450, bf16[]{:T(256)} %constant.84.clone.1), kind=kCustom, calls=%fused_computation.26 | custom fusion | bytes 4030976
  274.9 8.5 fusion.79
  283.4 32.6 %all-gather.14.cloned.1.call-done = bf16[32,256,512]{1,2,0:T(8,128)(2,1)} async-done(((bf16[32,256,32]{1,2,0:T(8,128)(2,1)}), bf16[32,256,512]{1,2,0:T(8,128)(2,1)}) %all-gather.14.cloned.1.call-update) | async-done | bytes 8388624 | tf_op jit(solution)/shard_map/all_gather | solution.py:86
  331.4 47.3 %gather_fusion = f32[3152,512]{1,0:T(8,128)} fusion(f32[32,123,512]{2,0,1:T(8,128)} %copy.164, s32[3152]{0:T(1024)S(1)} %reshape.430), kind=kCustom, calls=%fused_computation | custom fusion | bytes 12935808 | tf_op jit(solution)/shard_map/gather | solution.py:127
  378.7 8.7 reshape.433
  387.4 25.4 %multiply_reduce_fusion = (bf16[1576,2]{1,0:T(8,128)(2,1)}, bf16[1576,512]{1,0:T(8,128)(2,1)}, f32[1576,2,512]{2,1,0:T(2,128)}) fusion(f32[1576,2,512]{2,1,0:T(2,128)} %reshape.433, f32[1576,512]{1,0:T(8,128)} %reshape.482, f32[1576,2]{1,0:T(8,128)} %copy.160), kind=kLoop, calls=%fused_computation.7 | loop fusion | flops 7259056 | bytes 17770976 | tf_op jit(solution)/shard_map/reduce_sum | solution.py:152
  412.8 8.5 reshape.456
  421.3 22.1 %scatter_custom_fusion.1 = f32[3936,512]{1,0:T(8,128)} fusion(s32[3152]{0:T(1024)} %reshape.448, f32[3152,512]{1,0:T(8,128)} %reshape.456, f32[]{:T(128)} %constant.29.clone.1), kind=kCustom, calls=%fused_computation.20 | custom fusion | bytes 8061440
  449.2 8.1 copy.176
  457.3 9.4 fusion.11
  481.5 47.6 %gather_fusion.1 = f32[3152,512]{1,0:T(8,128)} fusion(f32[32,123,512]{2,0,1:T(8,128)} %copy.166, s32[3152]{0:T(1024)S(1)} %reshape.430), kind=kCustom, calls=%fused_computation.1 | custom fusion | bytes 12935808 | tf_op jit(solution)/shard_map/gather | solution.py:163
  529.0 8.3 reshape.439
  537.3 12.4 %multiply_reduce_fusion.1 = bf16[1576,512]{1,0:T(8,128)(2,1)} fusion(f32[1576,2,512]{2,1,0:T(2,128)} %reshape.439, f32[1576,2]{1,0:T(8,128)S(1)} %copy.167), kind=kLoop, calls=%fused_computation.8 | loop fusion | flops 2420736 | bytes 8081728 | tf_op jit(solution)/shard_map/reduce_sum | solution.py:163
  549.8 18.2 %fusion.72 = (bf16[208,2]{1,0:T(8,128)(2,1)S(1)}, bf16[200,512]{1,0:T(8,128)(2,1)S(1)}) fusion(bf16[1576,2]{1,0:T(8,128)(2,1)} %get-tuple-element.9, bf16[1576,512]{1,0:T(8,128)(2,1)} %multiply_reduce_fusion.1), kind=kCustom, calls=%all-reduce-scatter.6 | all-reduce-scatter fusion | flops 822530 | bytes 1826272
  582.6 22.1 %all-gather.22.cloned.1.call-done = bf16[8,197,512]{2,1,0:T(8,128)(2,1)} async-done(((bf16[1,197,512]{2,1,0:T(8,128)(2,1)}), bf16[8,197,512]{2,1,0:T(8,128)(2,1)}) %all-gather.22.cloned.1.call-update) | async-done | bytes 1613840 | tf_op jit(solution)/shard_map/all_gather | solution.py:183
  623.5 8.4 convolution_convert_fusion.1
  632.0 9.1 convolution_convert_fusion
  644.1 21.3 %fusion.71 = (bf16[200,512]{1,0:T(8,128)(2,1)S(1)}, bf16[200,512]{1,0:T(8,128)(2,1)S(1)}) fusion(bf16[1576,512]{1,0:T(8,128)(2,1)} %get-tuple-element.10, bf16[1576,512]{1,0:T(8,128)(2,1)} %convolution_convert_fusion.2), kind=kCustom, calls=%all-reduce-scatter.5 | all-reduce-scatter fusion | flops 1638401 | bytes 3637760
  669.8 80.9 %all-reduce.20.cloned.1.call-done = f32[512,32]{1,0:T(8,128)} async-done(((f32[512,32]{1,0:T(8,128)}), f32[512,32]{1,0:T(8,128)}) %all-reduce.20.cloned.1.call-update) | async-done | bytes 65552 | tf_op jit(solution)/shard_map/psum | solution.py:234
  756.2 64.4 %all-reduce.14 = (f32[512]{0:T(512)S(1)}, f32[512]{0:T(512)S(1)}) all-reduce(f32[512]{0:T(512)S(1)} %get-tuple-element.13, f32[512]{0:T(512)S(1)} %get-tuple-element.11), channel_id=1, replica_groups=mesh['dp'=16,'tensor'=8] {'dp','tensor'}, use_global_device_ids=true, to_apply=%region_33.34 | all-reduce | flops 1024 | bytes 8192 | tf_op jit(solution)/shard_map/psum | solution.py:234
  824.5 72.2 %reduce-scatter.15.cloned.1.call-done = bf16[32,192]{1,0:T(8,128)(2,1)} async-done(((bf16[512,192]{1,0:T(8,128)(2,1)}), bf16[32,192]{1,0:T(8,128)(2,1)}) %reduce-scatter.15.cloned.1.call-update) | async-done | bytes 12304 | tf_op jit(solution)/shard_map/reduce_scatter | solution.py:221
  898.1 86.4 %reduce-scatter.19.cloned.1.call-done = bf16[32,32,256]{2,1,0:T(8,128)(2,1)} async-done(((bf16[32,512,256]{2,1,0:T(8,128)(2,1)}), bf16[32,32,256]{2,1,0:T(8,128)(2,1)}) %reduce-scatter.19.cloned.1.call-update) | async-done | bytes 524304 | tf_op jit(solution)/shard_map/reduce_scatter | solution.py:227
  986.6 85.5 %reduce-scatter.21.cloned.1.call-done = bf16[32,256,32]{1,2,0:T(8,128)(2,1)} async-done(((bf16[32,256,512]{1,2,0:T(8,128)(2,1)}), bf16[32,256,32]{1,2,0:T(8,128)(2,1)}) %reduce-scatter.21.cloned.1.call-update) | async-done | bytes 524304 | tf_op jit(solution)/shard_map/reduce_scatter | solution.py:230
  (242 shorter events, 157.0 us)
Async XLA Ops:
  7.2 80.5 %all-gather.16.cloned.1.call-start = ((), (), s32[]{:S(2)}) async-start(), calls=%async_computation.11 | async-start | bytes 1843200 | tf_op jit(solution)/shard_map/all_gather | solution.py:91
  45.1 42.5 %copy-start.20 = (f32[512]{0:T(512)}, f32[512]{0:T(512)S(1)}, u32[]{:S(2)}) copy-start(f32[512]{0:T(512)S(1)} %convert_element_type.147) | copy-start | bytes 6148
  46.2 41.4 %copy-start.22 = (f32[197]{0:T(256)}, f32[197]{0:T(256)S(1)}, u32[]{:S(2)}) copy-start(f32[197]{0:T(256)S(1)} %broadcast_multiply_fusion.2) | copy-start | bytes 2368
  47.3 40.3 %copy-start.26 = (f32[197]{0:T(256)}, f32[197]{0:T(256)S(1)}, u32[]{:S(2)}) copy-start(f32[197]{0:T(256)S(1)} %fusion.31) | copy-start | bytes 2368
  47.4 40.3 %copy-start.24 = (f32[197]{0:T(256)}, f32[197]{0:T(256)S(1)}, u32[]{:S(2)}) copy-start(f32[197]{0:T(256)S(1)} %fusion.68) | copy-start | bytes 2368
  49.1 142.2 %all-gather.20.cloned.1.call-start = ((), (), s32[]{:S(2)}) async-start(), calls=%async_computation.13 | async-start | bytes 1843200 | tf_op jit(solution)/shard_map/all_gather | solution.py:143
  51.7 170.9 %all-gather.18.cloned.1.call-start = ((), (), s32[]{:S(2)}) async-start(), calls=%async_computation.12 | async-start | bytes 1843200 | tf_op jit(solution)/shard_map/all_gather | solution.py:115
  92.8 47.7 %copy-start.33 = (u32[128]{0:T(128)S(1)}, u32[128]{0:T(128)}, u32[]{:S(2)}) copy-start(u32[128]{0:T(128)} %constant.172) | copy-start | bytes 1540
  93.2 51.9 %copy-start.10 = (bf16[1576,64]{0,1:T(8,128)(2,1)}, bf16[1576,64]{0,1:T(8,128)(2,1)S(1)}, u32[]{:S(2)}) copy-start(bf16[1576,64]{0,1:T(8,128)(2,1)S(1)} %convert_element_type.154) | copy-start | bytes 605188
  93.2 50.7 %copy-start.1 = (bf16[197,512]{1,0:T(8,128)(2,1)S(1)}, bf16[197,512]{1,0:T(8,128)(2,1)}, u32[]{:S(2)}) copy-start(bf16[197,512]{1,0:T(8,128)(2,1)} %param.11) | copy-start | bytes 605188
  95.5 51.8 %copy-start.19 = (s32[1576,2]{0,1:T(2,128)S(1)}, s32[1576,2]{0,1:T(2,128)}, u32[]{:S(2)}) copy-start(s32[1576,2]{0,1:T(2,128)} %param.13) | copy-start | bytes 37828
  136.1 5.7 collective-permute-start
  146.2 128.8 %all-gather.12.cloned.1.call-start = ((), (), s32[]{:S(2)}) async-start(), calls=%async_computation.4 | async-start | bytes 8912896 | tf_op jit(solution)/shard_map/all_gather | solution.py:85
  146.7 169.3 %all-gather.14.cloned.1.call-start = ((), (), s32[]{:S(2)}) async-start(), calls=%async_computation.5 | async-start | bytes 8912896 | tf_op jit(solution)/shard_map/all_gather | solution.py:86
  147.3 457.3 %all-gather.22.cloned.1.call-start = ((), (), s32[]{:S(2)}) async-start(), calls=%async_computation.14 | async-start | bytes 1843200 | tf_op jit(solution)/shard_map/all_gather | solution.py:183
  549.8 29.5 %copy-start.12 = (bf16[197,512]{1,0:T(8,128)(2,1)S(1)}, bf16[197,512]{1,0:T(8,128)(2,1)}, u32[]{:S(2)}) copy-start(bf16[197,512]{1,0:T(8,128)(2,1)} %param.21) | copy-start | bytes 605188
  568.0 5.5 collective-permute-start.3
  571.5 3.8 collective-permute-start.2
  573.9 33.8 %copy-start.17 = (bf16[64,512]{0,1:T(8,128)(2,1)S(1)}, bf16[64,512]{0,1:T(8,128)(2,1)}, u32[]{:S(2)}) copy-start(bf16[64,512]{0,1:T(8,128)(2,1)} %all_gather.43) | copy-start | bytes 196612
  580.1 170.6 %all-reduce.20.cloned.1.call-start = ((), (), s32[]{:S(2)}) async-start(), calls=%async_computation.8 | async-start | bytes 524288 | tf_op jit(solution)/shard_map/psum | solution.py:234
  582.3 241.0 %reduce-scatter.17.cloned.1.call-start = ((), (), s32[]{:S(2)}) async-start(), calls=%async_computation.7 | async-start | bytes 139264 | tf_op jit(solution)/shard_map/reduce_scatter | solution.py:224
  620.9 275.9 %reduce-scatter.15.cloned.1.call-start = ((), (), s32[]{:S(2)}) async-start(), calls=%async_computation.6 | async-start | bytes 278528 | tf_op jit(solution)/shard_map/reduce_scatter | solution.py:221
  623.4 361.0 %reduce-scatter.19.cloned.1.call-start = ((), (), s32[]{:S(2)}) async-start(), calls=%async_computation.9 | async-start | bytes 8912896 | tf_op jit(solution)/shard_map/reduce_scatter | solution.py:227
  631.9 440.1 %reduce-scatter.21.cloned.1.call-start = ((), (), s32[]{:S(2)}) async-start(), calls=%async_computation.10 | async-start | bytes 8912896 | tf_op jit(solution)/shard_map/reduce_scatter | solution.py:230
  641.1 114.4 %copy-start.2 = (bf16[197,512]{1,0:T(8,128)(2,1)S(1)}, bf16[197,512]{1,0:T(8,128)(2,1)}, u32[]{:S(2)}) copy-start(bf16[197,512]{1,0:T(8,128)(2,1)} %param.11) | copy-start | bytes 605188
  641.2 114.4 %copy-start.21 = (f32[512]{0:T(512)S(1)}, f32[512]{0:T(512)}, u32[]{:S(2)}) copy-start(f32[512]{0:T(512)} %copy-done.20) | copy-start | bytes 6148
  641.2 114.4 %copy-start.23 = (f32[197]{0:T(256)S(1)}, f32[197]{0:T(256)}, u32[]{:S(2)}) copy-start(f32[197]{0:T(256)} %copy-done.22) | copy-start | bytes 2368
  641.2 114.6 %copy-start.27 = (f32[197]{0:T(256)S(1)}, f32[197]{0:T(256)}, u32[]{:S(2)}) copy-start(f32[197]{0:T(256)} %copy-done.26) | copy-start | bytes 2368
  641.2 114.7 %copy-start.25 = (f32[197]{0:T(256)S(1)}, f32[197]{0:T(256)}, u32[]{:S(2)}) copy-start(f32[197]{0:T(256)} %copy-done.24) | copy-start | bytes 2368
  641.2 180.9 %copy-start.13 = (bf16[197,512]{1,0:T(8,128)(2,1)S(1)}, bf16[197,512]{1,0:T(8,128)(2,1)}, u32[]{:S(2)}) copy-start(bf16[197,512]{1,0:T(8,128)(2,1)} %param.21) | copy-start | bytes 605188
  665.4 89.8 %collective-permute-start.4 = (bf16[21,512]{1,0:T(8,128)(2,1)S(1)}, bf16[21,512]{1,0:T(8,128)(2,1)S(1)}, u32[]{:S(2)}, u32[]{:S(2)}) collective-permute-start(bf16[21,512]{1,0:T(8,128)(2,1)S(1)} %slice.63), channel_id=1, source_target_pairs={{0,1},{1,2},{2,3},{3,4},{4,5},{5,6},{6,7},{8,9},{9,10},{10,11},{11... | collective-permute-start | bytes 64520
  752.0 69.7 %collective-permute-start.1 = (bf16[21,512]{1,0:T(8,128)(2,1)S(1)}, bf16[21,512]{1,0:T(8,128)(2,1)S(1)}, u32[]{:S(2)}, u32[]{:S(2)}) collective-permute-start(bf16[21,512]{1,0:T(8,128)(2,1)S(1)} %slice.60), channel_id=1, source_target_pairs={{0,1},{1,2},{2,3},{3,4},{4,5},{5,6},{6,7},{8,9},{9,10},{10,11},{11... | collective-permute-start | bytes 64520
  (18 other events, 168.1 us)
Sparse Core Ops, SparseCore 0:
  49.3 29.5 all-gather.15
  80.6 24.7 all-gather.19
  146.3 24.5 all-gather.17
  172.9 70.6 all-gather.11
  245.7 70.3 all-gather.13
  580.2 24.3 all-gather.21
  609.3 141.2 all-reduce.19
  753.8 67.3 reduce-scatter.16
  825.3 71.3 reduce-scatter.14
  900.0 84.4 reduce-scatter.18
  987.9 84.1 reduce-scatter.20
where the time goes:
time: 1090 us; the launch traced here: 1080 us
  waiting for transfers between devices  382 us (35%)
  local copies, waits for them, and re-layouts  257 us (24%)
  blocking collectives  251 us (23%)
  other arithmetic  84.4 us (8%)
  matrix products  71.1 us (7%)
  between operations  18 us (2%)
  starting transfers between devices  17.5 us (2%)
    unnamed x4, blocking collectives  114 us
    reduce_scatter x1, waiting for transfers between devices, body(): lax.psum_scatter(first_grad.astype(jnp.bfloat16), 'dp', scatter_dimension...  86.4 us
    reduce_scatter x1, waiting for transfers between devices, body(): lax.psum_scatter(second_grad.astype(jnp.bfloat16), 'dp', scatter_dimensio...  85.5 us
    psum x1, waiting for transfers between devices, body(): lax.psum((gain_one_part, gain_two_part, router_weight_part), ('dp', 'tens...  80.9 us
    reduce_scatter x1, waiting for transfers between devices, body(): lax.psum_scatter(qkv_weight_part.astype(jnp.bfloat16), 'dp', scatter_dime...  72.2 us
    psum x1, blocking collectives, body(): lax.psum((gain_one_part, gain_two_part, router_weight_part), ('dp', 'tens...  64.4 us
    unnamed x94, local copies, waits for them, and re-layouts  61.4 us
    gather x2, local copies, waits for them, and re-layouts, body(): picked = result[choices, safe_slot]  56 us
  transfers between devices with their start and end apart: 16, of which 7 were waited for; matrix products, arithmetic and copies ran while one was open for 21% of the time, Pallas kernels for 0%

commit v1 on v0

v1 whole, which is shorter than its diff:
```python
import functools
import math

import jax
import jax.numpy as jnp
from jax import lax
from jax.experimental import pallas as pl
from jax.experimental.pallas import tpu as pltpu
from jax.sharding import PartitionSpec as P

DH = 64
L = 197
CAP = 123
LP = 208
SLOT = 128
N_IMG = 8
ROWS = N_IMG * LP
D = 512
EPS = 1e-05
MESH = pl.DeviceIdType.MESH
BF = jnp.bfloat16
F32 = jnp.float32
N_SEM = 176


def dot(a, b):
    return lax.dot_general(a, b, (((1,), (0,)), ((), ())), preferred_element_type=F32)


def dot_nt(a, b):
    return lax.dot_general(a, b, (((1,), (1,)), ((), ())), preferred_element_type=F32)


def dot_tn(a, b):
    return lax.dot_general(a, b, (((0,), (0,)), ((), ())), preferred_element_type=F32)


def normalize(v):
    center = v - jnp.sum(v, -1, keepdims=True) * (1.0 / D)
    spread = jnp.sum(center * center, -1, keepdims=True) * (1.0 / D)
    inv = lax.rsqrt(spread + EPS)
    return center * inv, inv


def normalize_back(grad, unit, inv):
    mean = jnp.sum(grad, -1, keepdims=True) * (1.0 / D)
    along = jnp.sum(grad * unit, -1, keepdims=True) * (1.0 / D)
    return inv * (grad - mean - unit * along)


def split_two(v):
    high = v.astype(BF)
    return high, (v - high.astype(F32)).astype(BF)


def kernel(
    tok, cot, chooser, w_in, m_in, ein, eout,
    out, tg, gw, gm, gexp,
    W, M, T1, EW, CG, N2G, PM, SB, RB, SB2, RB2, DS, racc, dxacc,
    dEW, YR, YS, XR, CPD, CPM, CRD, CRM, CSD, CSM, ZRD, ZRM,
    xs, cpad, n1s, QKV, PF, MX, resid, xh2s, r2s, pos, gates,
    dW, DWC, DWS, XW, XS, ZW, ZS, YW, MG, MXR, MXS, MYR, MYS,
    send_sem, recv_sem, loc_sem,
):
    d = lax.axis_index("dp")
    t = lax.axis_index("tensor")
    y, x = lax.div(d, 4), lax.rem(d, 4)
    z, c = lax.div(t, 2), lax.rem(t, 2)
    oc = 1 - c
    used = [0, 0]

    def along_x(k):
        return {"dp": y * 4 + lax.rem(x + k, 4)}

    def along_y(k):
        return {"dp": lax.rem(y + k, 4) * 4 + x}

    def along_z(k):
        return {"tensor": lax.rem(z + k, 4) * 2 + c}

    core = {"tensor": z * 2 + oc}

    def along_t(k):
        return {"tensor": lax.rem(t + k, 8)}

    sent = []

    def send(src, dst, to):
        i = used[0]
        used[0] += 1
        cp = pltpu.make_async_remote_copy(
            src_ref=src, dst_ref=dst, send_sem=send_sem.at[i], recv_sem=recv_sem.at[i],
            device_id=to, device_id_type=MESH,
        )
        cp.start()
        sent.append(cp)
        return cp

    def local(src, dst):
        i = used[1]
        used[1] += 1
        cp = pltpu.make_async_copy(src, dst, loc_sem.at[i])
        cp.start()
        return cp

    def arrive(copies):
        for cp in copies:
            cp.wait_recv()

    def image(i):
        return pl.ds(pl.multiple_of(i * LP, 16), LP)

    bar = pltpu.get_barrier_semaphore()
    peers = [along_x(k) for k in (1, 2, 3)] + [along_y(k) for k in (1, 2, 3)]
    peers += [along_t(k) for k in range(1, 8)]
    for p in peers:
        pl.semaphore_signal(bar, inc=1, device_id=p, device_id_type=MESH)

    W[z, c, y, x] = w_in[...]
    M[y, x] = m_in[...]
    xs[...] = jnp.zeros((LP, D), F32)
    xs[0:L, :] = tok[...].astype(F32)
    cpad[...] = jnp.zeros((LP, D), F32)
    cpad[0:L, :] = cot[...].astype(F32)
    CG[image(t), :] = cpad[...].astype(BF)
    pl.semaphore_wait(bar, len(peers))

    w_y = [send(W.at[z, c, y, x], W.at[z, c, y, x], along_y(k)) for k in (1, 2, 3)]
    m_y = [send(M.at[y, x], M.at[y, x], along_y(k)) for k in (1, 2, 3)]
    own1 = [
        local(ein.at[pl.ds(4 * t, 4)], T1.at[t, :, :, pl.ds(0, 256)]),
        local(eout.at[pl.ds(4 * t, 4)], T1.at[t, :, :, pl.ds(256, 256)]),
    ]
    e_1 = []
    for k in range(1, 8):
        to = lax.rem(t + k, 8)
        e_1.append(send(ein.at[pl.ds(4 * to, 4)], T1.at[t, :, :, pl.ds(0, 256)], along_t(k)))
        e_1.append(send(eout.at[pl.ds(4 * to, 4)], T1.at[t, :, :, pl.ds(256, 256)], along_t(k)))
    arrive(w_y)
    w_z = [send(W.at[z, c, :, x], W.at[z, c, :, x], along_z(k)) for k in (1, 2, 3)]
    arrive(m_y)
    m_x = [send(M.at[:, x], M.at[:, x], along_x(k)) for k in (1, 2, 3)]
    arrive(w_z)
    w_x = [send(W.at[:, c, :, x], W.at[:, c, :, x], along_x(k)) for k in (1, 2, 3)]
    w_c = [send(W.at[:, c, :, x], W.at[:, c, :, x], core)]
    c_z = [send(CG.at[image(t)], CG.at[image(t)], along_z(k)) for k in (1, 2, 3)]
    c_c = [send(CG.at[image(t)], CG.at[image(t)], core)]

    sub8 = lax.broadcasted_iota(jnp.int32, (8, ROWS), 0)
    ids = 4 * t + lax.rem(sub8, 4)
    named = jnp.where(sub8 < 4, chooser[0:1, :], chooser[1:2, :])
    hits = jnp.where(named == ids, 1.0, 0.0).astype(F32)
    tri_r = lax.broadcasted_iota(jnp.int32, (128, 128), 0)
    tri_c = lax.broadcasted_iota(jnp.int32, (128, 128), 1)
    upper = jnp.where(tri_r < tri_c, 1.0, 0.0).astype(BF)
    carry = jnp.zeros((8, 1), F32)
    before = []
    for b in range(ROWS // 128):
        part = hits[:, b * 128 : (b + 1) * 128]
        before.append(dot(part.astype(BF), upper) + carry)
        carry = carry + jnp.sum(part, -1, keepdims=True)
    before = jnp.concatenate(before, 1)
    first = jnp.where(hits[0:4] > 0, before[0:4], 999.0)
    second = jnp.where(hits[4:8] > 0, before[4:8] + carry[0:4], 999.0)
    place = jnp.minimum(first, second)
    pos[0:4, :] = jnp.where(place < CAP, place, 999.0)
    slot_ids = lax.broadcasted_iota(jnp.int32, (SLOT, ROWS), 0).astype(F32)
    for i in range(4):
        PM[i * SLOT : (i + 1) * SLOT, :] = jnp.where(slot_ids == pos[i : i + 1, :], 1.0, 0.0).astype(BF)

    for cp in own1:
        cp.wait()
    arrive(e_1)
    e_2 = [
        send(T1.at[:, lax.rem(x + k, 4)], EW.at[:, y, x], along_x(k)) for k in (1, 2, 3)
    ]
    own2 = local(T1.at[:, x], EW.at[:, y, x])

    arrive(m_x)
    small = M[...].reshape(D, 128)
    small_rows = jnp.transpose(small.astype(F32))
    gain_one, gain_two = small_rows[32:33, :], small_rows[33:34, :]
    unit, _ = normalize(xs[...])
    n1s[...] = (unit * gain_one).astype(BF)

    own2.wait()
    e_3 = [send(EW.at[:, y, x], EW.at[:, y, x], along_y(k)) for k in (1, 2, 3)]
    for k, cp in zip((1, 2, 3), w_x):
        cp.wait_recv()
        xi = lax.rem(x + 4 - k, 4)
        w_c.append(send(W.at[:, c, :, xi], W.at[:, c, :, xi], core))
    arrive(w_c)

    lane = lax.broadcasted_iota(jnp.int32, (LP, LP), 1)
    resid[...] = xs[...]

    def head_forward(hz, carry):
        for hc in range(2):
            h = hz * 2 + hc
            wt = W[hz, hc].reshape(D, 256)
            qkv = dot(n1s[...], wt).astype(BF)
            QKV[h] = qkv
            scores = dot_nt(qkv[:, 0:64], qkv[:, 64:128]) * 0.125
            scores = jnp.where(lane < L, scores, -1e30)
            e = jnp.exp(scores - jnp.max(scores, -1, keepdims=True))
            probs = e / jnp.sum(e, -1, keepdims=True)
            PF[h] = probs
            mixed = dot(probs.astype(BF), qkv[:, 128:192]).astype(BF)
            MX[h] = mixed
            resid[...] += dot_nt(mixed, wt[:, 192:256])
        return carry

    lax.fori_loop(0, 4, head_forward, 0)

    for k, cp in zip((1, 2, 3), e_2):
        cp.wait_recv()
        xi = lax.rem(x + 4 - k, 4)
        for j in (1, 2, 3):
            e_3.append(send(EW.at[:, y, xi], EW.at[:, y, xi], along_y(j)))

    unit_two, inv_two = normalize(resid[...])
    xh2s[...] = unit_two
    r2s[...] = jnp.broadcast_to(inv_two, (LP, 128))
    real = lax.broadcasted_iota(jnp.int32, (LP, 1), 0) < L
    n2 = jnp.where(real, unit_two * gain_two, 0.0).astype(BF)
    N2G[image(t), :] = n2
    n_z = [send(N2G.at[image(t)], N2G.at[image(t)], along_z(k)) for k in (1, 2, 3)]
    n_c = [send(N2G.at[image(t)], N2G.at[image(t)], core)]
    for k, cp in zip((1, 2, 3), c_z):
        cp.wait_recv()
        im = image(lax.rem(z + 4 - k, 4) * 2 + c)
        c_c.append(send(CG.at[im], CG.at[im], core))
    arrive(c_c)
    cot_slots = dot(PM[...], CG[...])
    DS[...] = cot_slots.astype(BF)
    for k, cp in zip((1, 2, 3), n_z):
        cp.wait_recv()
        im = image(lax.rem(z + 4 - k, 4) * 2 + c)
        n_c.append(send(N2G.at[im], N2G.at[im], core))
    arrive(n_c)

    rows_x = dot(PM[...], N2G[...]).astype(BF)
    lane_e = lax.broadcasted_iota(jnp.int32, (4 * SLOT, 128), 1)
    row_e = 4 * t + lax.div(lax.broadcasted_iota(jnp.int32, (4 * SLOT, 128), 0), SLOT)

    def router_of(rows):
        logits = dot(rows, small)
        lanes = lax.broadcasted_iota(jnp.int32, logits.shape, 1)
        logits = jnp.where(lanes < 32, logits, -1e30)
        e = jnp.exp(logits - jnp.max(logits, -1, keepdims=True))
        return e / jnp.sum(e, -1, keepdims=True)

    slot_router = router_of(rows_x).astype(BF).astype(F32)
    gate = jnp.sum(jnp.where(lane_e == row_e, slot_router, 0.0), -1, keepdims=True)
    gates[...] = jnp.broadcast_to(gate, (4 * SLOT, 128))
    SB[:, :, 0:512] = rows_x.reshape(4, SLOT, D)
    SB[:, :, 512:1024] = (cot_slots * gate).astype(BF).reshape(4, SLOT, D)
    s_x = [send(SB.at[lax.rem(x + k, 4)], RB.at[x], along_x(k)) for k in (1, 2, 3)]
    RB[x] = SB[x]
    arrive(s_x)
    arrive(e_3)

    rows_e = RB[:, :, 0:512].reshape(4 * SLOT, D)
    grad_e = RB[:, :, 512:1024].reshape(4 * SLOT, D)
    racc[...] = jnp.zeros((4 * SLOT, D), F32)
    dxacc[...] = jnp.zeros((4 * SLOT, D), F32)

    def hidden(h, carry):
        w_first = EW[h, :, :, :, 0:256].reshape(D, 256)
        w_second = EW[h, :, :, :, 256:512].reshape(D, 256)
        inner = dot(rows_e, w_first)
        sq = inner * inner
        th = jnp.tanh(inner * (0.7978845608028654 + (0.7978845608028654 * 0.044715) * sq))
        half = 0.5 + 0.5 * th
        act = (inner * half).astype(BF)
        slope = half + 0.5 * inner * (1.0 - th * th) * (
            0.7978845608028654 + (3 * 0.7978845608028654 * 0.044715) * sq
        )
        d_inner = (dot(grad_e, w_second) * slope).astype(BF)
        racc[...] += dot_nt(act, w_second)
        dxacc[...] += dot_nt(d_inner, w_first)
        dEW[h, :, :, :, 0:256] = dot_tn(rows_e, d_inner).astype(BF).reshape(4, 4, 32, 256)
        dEW[h, :, :, :, 256:512] = dot_tn(grad_e, act).astype(BF).reshape(4, 4, 32, 256)
        return carry

    lax.fori_loop(0, 8, hidden, 0)
    SB2[:, :, 0:512] = racc[...].astype(BF).reshape(4, SLOT, D)
    SB2[:, :, 512:1024] = dxacc[...].astype(BF).reshape(4, SLOT, D)
    b_x = [send(SB2.at[lax.rem(x + k, 4)], RB2.at[x], along_x(k)) for k in (1, 2, 3)]
    g_y = [send(dEW.at[:, lax.rem(y + k, 4)], YR.at[k - 1], along_y(k)) for k in (1, 2, 3)]
    RB2[x] = SB2[x]
    arrive(b_x)

    res = RB2[:, :, 0:512].reshape(4 * SLOT, D)
    d_gate = jnp.sum(res.astype(F32) * DS[...].astype(F32), -1, keepdims=True)
    d_gate = jnp.where(lane_e == row_e, d_gate, 0.0).astype(BF)
    back = jnp.concatenate([RB2[:, :, 512:1024].reshape(4 * SLOT, D), d_gate], 1)
    weighted = PM[...] * gates[:, 0:1].astype(BF)
    for b in range(ROWS // 128):
        CPD[b * 128 : (b + 1) * 128, :] = dot_tn(PM[:, b * 128 : (b + 1) * 128], back).astype(BF)
    r_c = [send(CPD.at[image(2 * i + oc)], CRD.at[i], core) for i in range(4)]
    for b in range(ROWS // 128):
        CPM[b * 128 : (b + 1) * 128, :] = dot_tn(weighted[:, b * 128 : (b + 1) * 128], res).astype(BF)
    o_c = [send(CPM.at[image(2 * i + oc)], CRM.at[i], core) for i in range(4)]
    arrive(r_c)
    for i in range(4):
        CSD[i] = (CPD[image(2 * i + c), :].astype(F32) + CRD[i].astype(F32)).astype(BF)
    r_z = [send(CSD.at[lax.rem(z + k, 4)], ZRD.at[k - 1], along_z(k)) for k in (1, 2, 3)]
    arrive(o_c)
    for i in range(4):
        CSM[i] = (CPM[image(2 * i + c), :].astype(F32) + CRM[i].astype(F32)).astype(BF)
    o_z = [send(CSM.at[lax.rem(z + k, 4)], ZRM.at[k - 1], along_z(k)) for k in (1, 2, 3)]
    arrive(r_z)
    total = CSD[z].astype(F32)
    for k in range(3):
        total = total + ZRD[k].astype(F32)
    d_router = total[:, 512:640]
    d_n2 = total[:, 0:512]
    router = router_of(N2G[image(t), :])
    d_logits = router * (d_router - jnp.sum(d_router * router, -1, keepdims=True))
    dl_high, dl_low = split_two(d_logits)
    d_n2 = d_n2 + dot_nt(dl_high, small) + dot_nt(dl_low, small)
    n2_own = N2G[image(t), :]
    router_part = dot_tn(n2_own, dl_high) + dot_tn(n2_own, dl_low)
    unit_two = xh2s[...]
    alive = chooser[2:3, 0:512].astype(F32)
    gain_two_part = jnp.sum(d_n2 * unit_two, 0, keepdims=True)
    d_resid = cpad[...] * alive + normalize_back(d_n2 * gain_two, unit_two, r2s[:, 0:1])
    resid_low = d_resid.astype(BF)

    xs_grad = dxacc.at[0:LP]
    xs_grad[...] = jnp.zeros((LP, D), F32)
    n1 = n1s[...]

    def head_backward(hz, carry):
        for hc in range(2):
            h = hz * 2 + hc
            wt = W[hz, hc].reshape(D, 256)
            qkv = QKV[h]
            q, key, v = qkv[:, 0:64], qkv[:, 64:128], qkv[:, 128:192]
            d_mixed = dot(resid_low, wt[:, 192:256]).astype(BF)
            probs = PF[h]
            d_probs = dot_nt(d_mixed, v)
            d_scores = probs * (d_probs - jnp.sum(probs * d_probs, -1, keepdims=True))
            d_scores = (d_scores).astype(BF)
            dq = dot(d_scores, key) * 0.125
            dk = dot_tn(d_scores, q) * 0.125
            dv = dot_tn(probs.astype(BF), d_mixed)
            d_qkv = jnp.concatenate([dq, dk, dv], 1).astype(BF)
            xs_grad[...] += dot_nt(d_qkv, wt[:, 0:192])
            dW[hz, hc, :, :, :, 0:192] = dot_tn(n1, d_qkv).astype(BF).reshape(4, 4, 32, 192)
            dW[hz, hc, :, :, :, 192:256] = dot_tn(resid_low, MX[h]).astype(BF).reshape(4, 4, 32, 64)
        return carry

    lax.fori_loop(0, 4, head_backward, 0)
    a_c = [send(dW.at[:, oc], DWC, core)]

    d_n1 = xs_grad[...]
    unit, inv = normalize(xs[...])
    gain_one_part = jnp.sum(d_n1 * unit, 0, keepdims=True)
    gains = jnp.concatenate([gain_one_part, gain_two_part, jnp.zeros((6, D), F32)], 0)
    gains = jnp.transpose(jnp.concatenate([gains, jnp.zeros((120, D), F32)], 0))
    lane_m = lax.broadcasted_iota(jnp.int32, (D, 128), 1)
    shifted = jnp.where(lane_m == 32, gains[:, 0:1], jnp.where(lane_m == 33, gains[:, 1:2], router_part))
    MG[...] = shifted.reshape(4, 4, 32, 128)
    p_x = [send(MG.at[:, lax.rem(x + k, 4)], MXR.at[k - 1], along_x(k)) for k in (1, 2, 3)]
    arrive(a_c)
    for i in range(4):
        DWS[i] = (dW[i, c].astype(F32) + DWC[i].astype(F32)).astype(BF)
    a_x = [send(DWS.at[:, :, lax.rem(x + k, 4)], XW.at[k - 1], along_x(k)) for k in (1, 2, 3)]
    tg[...] = (d_resid + normalize_back(d_n1 * gain_one, unit, inv))[0:L, :]

    arrive(g_y)
    for h in range(8):
        s = dEW[h, y].astype(F32)
        for k in range(3):
            s = s + YR[k, h].astype(F32)
        YS[h] = s.astype(BF)
    g_x = [send(YS.at[:, lax.rem(x + k, 4)], XR.at[x], along_x(k)) for k in (1, 2, 3)]
    for h in range(8):
        XR[x, h] = YS[h, x]

    arrive(p_x)
    s = MG[:, x]
    for k in range(3):
        s = s + MXR[k]
    MXS[...] = s
    p_y = [send(MXS.at[lax.rem(y + k, 4)], MYR.at[k - 1], along_y(k)) for k in (1, 2, 3)]
    arrive(a_x)
    s = DWS[:, :, x].astype(F32)
    for k in range(3):
        s = s + XW[k].astype(F32)
    XS[...] = s.astype(BF)
    a_z = [send(XS.at[lax.rem(z + k, 4)], ZW.at[k - 1], along_z(k)) for k in (1, 2, 3)]
    arrive(p_y)
    s = MXS[y]
    for k in range(3):
        s = s + MYR[k]
    MYS[t] = s
    p_t = [send(MYS.at[t], MYS.at[t], along_t(k)) for k in range(1, 8)]
    arrive(a_z)
    s = XS[z].astype(F32)
    for k in range(3):
        s = s + ZW[k].astype(F32)
    ZS[...] = s.astype(BF)
    a_y = [send(ZS.at[lax.rem(y + k, 4)], YW.at[k - 1], along_y(k)) for k in (1, 2, 3)]
    arrive(o_z)
    moe = CSM[z].astype(F32)
    for k in range(3):
        moe = moe + ZRM[k].astype(F32)
    out[...] = (((resid[...] + moe) * alive)[0:L, :]).astype(BF)
    arrive(g_x)
    own3 = local(XR.at[:, t], gexp.at[t])
    g_t = [send(XR.at[:, lax.rem(t + k, 8)], gexp.at[t], along_t(k)) for k in range(1, 8)]
    arrive(a_y)
    s = ZS[y].astype(F32)
    for k in range(3):
        s = s + YW[k].astype(F32)
    gw[...] = s
    arrive(p_t)
    s = MYS[0]
    for k in range(1, 8):
        s = s + MYS[k]
    gm[...] = s
    own3.wait()
    arrive(g_t)
    for cp in sent:
        cp.wait_send()


def finish(gexp, gw, gm, g_in, g_out, g_qkv, g_o, g_router, g_gains):
    g_in[...] = gexp[:, :, 0:256].astype(F32)
    g_out[...] = gexp[:, :, 256:512].astype(F32)
    g_qkv[...] = gw[:, 0:192]
    g_o[...] = gw[:, 192:256]
    g_router[...] = gm[:, 0:32]
    g_gains[...] = jnp.transpose(gm[...])[32:40, :]


def body(
    tokens, image_counts, choices, gain_attn, qkv_weight, out_weight, gain_moe, router_weight,
    expert_in, expert_out, cotangent,
):
    t = lax.axis_index("tensor")
    count = image_counts[0]
    picks = choices.T.reshape(2, N_IMG, L)
    picks = jnp.where(jnp.arange(N_IMG)[None, :, None] < count, picks, -1)
    picks = jnp.pad(picks, ((0, 0), (0, 0), (0, LP - L)), constant_values=-1).reshape(2, ROWS)
    flag = jnp.broadcast_to((t < count).astype(jnp.int32), (6, ROWS))
    chooser = jnp.concatenate([picks, flag], 0)
    w_in = jnp.concatenate([qkv_weight, out_weight.T], 1)
    m_in = jnp.concatenate(
        [router_weight, gain_attn[:, None], gain_moe[:, None], jnp.zeros((32, 94), BF)], 1
    )
    vm = pl.BlockSpec(memory_space=pltpu.VMEM)

    def buf(*shape, dtype=BF):
        return pltpu.VMEM(shape, dtype)

    scratch = [
        buf(4, 2, 4, 4, 32, 256),
        buf(4, 4, 32, 128),
        buf(8, 4, 32, 512),
        buf(8, 4, 4, 32, 512),
        buf(ROWS, D),
        buf(ROWS, D),
        buf(4 * SLOT, ROWS),
        buf(4, SLOT, 1024),
        buf(4, SLOT, 1024),
        buf(4, SLOT, 1024),
        buf(4, SLOT, 1024),
        buf(4 * SLOT, D),
        buf(4 * SLOT, D, dtype=F32),
        buf(4 * SLOT, D, dtype=F32),
        buf(8, 4, 4, 32, 512),
        buf(3, 8, 4, 32, 512),
        buf(8, 4, 32, 512),
        buf(4, 8, 32, 512),
        buf(ROWS, 640),
        buf(ROWS, D),
        buf(4, LP, 640),
        buf(4, LP, D),
        buf(4, LP, 640),
        buf(4, LP, D),
        buf(3, LP, 640),
        buf(3, LP, D),
        buf(LP, D, dtype=F32),
        buf(LP, D, dtype=F32),
        buf(LP, D),
        buf(8, LP, 256),
        buf(8, LP, LP, dtype=F32),
        buf(8, LP, 64),
        buf(LP, D, dtype=F32),
        buf(LP, D, dtype=F32),
        buf(LP, 128, dtype=F32),
        buf(8, ROWS, dtype=F32),
        buf(4 * SLOT, 128, dtype=F32),
        buf(4, 2, 4, 4, 32, 256),
        buf(4, 4, 4, 32, 256),
        buf(4, 4, 4, 32, 256),
        buf(3, 4, 4, 32, 256),
        buf(4, 4, 32, 256),
        buf(3, 4, 32, 256),
        buf(4, 32, 256),
        buf(3, 32, 256),
        buf(4, 4, 32, 128, dtype=F32),
        buf(3, 4, 32, 128, dtype=F32),
        buf(4, 32, 128, dtype=F32),
        buf(3, 32, 128, dtype=F32),
        buf(8, 32, 128, dtype=F32),
        pltpu.SemaphoreType.DMA((N_SEM,)),
        pltpu.SemaphoreType.DMA((N_SEM,)),
        pltpu.SemaphoreType.DMA((8,)),
    ]
    out, tg, gw, gm, gexp = pl.pallas_call(
        kernel,
        name="block",
        out_shape=[
            jax.ShapeDtypeStruct((L, D), BF),
            jax.ShapeDtypeStruct((L, D), F32),
            jax.ShapeDtypeStruct((32, 256), F32),
            jax.ShapeDtypeStruct((32, 128), F32),
            jax.ShapeDtypeStruct((8, 4, 32, 512), BF),
        ],
        in_specs=[vm] * 7,
        out_specs=[vm] * 5,
        scratch_shapes=scratch,
        compiler_params=pltpu.CompilerParams(
            collective_id=0, has_side_effects=True, vmem_limit_bytes=60 * 2**20
        ),
    )(tokens, cotangent, chooser, w_in, m_in, expert_in, expert_out.transpose(0, 2, 1))
    g_in, g_out, g_qkv, g_o, g_router, g_gains = pl.pallas_call(
        finish,
        name="finish",
        out_shape=[
            jax.ShapeDtypeStruct((32, 32, 256), F32),
            jax.ShapeDtypeStruct((32, 32, 256), F32),
            jax.ShapeDtypeStruct((32, 192), F32),
            jax.ShapeDtypeStruct((32, 64), F32),
            jax.ShapeDtypeStruct((32, 32), F32),
            jax.ShapeDtypeStruct((8, 32), F32),
        ],
        in_specs=[vm] * 3,
        out_specs=[vm] * 6,
        compiler_params=pltpu.CompilerParams(vmem_limit_bytes=32 * 2**20),
    )(gexp.reshape(32, 32, 512), gw, gm)
    return (
        out, tg, g_gains[0], g_qkv, g_o.T, g_gains[1], g_router, g_in, g_out.transpose(0, 2, 1),
    )


def solution(mesh):
    rows = P(("dp", "tensor"), None)
    in_specs = (
        rows, P("dp"), P("dp", None), P("dp"), P("dp", "tensor"), P("tensor", "dp"), P("dp"),
        P("dp", None), P(None, "dp", "tensor"), P(None, "tensor", "dp"), rows,
    )
    out_specs = (
        rows, rows, P("dp"), P("dp", "tensor"), P("tensor", "dp"), P("dp"), P("dp", None),
        P(None, "dp", "tensor"), P(None, "tensor", "dp"),
    )
    return jax.shard_map(body, mesh=mesh, in_specs=in_specs, out_specs=out_specs, check_vma=False)
```

time: 1090 us -> 196 us (0.18)
  waiting for transfers between devices: 382 us -> 0 us
  blocking collectives: 251 us -> 0 us
  local copies, waits for them, and re-layouts: 257 us -> 7.53 us
  Pallas kernels: 0 us -> 186 us
  other arithmetic: 84.4 us -> 1.45 us
  matrix products: 71.1 us -> 0 us
  starting transfers between devices: 17.5 us -> 0 us
  between operations: 18 us -> 1.36 us
    reduce_scatter x4 -> x0, waiting for transfers between devices: 244 us -> none  [the longest x1 86.4 us: body(): lax.psum_scatter(first_grad.astype(jnp.bfloat16), 'dp', scatter_dimension...]
    pallas_call x0 -> x2, Pallas kernels: none -> 186 us  [the longest x1 184 us: body(): pl.pallas_call(kernel, name='block', out_shape=[jax.ShapeDtypeStruct((L,...]
    gather x9 -> x0, local copies, waits for them, and re-layouts: 120 us -> none  [the longest x2 56 us: body(): picked = result[choices, safe_slot]]
    unnamed x4 -> x0, blocking collectives: 114 us -> none
    psum x1 -> x0, waiting for transfers between devices: 80.9 us -> none  [body(): lax.psum((gain_one_part, gain_two_part, router_weight_part), ('dp', 'tens...]
    all_gather x4 -> x0, blocking collectives: 72.2 us -> none  [the longest x1 19.3 us: body(): lax.all_gather(out_weight, 'dp', axis=1, tiled=True)]
    dot_general x21 -> x0, matrix products: 71.1 us -> none  [the longest x1 9.41 us: body(): jnp.einsum('ecd,efd->ecf', result_grad, second_full, preferred_element_ty...]
    psum x1 -> x0, blocking collectives: 64.4 us -> none  [body(): lax.psum((gain_one_part, gain_two_part, router_weight_part), ('dp', 'tens...]
  transfers between devices with their start and end apart: 16 -> 0, of which waited for: 7 -> 0; matrix products, arithmetic and copies ran while one was open for 21% -> 0% of each run, Pallas kernels for 0% -> 0%
where the time goes in v1:
time: 196 us
  Pallas kernels  186 us (95%)
  local copies, waits for them, and re-layouts  7.53 us (4%)
    pallas_call x1, Pallas kernels, body(): pl.pallas_call(kernel, name='block', out_shape=[jax.ShapeDtypeStruct((L,...  184 us
    unnamed x24, local copies, waits for them, and re-layouts  5.91 us

profile of v1, /device:TPU:1, one launch (start us, length us, event | category | flops | bytes accessed | tf_op | source)
XLA Modules:
  0.0 195.9 jit_solution(11270684986734461627)
XLA Ops:
  1.3 0.0 copy-start.9
  1.3 0.1 pad.9.clone
  1.4 0.6 copy-done.9
  2.0 0.0 copy-start.10
  2.0 0.0 copy-start.8
  2.0 0.1 copy.20
  2.1 0.6 copy-done.10
  2.6 0.1 copy.21
  2.7 0.0 copy-done.8
  2.7 0.0 copy-start.6
  2.7 0.7 maximum_maximum_fusion.m_in
  3.4 0.0 copy-done.6
  3.4 0.1 reshape.32
  3.5 0.1 broadcast_select_fusion
  3.6 0.0 copy-start.5
  3.6 0.0 copy-start.7
  3.6 0.1 reshape.33
  3.7 0.6 copy-done.5
  4.3 0.0 copy-done.7
  4.3 0.7 pad_maximum_fusion.w_in
  5.0 0.6 concatenate.9.chooser
  5.7 184.1 %block.1 = (bf16[197,512]{1,0:T(8,128)(2,1)}, f32[197,512]{1,0:T(8,128)}, f32[32,256]{1,0:T(8,128)}, f32[32,128]{1,0:T(8,128)}, bf16[8,4,32,512]{3,2,1,0:T(8,128)(2,1)}) custom-call(bf16[197,512]{1,0:T(8,128)(2,1)} %tok.1, bf16[197,512]{1,0:T(8,128)(2,1)} %cot.1, s32[8,1664]{1,0:T(8,128)} %concatenate.9.chooser, bf16[32,256]{1,0:T(8,128)(2,1)} %pad_maximum_fusion.w_in, ...), custom_call_target="tpu_custom_call" | custom-call | tf_op jit(solution)/shard_map/block/pallas_call | solution.py:515
  189.8 0.0 copy-start
  189.8 1.2 copy-done
  191.0 0.8 copy-done.1
  191.8 0.7 copy-done.2
  192.5 1.4 finish.1
  193.9 0.5 slice_bitcast_fusion
  194.4 0.0 copy-done.4
  194.4 0.7 copy.25
  195.1 0.0 copy-done.3
  195.1 0.8 copy.26
  (7 shorter events, 0.0 us)
Async XLA Ops:
  1.3 0.7 copy-start.9
  2.0 0.7 copy-start.10
  2.0 0.8 copy-start.8
  2.7 0.7 copy-start.6
  3.6 0.7 copy-start.5
  3.6 0.7 copy-start.7
  189.8 1.2 copy-start
  191.0 0.8 copy-start.1
  191.8 0.7 copy-start.2
  192.5 1.9 copy-start.4
  193.9 1.2 copy-start.3

commit v2 on v1

v2 whole, which is shorter than its diff:
```python
import jax
import jax.numpy as jnp
from jax import lax
from jax.experimental import pallas as pl
from jax.experimental.pallas import tpu as pltpu
from jax.sharding import PartitionSpec as P

DH = 64
L = 197
CAP = 123
LP = 208
SLOT = 128
N_IMG = 8
LQ = 256
ROWS = N_IMG * LQ
D = 512
EPS = 1e-05
MESH = pl.DeviceIdType.MESH
BF = jnp.bfloat16
F32 = jnp.float32
N_SEM = 240


def dot(a, b):
    return lax.dot_general(a, b, (((1,), (0,)), ((), ())), preferred_element_type=F32)


def dot_nt(a, b):
    return lax.dot_general(a, b, (((1,), (1,)), ((), ())), preferred_element_type=F32)


def dot_tn(a, b):
    return lax.dot_general(a, b, (((0,), (0,)), ((), ())), preferred_element_type=F32)


def normalize(v):
    center = v - jnp.sum(v, -1, keepdims=True) * (1.0 / D)
    spread = jnp.sum(center * center, -1, keepdims=True) * (1.0 / D)
    inv = lax.rsqrt(spread + EPS)
    return center * inv, inv


def normalize_back(grad, unit, inv):
    mean = jnp.sum(grad, -1, keepdims=True) * (1.0 / D)
    along = jnp.sum(grad * unit, -1, keepdims=True) * (1.0 / D)
    return inv * (grad - mean - unit * along)


def split_two(v):
    high = v.astype(BF)
    return high, (v - high.astype(F32)).astype(BF)


def kernel(
    cnt, tok, cot, picks, qkv_in, out_in, router_in, gain_one_in, gain_two_in, ein, eout,
    out, tg, gw, gm, gexp,
    W, M, T1, EW, CG, N2G, PM, SB, RB, SB2, RB2, DS, racc, dxacc, ACT, DIN, XT, GT,
    YR, YS, XR, CPD, CPM, CRD, CRM, CSD, CSM, ZRD, ZRM,
    xs, cpad, n1s, QKV, PF, MX, resid, xh2s, r2s, chs, pos, gates,
    dW, DWC, DWS, XW, XS, ZW, MG, MXR, MXS, MYR, MYS,
    send_sem, recv_sem, loc_sem,
):
    d = lax.axis_index("dp")
    t = lax.axis_index("tensor")
    y, x = lax.div(d, 4), lax.rem(d, 4)
    z, c = lax.div(t, 2), lax.rem(t, 2)
    oc = 1 - c
    used = [0, 0]

    u, v = x + c * (y - x), y + c * (x - y)

    def next_to(n, i, k):
        return lax.rem(i + k, n)

    def along_uv(ku, kv):
        return lax.rem(y + ku * c + kv * oc, 4) * 4 + lax.rem(x + ku * oc + kv * c, 4)

    def along_u(k):
        return {"dp": along_uv(k, 0)}

    def along_v(k):
        return {"dp": along_uv(0, k)}

    def along_z(k):
        return {"tensor": lax.rem(z + k, 4) * 2 + c}

    def along_vz(kv, kz):
        return {"dp": along_uv(0, kv), "tensor": lax.rem(z + kz, 4) * 2 + c}

    def along_t(k):
        return {"tensor": lax.rem(t + k, 8)}

    core = {"tensor": z * 2 + oc}

    def place_uv(yi, xi):
        return yi + c * (xi - yi), xi + c * (yi - xi)

    def take(n):
        used[0] += n
        return used[0] - n

    sent = []

    def remote(src, dst, to, i):
        return pltpu.make_async_remote_copy(
            src_ref=src, dst_ref=dst, send_sem=send_sem.at[i], recv_sem=recv_sem.at[i],
            device_id=to, device_id_type=MESH,
        )

    def send(src, dst, to):
        cp = remote(src, dst, to, take(1))
        cp.start()
        sent.append(cp)
        return cp

    def local(src, dst):
        i = used[1]
        used[1] += 1
        cp = pltpu.make_async_copy(src, dst, loc_sem.at[i])
        cp.start()
        return cp

    def arrive(copies):
        for cp in copies:
            cp.wait_recv()

    VZ = [(kv, kz) for kz in range(4) for kv in range(4) if (kv, kz) != (0, 0)]
    ZORDER = (0, 1, 3, 2)

    bar = pltpu.get_barrier_semaphore()
    peers = [along_u(k) for k in (1, 2, 3)] + [along_vz(*k) for k in VZ]
    peers += [along_t(k) for k in range(1, 8) if k % 2 == 1]
    for p in peers:
        pl.semaphore_signal(bar, inc=1, device_id=p, device_id_type=MESH)

    eye_r = lax.broadcasted_iota(jnp.int32, (32, 32), 0)
    eye_c = lax.broadcasted_iota(jnp.int32, (32, 32), 1)

    def column(row):
        return jnp.sum(jnp.where(eye_r == eye_c, row.astype(F32), 0.0), -1, keepdims=True)

    W[c, z, v, u, :, 0:192] = qkv_in[...]
    W[c, z, v, u, :, 192:256] = out_in[...]
    M[v, u] = jnp.zeros((32, 128), BF)
    M[v, u, :, 0:32] = router_in[...]
    M[v, u, :, 32:33] = column(gain_one_in[...]).astype(BF)
    M[v, u, :, 33:34] = column(gain_two_in[...]).astype(BF)
    xs[...] = jnp.zeros((LP, D), F32)
    xs[0:L, :] = tok[...].astype(F32)
    cpad[...] = jnp.zeros((LP, D), F32)
    cpad[0:L, :] = cot[...].astype(F32)
    for i in range(N_IMG):
        CG[i, LP:LQ, :] = jnp.zeros((LQ - LP, D), BF)
        N2G[i, LP:LQ, :] = jnp.zeros((LQ - LP, D), BF)
    CG[t, 0:LP, :] = cpad[...].astype(BF)
    pl.semaphore_wait(bar, len(peers))

    w_1 = [send(W.at[c, z, v, u], W.at[c, z, v, u], along_vz(*k)) for k in VZ]
    m_1 = [send(M.at[v, u], M.at[v, u], along_v(k)) for k in (1, 2, 3)]

    e_1 = {}

    def first_hop(kz, kc):
        to_z = next_to(4, z, kz)
        to_c = c + kc * (oc - c)
        to_t = 2 * to_z + to_c
        src = [ein.at[pl.ds(4 * to_t, 4)], eout.at[pl.ds(4 * to_t, 4)]]
        dst = [T1.at[z, c, :, :, pl.ds(0, 256)], T1.at[z, c, :, :, pl.ds(256, 256)]]
        if kz == 0 and kc == 0:
            return [local(s, q) for s, q in zip(src, dst)]
        return [send(s, q, {"tensor": to_t}) for s, q in zip(src, dst)]

    for kz in ZORDER:
        for kc in (0, 1):
            e_1[kz, kc] = first_hop(kz, kc)

    def first_arrived(kz):
        for kc in (0, 1):
            for cp in e_1[kz, kc]:
                if kz == 0 and kc == 0:
                    cp.wait()
                else:
                    cp.wait_recv()

    e_2 = {}

    def second_hop(kz):
        zi = next_to(4, z, 4 - kz)
        e_2[kz] = [
            send(T1.at[zi, :, next_to(4, u, k)], EW.at[zi, :, v, u], along_u(k)) for k in (1, 2, 3)
        ]
        e_2[kz].append(local(T1.at[zi, :, u], EW.at[zi, :, v, u]))

    e_3_base = take(12)

    def third_hop_copy(i, k, zi):
        part = EW.at[zi, :, v]
        return remote(part, part, along_v(k), e_3_base + 3 * i + k - 1)

    def third_hop(kz):
        arrive(e_2[kz][:3])
        e_2[kz][3].wait()
        zi = next_to(4, z, 4 - kz)
        for k in (1, 2, 3):
            cp = third_hop_copy(ZORDER.index(kz), k, zi)
            cp.start()

    chs[...] = jnp.full((8, ROWS), -1, jnp.int32)
    for i in range(N_IMG):
        held = picks[:, i * L : (i + 1) * L]
        live = jnp.full((2, L), cnt[0], jnp.int32) > i
        chs[0:2, i * LQ : i * LQ + L] = jnp.where(live, held, -1)
    sub8 = lax.broadcasted_iota(jnp.int32, (8, ROWS), 0)
    ids = 4 * t + lax.rem(sub8, 4)
    named = jnp.where(sub8 < 4, chs[0:1, :], chs[1:2, :])
    hits = jnp.where(named == ids, 1.0, 0.0).astype(F32)
    tri_r = lax.broadcasted_iota(jnp.int32, (256, 256), 0)
    tri_c = lax.broadcasted_iota(jnp.int32, (256, 256), 1)
    upper = jnp.where(tri_r < tri_c, 1.0, 0.0).astype(BF)
    carry = jnp.zeros((8, 1), F32)
    before = []
    for b in range(N_IMG):
        part = hits[:, b * LQ : (b + 1) * LQ]
        before.append(dot(part.astype(BF), upper) + carry)
        carry = carry + jnp.sum(part, -1, keepdims=True)
    before = jnp.concatenate(before, 1)
    first = jnp.where(hits[0:4] > 0, before[0:4], 999.0)
    second = jnp.where(hits[4:8] > 0, before[4:8] + carry[0:4], 999.0)
    place = jnp.minimum(first, second)
    pos[0:4, :] = jnp.where(place < CAP, place, 999.0)

    arrive(w_1)
    w_u = [send(W.at[c, :, :, u], W.at[c, :, :, u], along_u(k)) for k in (1, 2, 3)]
    arrive(m_1)
    m_u = [send(M.at[:, u], M.at[:, u], along_u(k)) for k in (1, 2, 3)]
    w_c = [send(W.at[c, :, :, u], W.at[c, :, :, u], core)]
    first_arrived(0)
    second_hop(0)
    c_z = [send(CG.at[t, pl.ds(0, LP)], CG.at[t, pl.ds(0, LP)], along_z(k)) for k in (1, 2, 3)]
    c_c = [send(CG.at[t, pl.ds(0, LP)], CG.at[t, pl.ds(0, LP)], core)]

    slot_ids = lax.broadcasted_iota(jnp.int32, (SLOT, ROWS), 0).astype(F32)
    for i in range(4):
        PM[i * SLOT : (i + 1) * SLOT, :] = jnp.where(slot_ids == pos[i : i + 1, :], 1.0, 0.0).astype(BF)

    first_arrived(1)
    second_hop(1)
    first_arrived(3)
    second_hop(3)

    arrive(m_u)
    natural = [place_uv(yi, xi) for yi in range(4) for xi in range(4)]
    small = jnp.concatenate([M[vi, ui] for vi, ui in natural], 0)
    small_rows = jnp.transpose(small.astype(F32))
    gain_one, gain_two = small_rows[32:33, :], small_rows[33:34, :]
    unit, _ = normalize(xs[...])
    n1s[...] = (unit * gain_one).astype(BF)
    resid[...] = xs[...]

    for k in (1, 2, 3):
        w_u[k - 1].wait_recv()
        ui = next_to(4, u, 4 - k)
        w_c.append(send(W.at[c, :, :, ui], W.at[c, :, :, ui], core))
    third_hop(0)
    first_arrived(2)
    second_hop(2)
    arrive(w_c)

    lane = lax.broadcasted_iota(jnp.int32, (LP, LP), 1)

    def weights_of(hz, hc):
        if hc == 0:
            return W[0, hz].reshape(D, 256)
        return jnp.concatenate([W[1, hz, xi, yi] for yi in range(4) for xi in range(4)], 0)

    def head_forward(hz, carry):
        for hc in range(2):
            h = hz * 2 + hc
            wt = weights_of(hz, hc)
            qkv = dot(n1s[...], wt).astype(BF)
            QKV[h] = qkv
            scores = dot_nt(qkv[:, 0:64], qkv[:, 64:128]) * 0.125
            scores = jnp.where(lane < L, scores, -1e30)
            e = jnp.exp(scores - jnp.max(scores, -1, keepdims=True))
            probs = e * (1.0 / jnp.sum(e, -1, keepdims=True))
            PF[h] = probs
            mixed = dot(probs.astype(BF), qkv[:, 128:192]).astype(BF)
            MX[h] = mixed
            resid[...] += dot_nt(mixed, wt[:, 192:256])
        return carry

    lax.fori_loop(0, 2, head_forward, 0)
    third_hop(1)
    third_hop(3)
    lax.fori_loop(2, 4, head_forward, 0)

    unit_two, inv_two = normalize(resid[...])
    xh2s[...] = unit_two
    r2s[...] = jnp.broadcast_to(inv_two, (LP, 128))
    real = lax.broadcasted_iota(jnp.int32, (LP, 1), 0) < L
    N2G[t, 0:LP, :] = jnp.where(real, unit_two * gain_two, 0.0).astype(BF)
    n_z = [send(N2G.at[t, pl.ds(0, LP)], N2G.at[t, pl.ds(0, LP)], along_z(k)) for k in (2, 1, 3)]
    n_c = [send(N2G.at[t, pl.ds(0, LP)], N2G.at[t, pl.ds(0, LP)], core)]
    third_hop(2)
    for k, cp in zip((1, 2, 3), c_z):
        cp.wait_recv()
        im = next_to(4, z, 4 - k) * 2 + c
        c_c.append(send(CG.at[im, pl.ds(0, LP)], CG.at[im, pl.ds(0, LP)], core))
    arrive(c_c)
    cot_slots = dot(PM[...], CG[...].reshape(ROWS, D))
    DS[...] = cot_slots.astype(BF)
    for k, cp in sorted(zip((2, 1, 3), n_z), key=lambda kc: kc[0] % 2 == 0):
        cp.wait_recv()
        im = next_to(4, z, 4 - k) * 2 + c
        n_c.append(send(N2G.at[im, pl.ds(0, LP)], N2G.at[im, pl.ds(0, LP)], core))
    arrive(n_c)

    rows_x = dot(PM[...], N2G[...].reshape(ROWS, D)).astype(BF)
    lane_e = lax.broadcasted_iota(jnp.int32, (4 * SLOT, 128), 1)
    row_e = 4 * t + lax.div(lax.broadcasted_iota(jnp.int32, (4 * SLOT, 128), 0), SLOT)

    def router_of(rows):
        logits = dot(rows, small)
        lanes = lax.broadcasted_iota(jnp.int32, logits.shape, 1)
        logits = jnp.where(lanes < 32, logits, -1e30)
        e = jnp.exp(logits - jnp.max(logits, -1, keepdims=True))
        return e / jnp.sum(e, -1, keepdims=True)

    slot_router = router_of(rows_x).astype(BF).astype(F32)
    gate = jnp.sum(jnp.where(lane_e == row_e, slot_router, 0.0), -1, keepdims=True)
    gates[...] = jnp.broadcast_to(gate, (4 * SLOT, 128))
    SB[:, :, 0:512] = rows_x.reshape(4, SLOT, D)
    SB[:, :, 512:1024] = (DS[...].astype(F32) * gate).astype(BF).reshape(4, SLOT, D)
    s_u = [send(SB.at[next_to(4, u, k)], RB.at[u], along_u(k)) for k in (1, 2, 3)]
    RB[u] = SB[u]
    arrive(s_u)

    rows_e = RB[:, :, 0:512].reshape(4 * SLOT, D)
    grad_e = RB[:, :, 512:1024].reshape(4 * SLOT, D)
    racc[...] = jnp.zeros((4 * SLOT, D), F32)
    dxacc[...] = jnp.zeros((4 * SLOT, D), F32)

    def tile_of(zi, ci, lanes):
        return jnp.concatenate([EW[zi, ci, vi, ui, :, lanes] for vi, ui in natural], 0)

    def hidden_group(i, carry):
        kz = jnp.where(i < 2, i, 5 - i)
        zi = lax.rem(z + 4 - kz, 4)
        for k in (1, 2, 3):
            third_hop_copy(i, k, zi).wait_recv()

        def hidden(ci, carry):
            w_first = tile_of(zi, ci, slice(0, 256))
            w_second = tile_of(zi, ci, slice(256, 512))
            inner = dot(rows_e, w_first)
            sq = inner * inner
            th = jnp.tanh(inner * (0.7978845608028654 + (0.7978845608028654 * 0.044715) * sq))
            half = 0.5 + 0.5 * th
            act = (inner * half).astype(BF)
            slope = half + 0.5 * inner * (1.0 - th * th) * (
                0.7978845608028654 + (3 * 0.7978845608028654 * 0.044715) * sq
            )
            d_inner = (dot(grad_e, w_second) * slope).astype(BF)
            ACT[zi, ci] = act
            DIN[zi, ci] = d_inner
            racc[...] += dot_nt(act, w_second)
            dxacc[...] += dot_nt(d_inner, w_first)
            return carry

        return lax.fori_loop(0, 2, hidden, carry)

    lax.fori_loop(0, 4, hidden_group, 0)
    SB2[:, :, 0:512] = racc[...].astype(BF).reshape(4, SLOT, D)
    SB2[:, :, 512:1024] = dxacc[...].astype(BF).reshape(4, SLOT, D)
    b_u = [send(SB2.at[next_to(4, u, k)], RB2.at[u], along_u(k)) for k in (1, 2, 3)]
    RB2[u] = SB2[u]

    dEW = EW
    for i in range(4):
        for k in (1, 2, 3):
            third_hop_copy(i, k, next_to(4, z, 4 - ZORDER[i])).wait_send()
    XT[...] = jnp.transpose(rows_e)
    GT[...] = jnp.transpose(grad_e)
    g_v_base = take(24)

    def grad_copy(h, k):
        zi, ci = lax.div(h, 2), lax.rem(h, 2)
        return remote(
            dEW.at[zi, ci, next_to(4, v, k)], YR.at[k - 1, zi, ci], along_v(k), g_v_base + 3 * h + k - 1
        )

    def expert_grads(h, carry):
        zi, ci = lax.div(h, 2), lax.rem(h, 2)
        g_first = dot(XT[...], DIN[zi, ci]).astype(BF)
        g_second = dot(GT[...], ACT[zi, ci]).astype(BF)
        for i, (vi, ui) in enumerate(natural):
            dEW[zi, ci, vi, ui, :, 0:256] = g_first[i * 32 : (i + 1) * 32, :]
            dEW[zi, ci, vi, ui, :, 256:512] = g_second[i * 32 : (i + 1) * 32, :]
        for k in (1, 2, 3):
            grad_copy(h, k).start()
        return carry

    lax.fori_loop(0, 8, expert_grads, 0)
    arrive(b_u)

    res = RB2[:, :, 0:512].reshape(4 * SLOT, D)
    back = RB2[:, :, 512:1024].reshape(4 * SLOT, D)
    d_gate = jnp.sum(res.astype(F32) * DS[...].astype(F32), -1, keepdims=True)
    d_gate = jnp.where(lane_e == row_e, d_gate, 0.0).astype(BF)

    def columns_of(i):
        return pl.ds(pl.multiple_of(i * LQ, LQ), LQ)

    def grad_rows(i):
        hot = PM[:, columns_of(i)]
        CPD[i, 0:LP, :] = dot_tn(hot, back)[0:LP].astype(BF)
        by_expert = dot_tn(d_gate, hot)[0:32].astype(BF)
        CPD[i, LP : LP + 16, 0:256] = by_expert[0:16]
        CPD[i, LP : LP + 16, 256:512] = by_expert[16:32]

    r_c, r_z, o_c, o_z = {}, {}, {}, {}
    for kz in (2, 1, 3, 0):
        i = next_to(4, z, kz)
        grad_rows(2 * i + oc)
        r_c[kz] = send(CPD.at[2 * i + oc], CRD.at[i], core)
    for kz in (2, 1, 3, 0):
        i = next_to(4, z, kz)
        grad_rows(2 * i + c)
        r_c[kz].wait_recv()
        CSD[i] = (CPD[2 * i + c].astype(F32) + CRD[i].astype(F32)).astype(BF)
        if kz:
            r_z[kz] = send(CSD.at[i], ZRD.at[kz - 1], along_z(kz))

    def moe_rows(i):
        hot = PM[:, columns_of(i)] * gates[:, 0:1].astype(BF)
        CPM[i] = dot_tn(hot, res)[0:LP].astype(BF)

    for kz in (2, 1, 3, 0):
        i = next_to(4, z, kz)
        moe_rows(2 * i + oc)
        o_c[kz] = send(CPM.at[2 * i + oc], CRM.at[i], core)
    for kz in (2, 1, 3, 0):
        i = next_to(4, z, kz)
        moe_rows(2 * i + c)
        o_c[kz].wait_recv()
        CSM[i] = (CPM[2 * i + c].astype(F32) + CRM[i].astype(F32)).astype(BF)
        if kz:
            o_z[kz] = send(CSM.at[i], ZRM.at[kz - 1], along_z(kz))

    g_u = {}

    def sum_over_v(zi):
        for ci in range(2):
            for k in (1, 2, 3):
                grad_copy(2 * zi + ci, k).wait_recv()
            s = dEW[zi, ci, v].astype(F32)
            for k in range(3):
                s = s + YR[k, zi, ci].astype(F32)
            YS[zi, ci] = s.astype(BF)
        g_u[zi] = [
            send(YS.at[zi, :, next_to(4, u, k)], XR.at[zi, :, u], along_u(k)) for k in (1, 2, 3)
        ]
        for ci in range(2):
            XR[zi, ci, u] = YS[zi, ci, u]

    sum_over_v(0)
    sum_over_v(1)

    for kz in (1, 3, 2):
        r_z[kz].wait_recv()
    total = CSD[z].astype(F32)
    for k in range(3):
        total = total + ZRD[k].astype(F32)
    d_n2 = total[0:LP]
    d_router = jnp.concatenate([total[LP:, 0:256], total[LP:, 256:512], jnp.zeros((96, 256), F32)], 0)
    d_router = jnp.transpose(d_router)[0:LP]
    n2_own = N2G[t, 0:LP, :]
    router = router_of(n2_own)
    d_logits = router * (d_router - jnp.sum(d_router * router, -1, keepdims=True))
    dl_high, dl_low = split_two(d_logits)
    d_n2 = d_n2 + dot_nt(dl_high, small) + dot_nt(dl_low, small)
    unit_two = xh2s[...]
    alive = jnp.where(jnp.full((1, D), cnt[0], jnp.int32) > t, 1.0, 0.0)
    d_resid = cpad[...] * alive + normalize_back(d_n2 * gain_two, unit_two, r2s[:, 0:1])
    resid_low = d_resid.astype(BF)
    router_part = dot_tn(n2_own, dl_high) + dot_tn(n2_own, dl_low)
    gain_two_part = jnp.sum(d_n2 * unit_two, 0, keepdims=True)

    xs_grad = dxacc.at[0:LP]
    xs_grad[...] = jnp.zeros((LP, D), F32)
    n1_cols = jnp.transpose(n1s[...])
    resid_cols = jnp.transpose(resid_low)
    a_c_base = take(4)

    def swap_copy(hz):
        return remote(dW.at[oc, hz], DWC.at[hz], core, a_c_base + hz)

    def head_backward(hz, carry):
        for hc in range(2):
            h = hz * 2 + hc
            wt = weights_of(hz, hc)
            qkv = QKV[h]
            q, key, val = qkv[:, 0:64], qkv[:, 64:128], qkv[:, 128:192]
            d_mixed = dot(resid_low, wt[:, 192:256]).astype(BF)
            probs = PF[h]
            d_probs = dot_nt(d_mixed, val)
            d_scores = probs * (d_probs - jnp.sum(probs * d_probs, -1, keepdims=True))
            d_scores = d_scores.astype(BF)
            dq = dot(d_scores, key) * 0.125
            dk = dot_tn(d_scores, q) * 0.125
            dv = dot_tn(probs.astype(BF), d_mixed)
            d_qkv = jnp.concatenate([dq, dk, dv], 1).astype(BF)
            xs_grad[...] += dot_nt(d_qkv, wt[:, 0:192])
            grad = jnp.concatenate([dot(n1_cols, d_qkv), dot(resid_cols, MX[h])], 1).astype(BF)
            if hc == 0:
                dW[0, hz] = grad.reshape(4, 4, 32, 256)
            else:
                for yi in range(4):
                    for xi in range(4):
                        b = (yi * 4 + xi) * 32
                        dW[1, hz, xi, yi] = grad[b : b + 32]
        swap_copy(hz).start()
        return carry

    lax.fori_loop(0, 2, head_backward, 0)
    sum_over_v(2)
    sum_over_v(3)
    lax.fori_loop(2, 4, head_backward, 0)

    a_u = []
    for i in range(4):
        swap_copy(i).wait_recv()
        DWS[i] = (dW[c, i].astype(F32) + DWC[i].astype(F32)).astype(BF)
        a_u += [
            send(DWS.at[i, :, next_to(4, u, k)], XW.at[k - 1, i], along_u(k)) for k in (1, 2, 3)
        ]
    d_n1 = xs_grad[...]
    unit, inv = normalize(xs[...])
    gain_one_part = jnp.sum(d_n1 * unit, 0, keepdims=True)
    gains = jnp.concatenate([gain_one_part, gain_two_part, jnp.zeros((126, D), F32)], 0)
    gains = jnp.transpose(gains)
    lane_m = lax.broadcasted_iota(jnp.int32, (D, 128), 1)
    merged = jnp.where(lane_m == 32, gains[:, 0:1], jnp.where(lane_m == 33, gains[:, 1:2], router_part))
    for i, (vi, ui) in enumerate(natural):
        MG[vi, ui] = merged[i * 32 : (i + 1) * 32]
    p_u = [send(MG.at[:, next_to(4, u, k)], MXR.at[k - 1], along_u(k)) for k in (1, 2, 3)]
    tg[...] = (d_resid + normalize_back(d_n1 * gain_one, unit, inv))[0:L, :]

    g_t = []

    for zi in range(4):
        arrive(g_u[zi])
    for k in range(1, 8):
        to = next_to(8, t, k)
        g_t.append(send(XR.at[lax.div(to, 2), lax.rem(to, 2)], gexp.at[t], along_t(k)))
    gexp[t] = XR[z, c]

    arrive(p_u)
    s = MG[:, u]
    for k in range(3):
        s = s + MXR[k]
    MXS[...] = s
    p_v = [send(MXS.at[next_to(4, v, k)], MYR.at[k - 1], along_v(k)) for k in (1, 2, 3)]
    arrive(a_u)
    s = DWS[:, :, u].astype(F32)
    for k in range(3):
        s = s + XW[k].astype(F32)
    XS[...] = s.astype(BF)
    a_2 = [
        send(XS.at[next_to(4, z, kz), next_to(4, v, kv)], ZW.at[kz * 4 + kv], along_vz(kv, kz))
        for kv, kz in VZ
    ]
    arrive(p_v)
    s = MXS[v]
    for k in range(3):
        s = s + MYR[k]
    MYS[t] = s
    p_t = [send(MYS.at[t], MYS.at[t], along_t(k)) for k in range(1, 8)]
    for kz in (1, 3, 2):
        o_z[kz].wait_recv()
    moe = CSM[z].astype(F32)
    for k in range(3):
        moe = moe + ZRM[k].astype(F32)
    out[...] = (((resid[...] + moe) * alive)[0:L, :]).astype(BF)
    arrive(a_2)
    s = XS[z, v].astype(F32)
    for kv, kz in VZ:
        s = s + ZW[kz * 4 + kv].astype(F32)
    gw[...] = s
    arrive(p_t)
    s = MYS[0]
    for k in range(1, 8):
        s = s + MYS[k]
    gm[...] = s
    arrive(g_t)
    for cp in sent:
        cp.wait_send()
    for h in range(8):
        for k in (1, 2, 3):
            grad_copy(h, k).wait_send()
    for hz in range(4):
        swap_copy(hz).wait_send()


def finish(gexp, gw, gm, out_in, tg_in, out, tg, g_in, g_out, g_qkv, g_o, g_router, g_one, g_two):
    out[...] = out_in[...]
    tg[...] = tg_in[...]
    g_in[...] = gexp[:, :, 0:256].astype(F32)
    g_out[...] = gexp[:, :, 256:512].astype(F32)
    g_qkv[...] = gw[:, 0:192]
    g_o[...] = gw[:, 192:256]
    g_router[...] = gm[:, 0:32]
    rows = jnp.transpose(gm[...])
    g_one[...] = rows[32:33, :]
    g_two[...] = rows[33:34, :]


def body(
    tokens, image_counts, choices, gain_attn, qkv_weight, out_weight, gain_moe, router_weight,
    expert_in, expert_out, cotangent,
):
    vm = pl.BlockSpec(memory_space=pltpu.VMEM)
    sm = pl.BlockSpec(memory_space=pltpu.SMEM)

    def buf(*shape, dtype=BF):
        return pltpu.VMEM(shape, dtype)

    scratch = [
        buf(2, 4, 4, 4, 32, 256),
        buf(4, 4, 32, 128),
        buf(4, 2, 4, 32, 512),
        buf(4, 2, 4, 4, 32, 512),
        buf(N_IMG, LQ, D),
        buf(N_IMG, LQ, D),
        buf(4 * SLOT, ROWS),
        buf(4, SLOT, 1024),
        buf(4, SLOT, 1024),
        buf(4, SLOT, 1024),
        buf(4, SLOT, 1024),
        buf(4 * SLOT, D),
        buf(4 * SLOT, D, dtype=F32),
        buf(4 * SLOT, D, dtype=F32),
        buf(4, 2, 4 * SLOT, 256),
        buf(4, 2, 4 * SLOT, 256),
        buf(D, 4 * SLOT),
        buf(D, 4 * SLOT),
        buf(3, 4, 2, 4, 32, 512),
        buf(4, 2, 4, 32, 512),
        buf(4, 2, 4, 32, 512),
        buf(N_IMG, LP + 16, D),
        buf(N_IMG, LP, D),
        buf(4, LP + 16, D),
        buf(4, LP, D),
        buf(4, LP + 16, D),
        buf(4, LP, D),
        buf(3, LP + 16, D),
        buf(3, LP, D),
        buf(LP, D, dtype=F32),
        buf(LP, D, dtype=F32),
        buf(LP, D),
        buf(8, LP, 256),
        buf(8, LP, LP, dtype=F32),
        buf(8, LP, 64),
        buf(LP, D, dtype=F32),
        buf(LP, D, dtype=F32),
        buf(LP, 128, dtype=F32),
        buf(8, ROWS, dtype=jnp.int32),
        buf(8, ROWS, dtype=F32),
        buf(4 * SLOT, 128, dtype=F32),
        buf(2, 4, 4, 4, 32, 256),
        buf(4, 4, 4, 32, 256),
        buf(4, 4, 4, 32, 256),
        buf(3, 4, 4, 32, 256),
        buf(4, 4, 32, 256),
        buf(16, 32, 256),
        buf(4, 4, 32, 128, dtype=F32),
        buf(3, 4, 32, 128, dtype=F32),
        buf(4, 32, 128, dtype=F32),
        buf(3, 32, 128, dtype=F32),
        buf(8, 32, 128, dtype=F32),
        pltpu.SemaphoreType.DMA((N_SEM,)),
        pltpu.SemaphoreType.DMA((N_SEM,)),
        pltpu.SemaphoreType.DMA((8,)),
    ]
    out, tg, gw, gm, gexp = pl.pallas_call(
        kernel,
        name="block",
        out_shape=[
            jax.ShapeDtypeStruct((L, D), BF),
            jax.ShapeDtypeStruct((L, D), F32),
            jax.ShapeDtypeStruct((32, 256), F32),
            jax.ShapeDtypeStruct((32, 128), F32),
            jax.ShapeDtypeStruct((8, 4, 32, 512), BF),
        ],
        in_specs=[sm] + [vm] * 10,
        out_specs=[vm] * 5,
        scratch_shapes=scratch,
        compiler_params=pltpu.CompilerParams(
            collective_id=0, has_side_effects=True, vmem_limit_bytes=60 * 2**20
        ),
    )(
        image_counts, tokens, cotangent, choices.T, qkv_weight, out_weight.T, router_weight,
        gain_attn[None, :], gain_moe[None, :], expert_in, expert_out.transpose(0, 2, 1),
    )
    out, tg, g_in, g_out, g_qkv, g_o, g_router, g_one, g_two = pl.pallas_call(
        finish,
        name="finish",
        out_shape=[
            jax.ShapeDtypeStruct((L, D), BF),
            jax.ShapeDtypeStruct((L, D), F32),
            jax.ShapeDtypeStruct((32, 32, 256), F32),
            jax.ShapeDtypeStruct((32, 32, 256), F32),
            jax.ShapeDtypeStruct((32, 192), F32),
            jax.ShapeDtypeStruct((32, 64), F32),
            jax.ShapeDtypeStruct((32, 32), F32),
            jax.ShapeDtypeStruct((1, 32), F32),
            jax.ShapeDtypeStruct((1, 32), F32),
        ],
        in_specs=[vm] * 5,
        out_specs=[vm] * 9,
        compiler_params=pltpu.CompilerParams(vmem_limit_bytes=32 * 2**20),
    )(gexp.reshape(32, 32, 512), gw, gm, out, tg)
    return (
        out, tg, g_one.reshape(32), g_qkv, g_o.T, g_two.reshape(32), g_router, g_in,
        g_out.transpose(0, 2, 1),
    )


def solution(mesh):
    rows = P(("dp", "tensor"), None)
    in_specs = (
        rows, P("dp"), P("dp", None), P("dp"), P("dp", "tensor"), P("tensor", "dp"), P("dp"),
        P("dp", None), P(None, "dp", "tensor"), P(None, "tensor", "dp"), rows,
    )
    out_specs = (
        rows, rows, P("dp"), P("dp", "tensor"), P("tensor", "dp"), P("dp"), P("dp", None),
        P(None, "dp", "tensor"), P(None, "tensor", "dp"),
    )
    return jax.shard_map(body, mesh=mesh, in_specs=in_specs, out_specs=out_specs, check_vma=False)
```

time: 196 us -> 142 us (0.72)
  Pallas kernels: 186 us -> 136 us
  local copies, waits for them, and re-layouts: 7.53 us -> 4.62 us
    pallas_call x1, Pallas kernels: 184 us -> 135 us  [body(): pl.pallas_call(kernel, name='block', out_shape=[jax.ShapeDtypeStruct((L,...]
    unnamed x24 -> x10, local copies, waits for them, and re-layouts: 5.91 us -> 4.62 us
where the time goes in v2:
time: 142 us
  Pallas kernels  136 us (96%)
  local copies, waits for them, and re-layouts  4.62 us (3%)
    pallas_call x1, Pallas kernels, body(): pl.pallas_call(kernel, name='block', out_shape=[jax.ShapeDtypeStruct((L,...  135 us
    unnamed x10, local copies, waits for them, and re-layouts  4.62 us

profile of v2, /device:TPU:1, one launch (start us, length us, event | category | flops | bytes accessed | tf_op | source)
XLA Modules:
  0.0 142.1 jit_solution(18333189296269277377)
XLA Ops:
  1.3 134.6 %block.1 = (bf16[197,512]{1,0:T(8,128)(2,1)}, f32[197,512]{1,0:T(8,128)}, f32[32,256]{1,0:T(8,128)}, f32[32,128]{1,0:T(8,128)}, bf16[8,4,32,512]{3,2,1,0:T(8,128)(2,1)}) custom-call(s32[1]{0:T(128)S(6)} %copy.20.cnt, bf16[197,512]{1,0:T(8,128)(2,1)} %tok.1, bf16[197,512]{1,0:T(8,128)(2,1)} %cot.1, s32[2,1576]{1,0:T(2,128)} %bitcast.12, ...), custom_call_target="tpu_custom_call" | custom-call | tf_op jit(solution)/shard_map/block/pallas_call | solution.py:685
  135.9 0.0 copy-start
  135.9 1.2 copy-done
  137.1 0.0 copy-start.1
  137.1 1.0 copy-done.1
  138.1 0.0 copy-start.2
  138.1 0.9 copy-done.2
  139.0 0.0 copy-start.3
  139.0 0.8 copy-done.3
  139.8 0.0 copy-start.4
  139.8 0.7 copy-done.4
  140.5 1.6 %finish.1 = (bf16[197,512]{1,0:T(8,128)(2,1)}, f32[197,512]{1,0:T(8,128)}, f32[32,32,256]{2,1,0:T(8,128)}, f32[32,32,256]{2,1,0:T(8,128)}, f32[32,192]{1,0:T(8,1...) custom-call(bf16[32,32,512]{2,1,0:T(8,128)(2,1)S(1)} %bitcast.10, ...), custom_call_target="tpu_custom_call" | custom-call | tf_op jit(solution)/shard_map/finish/pallas_call | solution.py:705
Async XLA Ops:
  135.9 1.2 copy-start
  137.1 1.0 copy-start.1
  138.1 0.9 copy-start.2
  139.0 0.8 copy-start.3
  139.8 0.7 copy-start.4

commit v3 on v2

--- a/solution.py
+++ b/solution.py
@@ -54,9 +54,9 @@
 def kernel(
     cnt, tok, cot, picks, qkv_in, out_in, router_in, gain_one_in, gain_two_in, ein, eout,
     out, tg, gw, gm, gexp,
-    W, M, T1, EW, CG, N2G, PM, SB, RB, SB2, RB2, DS, racc, dxacc, ACT, DIN, XT, GT,
+    W, M, T1, EW, CG, N2G, PM, SB, RB, SB2, RB2, DS, racc, dxacc, ACT, DIN, INN, DAC, XT, GT,
     YR, YS, XR, CPD, CPM, CRD, CRM, CSD, CSM, ZRD, ZRM,
-    xs, cpad, n1s, QKV, PF, MX, resid, xh2s, r2s, chs, pos, gates,
+    toks, cots, outs, tgs, xs, cpad, n1s, QKV, PF, MX, DM, DSC, DQ, resid, xh2s, r2s, chs, pos, gates,
     dW, DWC, DWS, XW, XS, ZW, MG, MXR, MXS, MYR, MYS,
     send_sem, recv_sem, loc_sem,
 ):
@@ -133,6 +133,7 @@
     for p in peers:
         pl.semaphore_signal(bar, inc=1, device_id=p, device_id_type=MESH)
 
+    load_tok, load_cot = local(tok, toks), local(cot, cots)
     eye_r = lax.broadcasted_iota(jnp.int32, (32, 32), 0)
     eye_c = lax.broadcasted_iota(jnp.int32, (32, 32), 1)
 
@@ -145,14 +146,6 @@
     M[v, u, :, 0:32] = router_in[...]
     M[v, u, :, 32:33] = column(gain_one_in[...]).astype(BF)
     M[v, u, :, 33:34] = column(gain_two_in[...]).astype(BF)
-    xs[...] = jnp.zeros((LP, D), F32)
-    xs[0:L, :] = tok[...].astype(F32)
-    cpad[...] = jnp.zeros((LP, D), F32)
-    cpad[0:L, :] = cot[...].astype(F32)
-    for i in range(N_IMG):
-        CG[i, LP:LQ, :] = jnp.zeros((LQ - LP, D), BF)
-        N2G[i, LP:LQ, :] = jnp.zeros((LQ - LP, D), BF)
-    CG[t, 0:LP, :] = cpad[...].astype(BF)
     pl.semaphore_wait(bar, len(peers))
 
     w_1 = [send(W.at[c, z, v, u], W.at[c, z, v, u], along_vz(*k)) for k in VZ]
@@ -204,6 +197,17 @@
         for k in (1, 2, 3):
             cp = third_hop_copy(ZORDER.index(kz), k, zi)
             cp.start()
+
+    load_tok.wait()
+    load_cot.wait()
+    xs[...] = jnp.zeros((LP, D), F32)
+    xs[0:L, :] = toks[...].astype(F32)
+    cpad[...] = jnp.zeros((LP, D), F32)
+    cpad[0:L, :] = cots[...].astype(F32)
+    for i in range(N_IMG):
+        CG[i, LP:LQ, :] = jnp.zeros((LQ - LP, D), BF)
+        N2G[i, LP:LQ, :] = jnp.zeros((LQ - LP, D), BF)
+    CG[t, 0:LP, :] = cpad[...].astype(BF)
 
     chs[...] = jnp.full((8, ROWS), -1, jnp.int32)
     for i in range(N_IMG):
@@ -230,10 +234,13 @@
     pos[0:4, :] = jnp.where(place < CAP, place, 999.0)
 
     arrive(w_1)
-    w_u = [send(W.at[c, :, :, u], W.at[c, :, :, u], along_u(k)) for k in (1, 2, 3)]
+    w_u, w_c = [], []
+    for i in range(4):
+        w_u.append([send(W.at[c, i, :, u], W.at[c, i, :, u], along_u(k)) for k in (1, 2, 3)])
     arrive(m_1)
     m_u = [send(M.at[:, u], M.at[:, u], along_u(k)) for k in (1, 2, 3)]
-    w_c = [send(W.at[c, :, :, u], W.at[c, :, :, u], core)]
+    for i in range(4):
+        w_c.append([send(W.at[c, i, :, u], W.at[c, i, :, u], core)])
     first_arrived(0)
     second_hop(0)
     c_z = [send(CG.at[t, pl.ds(0, LP)], CG.at[t, pl.ds(0, LP)], along_z(k)) for k in (1, 2, 3)]
@@ -255,44 +262,50 @@
     gain_one, gain_two = small_rows[32:33, :], small_rows[33:34, :]
     unit, _ = normalize(xs[...])
     n1s[...] = (unit * gain_one).astype(BF)
-    resid[...] = xs[...]
-
-    for k in (1, 2, 3):
-        w_u[k - 1].wait_recv()
-        ui = next_to(4, u, 4 - k)
-        w_c.append(send(W.at[c, :, :, ui], W.at[c, :, :, ui], core))
+
+    lane = lax.broadcasted_iota(jnp.int32, (LP, LP), 1)
+
+    def weights_of(h):
+        if h % 2 == 0:
+            return W[0, h // 2].reshape(D, 256)
+        return jnp.concatenate([W[1, h // 2, xi, yi] for yi in range(4) for xi in range(4)], 0)
+
+    def pass_on(i):
+        for k in (1, 2, 3):
+            w_u[i][k - 1].wait_recv()
+            ui = next_to(4, u, 4 - k)
+            w_c[i].append(send(W.at[c, i, :, ui], W.at[c, i, :, ui], core))
+
+    def project(i):
+        arrive(w_c[i])
+        for h in (2 * i, 2 * i + 1):
+            QKV[h] = dot(n1s[...], weights_of(h)).astype(BF)
+
+    pass_on(0)
+    pass_on(1)
     third_hop(0)
+    project(0)
+    pass_on(2)
+    project(1)
+    pass_on(3)
     first_arrived(2)
     second_hop(2)
-    arrive(w_c)
-
-    lane = lax.broadcasted_iota(jnp.int32, (LP, LP), 1)
-
-    def weights_of(hz, hc):
-        if hc == 0:
-            return W[0, hz].reshape(D, 256)
-        return jnp.concatenate([W[1, hz, xi, yi] for yi in range(4) for xi in range(4)], 0)
-
-    def head_forward(hz, carry):
-        for hc in range(2):
-            h = hz * 2 + hc
-            wt = weights_of(hz, hc)
-            qkv = dot(n1s[...], wt).astype(BF)
-            QKV[h] = qkv
-            scores = dot_nt(qkv[:, 0:64], qkv[:, 64:128]) * 0.125
-            scores = jnp.where(lane < L, scores, -1e30)
-            e = jnp.exp(scores - jnp.max(scores, -1, keepdims=True))
-            probs = e * (1.0 / jnp.sum(e, -1, keepdims=True))
-            PF[h] = probs
-            mixed = dot(probs.astype(BF), qkv[:, 128:192]).astype(BF)
-            MX[h] = mixed
-            resid[...] += dot_nt(mixed, wt[:, 192:256])
-        return carry
-
-    lax.fori_loop(0, 2, head_forward, 0)
+    project(2)
     third_hop(1)
-    third_hop(3)
-    lax.fori_loop(2, 4, head_forward, 0)
+    project(3)
+    for h in range(8):
+        qkv = QKV[h]
+        PF[h] = jnp.where(lane < L, dot_nt(qkv[:, 0:64], qkv[:, 64:128]) * 0.125, -1e30)
+    for h in range(8):
+        scores = PF[h]
+        e = jnp.exp(scores - jnp.max(scores, -1, keepdims=True))
+        PF[h] = e * (1.0 / jnp.sum(e, -1, keepdims=True))
+    for h in range(8):
+        MX[h] = dot(PF[h].astype(BF), QKV[h][:, 128:192]).astype(BF)
+    attended = xs[...]
+    for h in range(8):
+        attended = attended + dot_nt(MX[h], weights_of(h)[:, 192:256])
+    resid[...] = attended
 
     unit_two, inv_two = normalize(resid[...])
     xh2s[...] = unit_two
@@ -301,6 +314,7 @@
     N2G[t, 0:LP, :] = jnp.where(real, unit_two * gain_two, 0.0).astype(BF)
     n_z = [send(N2G.at[t, pl.ds(0, LP)], N2G.at[t, pl.ds(0, LP)], along_z(k)) for k in (2, 1, 3)]
     n_c = [send(N2G.at[t, pl.ds(0, LP)], N2G.at[t, pl.ds(0, LP)], core)]
+    third_hop(3)
     third_hop(2)
     for k, cp in zip((1, 2, 3), c_z):
         cp.wait_recv()
@@ -339,68 +353,97 @@
     grad_e = RB[:, :, 512:1024].reshape(4 * SLOT, D)
     racc[...] = jnp.zeros((4 * SLOT, D), F32)
     dxacc[...] = jnp.zeros((4 * SLOT, D), F32)
+    XT[...] = jnp.transpose(rows_e)
+    GT[...] = jnp.transpose(grad_e)
+    g_v_base = take(12)
+
+    def z_of(i):
+        kz = ZORDER[i] if isinstance(i, int) else jnp.where(i < 2, i, 5 - i)
+        return lax.rem(z + 4 - kz, 4)
+
+    def grad_copy(i, k):
+        zi = z_of(i)
+        return remote(
+            EW.at[zi, :, next_to(4, v, k)], YR.at[k - 1, zi], along_v(k), g_v_base + 3 * i + k - 1
+        )
 
     def tile_of(zi, ci, lanes):
         return jnp.concatenate([EW[zi, ci, vi, ui, :, lanes] for vi, ui in natural], 0)
 
-    def hidden_group(i, carry):
-        kz = jnp.where(i < 2, i, 5 - i)
-        zi = lax.rem(z + 4 - kz, 4)
+    def hidden_units(i, carry):
+        zi = z_of(i)
         for k in (1, 2, 3):
             third_hop_copy(i, k, zi).wait_recv()
-
-        def hidden(ci, carry):
-            w_first = tile_of(zi, ci, slice(0, 256))
-            w_second = tile_of(zi, ci, slice(256, 512))
-            inner = dot(rows_e, w_first)
+        for ci in range(2):
+            INN[ci] = dot(rows_e, tile_of(zi, ci, slice(0, 256)))
+        for ci in range(2):
+            DAC[ci] = dot(grad_e, tile_of(zi, ci, slice(256, 512)))
+        for ci in range(2):
+            inner = INN[ci]
             sq = inner * inner
             th = jnp.tanh(inner * (0.7978845608028654 + (0.7978845608028654 * 0.044715) * sq))
             half = 0.5 + 0.5 * th
-            act = (inner * half).astype(BF)
+            ACT[ci] = (inner * half).astype(BF)
             slope = half + 0.5 * inner * (1.0 - th * th) * (
                 0.7978845608028654 + (3 * 0.7978845608028654 * 0.044715) * sq
             )
-            d_inner = (dot(grad_e, w_second) * slope).astype(BF)
-            ACT[zi, ci] = act
-            DIN[zi, ci] = d_inner
-            racc[...] += dot_nt(act, w_second)
-            dxacc[...] += dot_nt(d_inner, w_first)
-            return carry
-
-        return lax.fori_loop(0, 2, hidden, carry)
-
-    lax.fori_loop(0, 4, hidden_group, 0)
+            DIN[ci] = (DAC[ci] * slope).astype(BF)
+        acc = racc[...]
+        for ci in range(2):
+            acc = acc + dot_nt(ACT[ci], tile_of(zi, ci, slice(256, 512)))
+        racc[...] = acc
+        acc = dxacc[...]
+        for ci in range(2):
+            acc = acc + dot_nt(DIN[ci], tile_of(zi, ci, slice(0, 256)))
+        dxacc[...] = acc
+        for k in (1, 2, 3):
+            third_hop_copy(i, k, zi).wait_send()
+        for ci in range(2):
+            grad = dot(XT[...], DIN[ci]).astype(BF)
+            for b, (vi, ui) in enumerate(natural):
+                EW[zi, ci, vi, ui, :, 0:256] = grad[b * 32 : (b + 1) * 32, :]
+        for ci in range(2):
+            grad = dot(GT[...], ACT[ci]).astype(BF)
+            for b, (vi, ui) in enumerate(natural):
+                EW[zi, ci, vi, ui, :, 256:512] = grad[b * 32 : (b + 1) * 32, :]
+        for k in (1, 2, 3):
+            grad_copy(i, k).start()
+        return carry
+
+    lax.fori_loop(0, 4, hidden_units, 0)
     SB2[:, :, 0:512] = racc[...].astype(BF).reshape(4, SLOT, D)
     SB2[:, :, 512:1024] = dxacc[...].astype(BF).reshape(4, SLOT, D)
     b_u = [send(SB2.at[next_to(4, u, k)], RB2.at[u], along_u(k)) for k in (1, 2, 3)]
     RB2[u] = SB2[u]
 
-    dEW = EW
-    for i in range(4):
+    g_u, g_t = {}, []
+
+    def sum_over_v(i):
+        zi = z_of(i)
         for k in (1, 2, 3):
-            third_hop_copy(i, k, next_to(4, z, 4 - ZORDER[i])).wait_send()
-    XT[...] = jnp.transpose(rows_e)
-    GT[...] = jnp.transpose(grad_e)
-    g_v_base = take(24)
-
-    def grad_copy(h, k):
-        zi, ci = lax.div(h, 2), lax.rem(h, 2)
-        return remote(
-            dEW.at[zi, ci, next_to(4, v, k)], YR.at[k - 1, zi, ci], along_v(k), g_v_base + 3 * h + k - 1
-        )
-
-    def expert_grads(h, carry):
-        zi, ci = lax.div(h, 2), lax.rem(h, 2)
-        g_first = dot(XT[...], DIN[zi, ci]).astype(BF)
-        g_second = dot(GT[...], ACT[zi, ci]).astype(BF)
-        for i, (vi, ui) in enumerate(natural):
-            dEW[zi, ci, vi, ui, :, 0:256] = g_first[i * 32 : (i + 1) * 32, :]
-            dEW[zi, ci, vi, ui, :, 256:512] = g_second[i * 32 : (i + 1) * 32, :]
-        for k in (1, 2, 3):
-            grad_copy(h, k).start()
-        return carry
-
-    lax.fori_loop(0, 8, expert_grads, 0)
+            grad_copy(i, k).wait_recv()
+        for ci in range(2):
+            s = EW[zi, ci, v].astype(F32)
+            for k in range(3):
+                s = s + YR[k, zi, ci].astype(F32)
+            YS[zi, ci] = s.astype(BF)
+        g_u[i] = [
+            send(YS.at[zi, :, next_to(4, u, k)], XR.at[zi, :, u], along_u(k)) for k in (1, 2, 3)
+        ]
+        for ci in range(2):
+            XR[zi, ci, u] = YS[zi, ci, u]
+
+    def last_hop(i):
+        zi = z_of(i)
+        arrive(g_u[i])
+        for kc in (0, 1):
+            ci = c + kc * (oc - c)
+            if i == 0 and kc == 0:
+                g_t.append(local(XR.at[zi, ci], gexp.at[t]))
+            else:
+                g_t.append(send(XR.at[zi, ci], gexp.at[t], {"tensor": 2 * zi + ci}))
+
+    sum_over_v(0)
     arrive(b_u)
 
     res = RB2[:, :, 0:512].reshape(4 * SLOT, D)
@@ -447,25 +490,12 @@
         if kz:
             o_z[kz] = send(CSM.at[i], ZRM.at[kz - 1], along_z(kz))
 
-    g_u = {}
-
-    def sum_over_v(zi):
-        for ci in range(2):
-            for k in (1, 2, 3):
-                grad_copy(2 * zi + ci, k).wait_recv()
-            s = dEW[zi, ci, v].astype(F32)
-            for k in range(3):
-                s = s + YR[k, zi, ci].astype(F32)
-            YS[zi, ci] = s.astype(BF)
-        g_u[zi] = [
-            send(YS.at[zi, :, next_to(4, u, k)], XR.at[zi, :, u], along_u(k)) for k in (1, 2, 3)
-        ]
-        for ci in range(2):
-            XR[zi, ci, u] = YS[zi, ci, u]
-
-    sum_over_v(0)
     sum_over_v(1)
-
+    last_hop(0)
+    sum_over_v(2)
+    last_hop(1)
+    sum_over_v(3)
+    last_hop(2)
     for kz in (1, 3, 2):
         r_z[kz].wait_recv()
     total = CSD[z].astype(F32)
@@ -486,55 +516,45 @@
     router_part = dot_tn(n2_own, dl_high) + dot_tn(n2_own, dl_low)
     gain_two_part = jnp.sum(d_n2 * unit_two, 0, keepdims=True)
 
-    xs_grad = dxacc.at[0:LP]
-    xs_grad[...] = jnp.zeros((LP, D), F32)
     n1_cols = jnp.transpose(n1s[...])
     resid_cols = jnp.transpose(resid_low)
-    a_c_base = take(4)
-
-    def swap_copy(hz):
-        return remote(dW.at[oc, hz], DWC.at[hz], core, a_c_base + hz)
-
-    def head_backward(hz, carry):
-        for hc in range(2):
-            h = hz * 2 + hc
-            wt = weights_of(hz, hc)
-            qkv = QKV[h]
-            q, key, val = qkv[:, 0:64], qkv[:, 64:128], qkv[:, 128:192]
-            d_mixed = dot(resid_low, wt[:, 192:256]).astype(BF)
-            probs = PF[h]
-            d_probs = dot_nt(d_mixed, val)
-            d_scores = probs * (d_probs - jnp.sum(probs * d_probs, -1, keepdims=True))
-            d_scores = d_scores.astype(BF)
-            dq = dot(d_scores, key) * 0.125
-            dk = dot_tn(d_scores, q) * 0.125
-            dv = dot_tn(probs.astype(BF), d_mixed)
-            d_qkv = jnp.concatenate([dq, dk, dv], 1).astype(BF)
-            xs_grad[...] += dot_nt(d_qkv, wt[:, 0:192])
-            grad = jnp.concatenate([dot(n1_cols, d_qkv), dot(resid_cols, MX[h])], 1).astype(BF)
-            if hc == 0:
-                dW[0, hz] = grad.reshape(4, 4, 32, 256)
-            else:
-                for yi in range(4):
-                    for xi in range(4):
-                        b = (yi * 4 + xi) * 32
-                        dW[1, hz, xi, yi] = grad[b : b + 32]
-        swap_copy(hz).start()
-        return carry
-
-    lax.fori_loop(0, 2, head_backward, 0)
-    sum_over_v(2)
-    sum_over_v(3)
-    lax.fori_loop(2, 4, head_backward, 0)
+    for h in range(8):
+        DM[h] = dot(resid_low, weights_of(h)[:, 192:256]).astype(BF)
+    for h in range(8):
+        DSC[h] = dot_nt(DM[h], QKV[h][:, 128:192])
+    for h in range(8):
+        probs, d_probs = PF[h], DSC[h]
+        DSC[h] = probs * (d_probs - jnp.sum(probs * d_probs, -1, keepdims=True))
+    for h in range(8):
+        DQ[h, :, 0:64] = (dot(DSC[h].astype(BF), QKV[h][:, 64:128]) * 0.125).astype(BF)
+    for h in range(8):
+        DQ[h, :, 128:192] = dot_tn(PF[h].astype(BF), DM[h]).astype(BF)
+    for h in range(8):
+        DQ[h, :, 64:128] = (dot_tn(DSC[h].astype(BF), QKV[h][:, 0:64]) * 0.125).astype(BF)
+    a_c = []
+    for h in range(8):
+        grad = jnp.concatenate([dot(n1_cols, DQ[h, :, 0:192]), dot(resid_cols, MX[h])], 1).astype(BF)
+        hz = h // 2
+        if h % 2 == 0:
+            dW[0, hz] = grad.reshape(4, 4, 32, 256)
+        else:
+            for yi in range(4):
+                for xi in range(4):
+                    b = (yi * 4 + xi) * 32
+                    dW[1, hz, xi, yi] = grad[b : b + 32]
+            a_c.append(send(dW.at[oc, hz], DWC.at[hz], core))
+    d_n1 = jnp.zeros((LP, D), F32)
+    for h in range(8):
+        d_n1 = d_n1 + dot_nt(DQ[h, :, 0:192], weights_of(h)[:, 0:192])
+    last_hop(3)
 
     a_u = []
     for i in range(4):
-        swap_copy(i).wait_recv()
+        a_c[i].wait_recv()
         DWS[i] = (dW[c, i].astype(F32) + DWC[i].astype(F32)).astype(BF)
         a_u += [
             send(DWS.at[i, :, next_to(4, u, k)], XW.at[k - 1, i], along_u(k)) for k in (1, 2, 3)
         ]
-    d_n1 = xs_grad[...]
     unit, inv = normalize(xs[...])
     gain_one_part = jnp.sum(d_n1 * unit, 0, keepdims=True)
     gains = jnp.concatenate([gain_one_part, gain_two_part, jnp.zeros((126, D), F32)], 0)
@@ -544,16 +564,9 @@
     for i, (vi, ui) in enumerate(natural):
         MG[vi, ui] = merged[i * 32 : (i + 1) * 32]
     p_u = [send(MG.at[:, next_to(4, u, k)], MXR.at[k - 1], along_u(k)) for k in (1, 2, 3)]
-    tg[...] = (d_resid + normalize_back(d_n1 * gain_one, unit, inv))[0:L, :]
-
-    g_t = []
-
-    for zi in range(4):
-        arrive(g_u[zi])
-    for k in range(1, 8):
-        to = next_to(8, t, k)
-        g_t.append(send(XR.at[lax.div(to, 2), lax.rem(to, 2)], gexp.at[t], along_t(k)))
-    gexp[t] = XR[z, c]
+    tgs[...] = (d_resid + normalize_back(d_n1 * gain_one, unit, inv))[0:L, :]
+    store_tg = local(tgs, tg)
+
 
     arrive(p_u)
     s = MG[:, u]
@@ -581,7 +594,8 @@
     moe = CSM[z].astype(F32)
     for k in range(3):
         moe = moe + ZRM[k].astype(F32)
-    out[...] = (((resid[...] + moe) * alive)[0:L, :]).astype(BF)
+    outs[...] = (((resid[...] + moe) * alive)[0:L, :]).astype(BF)
+    store_out = local(outs, out)
     arrive(a_2)
     s = XS[z, v].astype(F32)
     for kv, kz in VZ:
@@ -592,14 +606,15 @@
     for k in range(1, 8):
         s = s + MYS[k]
     gm[...] = s
-    arrive(g_t)
+    arrive(g_t[1:])
+    g_t[0].wait()
+    store_tg.wait()
+    store_out.wait()
     for cp in sent:
         cp.wait_send()
-    for h in range(8):
+    for i in range(4):
         for k in (1, 2, 3):
-            grad_copy(h, k).wait_send()
-    for hz in range(4):
-        swap_copy(hz).wait_send()
+            grad_copy(i, k).wait_send()
 
 
 def finish(gexp, gw, gm, out_in, tg_in, out, tg, g_in, g_out, g_qkv, g_o, g_router, g_one, g_two):
@@ -621,6 +636,7 @@
 ):
     vm = pl.BlockSpec(memory_space=pltpu.VMEM)
     sm = pl.BlockSpec(memory_space=pltpu.SMEM)
+    hbm = pl.BlockSpec(memory_space=pl.ANY)
 
     def buf(*shape, dtype=BF):
         return pltpu.VMEM(shape, dtype)
@@ -640,8 +656,10 @@
         buf(4 * SLOT, D),
         buf(4 * SLOT, D, dtype=F32),
         buf(4 * SLOT, D, dtype=F32),
-        buf(4, 2, 4 * SLOT, 256),
-        buf(4, 2, 4 * SLOT, 256),
+        buf(2, 4 * SLOT, 256),
+        buf(2, 4 * SLOT, 256),
+        buf(2, 4 * SLOT, 256, dtype=F32),
+        buf(2, 4 * SLOT, 256, dtype=F32),
         buf(D, 4 * SLOT),
         buf(D, 4 * SLOT),
         buf(3, 4, 2, 4, 32, 512),
@@ -655,12 +673,19 @@
         buf(4, LP, D),
         buf(3, LP + 16, D),
         buf(3, LP, D),
+        buf(L, D),
+        buf(L, D),
+        buf(L, D),
+        buf(L, D, dtype=F32),
         buf(LP, D, dtype=F32),
         buf(LP, D, dtype=F32),
         buf(LP, D),
         buf(8, LP, 256),
         buf(8, LP, LP, dtype=F32),
         buf(8, LP, 64),
+        buf(8, LP, 64),
+        buf(8, LP, LP, dtype=F32),
+        buf(8, LP, 256),
         buf(LP, D, dtype=F32),
         buf(LP, D, dtype=F32),
         buf(LP, 128, dtype=F32),
@@ -680,7 +705,7 @@
         buf(8, 32, 128, dtype=F32),
         pltpu.SemaphoreType.DMA((N_SEM,)),
         pltpu.SemaphoreType.DMA((N_SEM,)),
-        pltpu.SemaphoreType.DMA((8,)),
+        pltpu.SemaphoreType.DMA((12,)),
     ]
     out, tg, gw, gm, gexp = pl.pallas_call(
         kernel,
@@ -692,8 +717,8 @@
             jax.ShapeDtypeStruct((32, 128), F32),
             jax.ShapeDtypeStruct((8, 4, 32, 512), BF),
         ],
-        in_specs=[sm] + [vm] * 10,
-        out_specs=[vm] * 5,
+        in_specs=[sm, hbm, hbm] + [vm] * 6 + [hbm, hbm],
+        out_specs=[hbm, hbm, vm, vm, hbm],
         scratch_shapes=scratch,
         compiler_params=pltpu.CompilerParams(
             collective_id=0, has_side_effects=True, vmem_limit_bytes=60 * 2**20
@@ -718,7 +743,7 @@
         ],
         in_specs=[vm] * 5,
         out_specs=[vm] * 9,
-        compiler_params=pltpu.CompilerParams(vmem_limit_bytes=32 * 2**20),
+        compiler_params=pltpu.CompilerParams(vmem_limit_bytes=60 * 2**20),
     )(gexp.reshape(32, 32, 512), gw, gm, out, tg)
     return (
         out, tg, g_one.reshape(32), g_qkv, g_o.T, g_two.reshape(32), g_router, g_in,

time: 142 us -> 134 us (0.944)
  local copies, waits for them, and re-layouts: 4.62 us -> 0 us
  Pallas kernels: 136 us -> 133 us
    pallas_call x1, Pallas kernels: 135 us -> 130 us  [body(): pl.pallas_call(kernel, name='block', out_shape=[jax.ShapeDtypeStruct((L,...]
    unnamed x10 -> x0, local copies, waits for them, and re-layouts: 4.62 us -> none
    pallas_call x1, Pallas kernels: 1.58 us -> 3.05 us  [body(): pl.pallas_call(finish, name='finish', out_shape=[jax.ShapeDtypeStruct((L,...]
where the time goes in v3:
time: 134 us
  Pallas kernels  133 us (99%)
    pallas_call x1, Pallas kernels, body(): pl.pallas_call(kernel, name='block', out_shape=[jax.ShapeDtypeStruct((L,...  130 us
    pallas_call x1, Pallas kernels, body(): pl.pallas_call(finish, name='finish', out_shape=[jax.ShapeDtypeStruct((L,...  3.05 us

profile of v3, /device:TPU:1, one launch (start us, length us, event | category | flops | bytes accessed | tf_op | source)
XLA Modules:
  0.0 134.2 jit_solution(17712737112676054763)
XLA Ops:
  1.3 129.9 %block.1 = (bf16[197,512]{1,0:T(8,128)(2,1)}, f32[197,512]{1,0:T(8,128)}, f32[32,256]{1,0:T(8,128)}, f32[32,128]{1,0:T(8,128)}, bf16[8,4,32,512]{3,2,1,0:T(8,128)(2,1)}) custom-call(s32[1]{0:T(128)S(6)} %copy.20.cnt, bf16[197,512]{1,0:T(8,128)(2,1)} %tok.1, bf16[197,512]{1,0:T(8,128)(2,1)} %cot.1, s32[2,1576]{1,0:T(2,128)} %bitcast.12, ...), custom_call_target="tpu_custom_call" | custom-call | tf_op jit(solution)/shard_map/block/pallas_call | solution.py:710
  131.2 3.0 %finish.1 = (bf16[197,512]{1,0:T(8,128)(2,1)}, f32[197,512]{1,0:T(8,128)}, f32[32,32,256]{2,1,0:T(8,128)}, f32[32,32,256]{2,1,0:T(8,128)}, f32[32,192]{1,0:T(8,1...) custom-call(bf16[32,32,512]{2,1,0:T(8,128)(2,1)} %bitcast.10, ...), custom_call_target="tpu_custom_call" | custom-call | tf_op jit(solution)/shard_map/finish/pallas_call | solution.py:730

commit v4 on v3

--- a/solution.py
+++ b/solution.py
@@ -54,10 +54,10 @@
 def kernel(
     cnt, tok, cot, picks, qkv_in, out_in, router_in, gain_one_in, gain_two_in, ein, eout,
     out, tg, gw, gm, gexp,
-    W, M, T1, EW, CG, N2G, PM, SB, RB, SB2, RB2, DS, racc, dxacc, ACT, DIN, INN, DAC, XT, GT,
-    YR, YS, XR, CPD, CPM, CRD, CRM, CSD, CSM, ZRD, ZRM,
-    toks, cots, outs, tgs, xs, cpad, n1s, QKV, PF, MX, DM, DSC, DQ, resid, xh2s, r2s, chs, pos, gates,
-    dW, DWC, DWS, XW, XS, ZW, MG, MXR, MXS, MYR, MYS,
+    W, M, T1, EW, CG, N2G, PM, SBX, SBG, RBX, RBG, RBR, RBD, DS, racc, dxacc, ACT, DIN, INN, DAC, XT, GT,
+    YA, YB, CRD, CRM, CSD, CSM, ZRD, ZRM,
+    toks, cots, outs, tgs, xs, cpad, n1s, n2s, QKV, PF, MX, DM, DSC, DQ, resid, xh2s, r2s, chs, pos, gates,
+    dW, DWC, DWS, XW, XS, ZW, MG, MXR, MXS, MYR, MYS, GA, GB, GC,
     send_sem, recv_sem, loc_sem,
 ):
     d = lax.axis_index("dp")
@@ -112,6 +112,11 @@
         cp.start()
         sent.append(cp)
         return cp
+
+    def left(copies):
+        for cp in copies:
+            cp.wait_send()
+            sent[:] = [q for q in sent if q is not cp]
 
     def local(src, dst):
         i = used[1]
@@ -184,19 +189,28 @@
         ]
         e_2[kz].append(local(T1.at[zi, :, u], EW.at[zi, :, v, u]))
 
-    e_3_base = take(12)
-
-    def third_hop_copy(i, k, zi):
-        part = EW.at[zi, :, v]
-        return remote(part, part, along_v(k), e_3_base + 3 * i + k - 1)
+    e_3_base = take(16)
+
+    def third_hop_copy(i, n, zi):
+        step = (1, 3)[n % 2]
+        if n < 2:
+            part = EW.at[zi, :, v]
+        else:
+            part = EW.at[zi, n - 2, next_to(4, v, 4 - step)]
+        return remote(part, part, along_v(step), e_3_base + 4 * i + n)
 
     def third_hop(kz):
         arrive(e_2[kz][:3])
         e_2[kz][3].wait()
         zi = next_to(4, z, 4 - kz)
-        for k in (1, 2, 3):
-            cp = third_hop_copy(ZORDER.index(kz), k, zi)
-            cp.start()
+        for n in (0, 1):
+            third_hop_copy(ZORDER.index(kz), n, zi).start()
+
+    def third_hop_on(kz):
+        zi = next_to(4, z, 4 - kz)
+        for n in (0, 1):
+            third_hop_copy(ZORDER.index(kz), n, zi).wait_recv()
+            third_hop_copy(ZORDER.index(kz), n + 2, zi).start()
 
     load_tok.wait()
     load_cot.wait()
@@ -243,9 +257,6 @@
         w_c.append([send(W.at[c, i, :, u], W.at[c, i, :, u], core)])
     first_arrived(0)
     second_hop(0)
-    c_z = [send(CG.at[t, pl.ds(0, LP)], CG.at[t, pl.ds(0, LP)], along_z(k)) for k in (1, 2, 3)]
-    c_c = [send(CG.at[t, pl.ds(0, LP)], CG.at[t, pl.ds(0, LP)], core)]
-
     slot_ids = lax.broadcasted_iota(jnp.int32, (SLOT, ROWS), 0).astype(F32)
     for i in range(4):
         PM[i * SLOT : (i + 1) * SLOT, :] = jnp.where(slot_ids == pos[i : i + 1, :], 1.0, 0.0).astype(BF)
@@ -254,6 +265,8 @@
     second_hop(1)
     first_arrived(3)
     second_hop(3)
+    c_z = [send(CG.at[t, pl.ds(0, LP)], CG.at[t, pl.ds(0, LP)], along_z(k)) for k in (2, 1, 3)]
+    c_c = [send(CG.at[t, pl.ds(0, LP)], CG.at[t, pl.ds(0, LP)], core)]
 
     arrive(m_u)
     natural = [place_uv(yi, xi) for yi in range(4) for xi in range(4)]
@@ -293,6 +306,7 @@
     project(2)
     third_hop(1)
     project(3)
+    third_hop(3)
     for h in range(8):
         qkv = QKV[h]
         PF[h] = jnp.where(lane < L, dot_nt(qkv[:, 0:64], qkv[:, 64:128]) * 0.125, -1e30)
@@ -311,18 +325,21 @@
     xh2s[...] = unit_two
     r2s[...] = jnp.broadcast_to(inv_two, (LP, 128))
     real = lax.broadcasted_iota(jnp.int32, (LP, 1), 0) < L
-    N2G[t, 0:LP, :] = jnp.where(real, unit_two * gain_two, 0.0).astype(BF)
+    n2s[...] = jnp.where(real, unit_two * gain_two, 0.0).astype(BF)
+    N2G[t, 0:LP, :] = n2s[...]
     n_z = [send(N2G.at[t, pl.ds(0, LP)], N2G.at[t, pl.ds(0, LP)], along_z(k)) for k in (2, 1, 3)]
     n_c = [send(N2G.at[t, pl.ds(0, LP)], N2G.at[t, pl.ds(0, LP)], core)]
-    third_hop(3)
     third_hop(2)
-    for k, cp in zip((1, 2, 3), c_z):
+    third_hop_on(0)
+    for k, cp in sorted(zip((2, 1, 3), c_z), key=lambda kc: kc[0] % 2 == 0):
         cp.wait_recv()
         im = next_to(4, z, 4 - k) * 2 + c
         c_c.append(send(CG.at[im, pl.ds(0, LP)], CG.at[im, pl.ds(0, LP)], core))
     arrive(c_c)
+    third_hop_on(1)
     cot_slots = dot(PM[...], CG[...].reshape(ROWS, D))
     DS[...] = cot_slots.astype(BF)
+    third_hop_on(3)
     for k, cp in sorted(zip((2, 1, 3), n_z), key=lambda kc: kc[0] % 2 == 0):
         cp.wait_recv()
         im = next_to(4, z, 4 - k) * 2 + c
@@ -330,6 +347,11 @@
     arrive(n_c)
 
     rows_x = dot(PM[...], N2G[...].reshape(ROWS, D)).astype(BF)
+    SBX[...] = rows_x.reshape(4, SLOT, D)
+    for kz in range(4):
+        left(e_2[kz][:3])
+    s_x = [send(SBX.at[next_to(4, u, k)], RBX.at[u], along_u(k)) for k in (2, 1, 3)]
+    RBX[u] = SBX[u]
     lane_e = lax.broadcasted_iota(jnp.int32, (4 * SLOT, 128), 1)
     row_e = 4 * t + lax.div(lax.broadcasted_iota(jnp.int32, (4 * SLOT, 128), 0), SLOT)
 
@@ -343,95 +365,124 @@
     slot_router = router_of(rows_x).astype(BF).astype(F32)
     gate = jnp.sum(jnp.where(lane_e == row_e, slot_router, 0.0), -1, keepdims=True)
     gates[...] = jnp.broadcast_to(gate, (4 * SLOT, 128))
-    SB[:, :, 0:512] = rows_x.reshape(4, SLOT, D)
-    SB[:, :, 512:1024] = (DS[...].astype(F32) * gate).astype(BF).reshape(4, SLOT, D)
-    s_u = [send(SB.at[next_to(4, u, k)], RB.at[u], along_u(k)) for k in (1, 2, 3)]
-    RB[u] = SB[u]
-    arrive(s_u)
-
-    rows_e = RB[:, :, 0:512].reshape(4 * SLOT, D)
-    grad_e = RB[:, :, 512:1024].reshape(4 * SLOT, D)
+    SBG[...] = (DS[...].astype(F32) * gate).astype(BF).reshape(4, SLOT, D)
+    s_g = [send(SBG.at[next_to(4, u, k)], RBG.at[u], along_u(k)) for k in (2, 1, 3)]
+    RBG[u] = SBG[u]
+    third_hop_on(2)
+    arrive(s_x)
+
     racc[...] = jnp.zeros((4 * SLOT, D), F32)
     dxacc[...] = jnp.zeros((4 * SLOT, D), F32)
-    XT[...] = jnp.transpose(rows_e)
-    GT[...] = jnp.transpose(grad_e)
-    g_v_base = take(12)
 
     def z_of(i):
         kz = ZORDER[i] if isinstance(i, int) else jnp.where(i < 2, i, 5 - i)
         return lax.rem(z + 4 - kz, 4)
 
-    def grad_copy(i, k):
-        zi = z_of(i)
-        return remote(
-            EW.at[zi, :, next_to(4, v, k)], YR.at[k - 1, zi], along_v(k), g_v_base + 3 * i + k - 1
-        )
-
     def tile_of(zi, ci, lanes):
         return jnp.concatenate([EW[zi, ci, vi, ui, :, lanes] for vi, ui in natural], 0)
 
-    def hidden_units(i, carry):
+    def forward_units(i, carry):
         zi = z_of(i)
-        for k in (1, 2, 3):
-            third_hop_copy(i, k, zi).wait_recv()
+        for n in (0, 1):
+            third_hop_copy(i, n, zi).wait_send()
+            third_hop_copy(i, n + 2, zi).wait()
+        rows_e = RBX[...].reshape(4 * SLOT, D)
         for ci in range(2):
-            INN[ci] = dot(rows_e, tile_of(zi, ci, slice(0, 256)))
+            INN[i, ci] = dot(rows_e, tile_of(zi, ci, slice(0, 256)))
+        for ci in range(2):
+            inner = INN[i, ci]
+            sq = inner * inner
+            th = jnp.tanh(inner * (0.7978845608028654 + (0.7978845608028654 * 0.044715) * sq))
+            half = 0.5 + 0.5 * th
+            ACT[i, ci] = (inner * half).astype(BF)
+            INN[i, ci] = half + 0.5 * inner * (1.0 - th * th) * (
+                0.7978845608028654 + (3 * 0.7978845608028654 * 0.044715) * sq
+            )
+        acc = racc[...]
+        for ci in range(2):
+            acc = acc + dot_nt(ACT[i, ci], tile_of(zi, ci, slice(256, 512)))
+        racc[...] = acc
+        return carry
+
+    def backward_units(i, carry):
+        zi = z_of(i)
+        grad_e = RBG[...].reshape(4 * SLOT, D)
         for ci in range(2):
             DAC[ci] = dot(grad_e, tile_of(zi, ci, slice(256, 512)))
         for ci in range(2):
-            inner = INN[ci]
-            sq = inner * inner
-            th = jnp.tanh(inner * (0.7978845608028654 + (0.7978845608028654 * 0.044715) * sq))
-            half = 0.5 + 0.5 * th
-            ACT[ci] = (inner * half).astype(BF)
-            slope = half + 0.5 * inner * (1.0 - th * th) * (
-                0.7978845608028654 + (3 * 0.7978845608028654 * 0.044715) * sq
-            )
-            DIN[ci] = (DAC[ci] * slope).astype(BF)
-        acc = racc[...]
-        for ci in range(2):
-            acc = acc + dot_nt(ACT[ci], tile_of(zi, ci, slice(256, 512)))
-        racc[...] = acc
+            DIN[i, ci] = (DAC[ci] * INN[i, ci]).astype(BF)
         acc = dxacc[...]
         for ci in range(2):
-            acc = acc + dot_nt(DIN[ci], tile_of(zi, ci, slice(0, 256)))
+            acc = acc + dot_nt(DIN[i, ci], tile_of(zi, ci, slice(0, 256)))
         dxacc[...] = acc
-        for k in (1, 2, 3):
-            third_hop_copy(i, k, zi).wait_send()
+        return carry
+
+    lax.fori_loop(0, 4, forward_units, 0)
+    left(s_x)
+    SBX[...] = racc[...].astype(BF).reshape(4, SLOT, D)
+    b_r = [send(SBX.at[next_to(4, u, k)], RBR.at[u], along_u(k)) for k in (2, 1, 3)]
+    RBR[u] = SBX[u]
+    arrive(s_g)
+    lax.fori_loop(0, 4, backward_units, 0)
+    left(s_g)
+    SBG[...] = dxacc[...].astype(BF).reshape(4, SLOT, D)
+    b_d = [send(SBG.at[next_to(4, u, k)], RBD.at[u], along_u(k)) for k in (2, 1, 3)]
+    RBD[u] = SBG[u]
+
+    XT[...] = jnp.transpose(RBX[...].reshape(4 * SLOT, D))
+    GT[...] = jnp.transpose(RBG[...].reshape(4 * SLOT, D))
+    g_v_base = take(16)
+
+    def grad_copy(i, n):
+        zi = z_of(i)
+        step = (1, 3)[n % 2]
+        if n < 2:
+            return remote(
+                EW.at[zi, n, next_to(4, v, 2)], YA.at[n, zi], along_v(step), g_v_base + 4 * i + n
+            )
+        return remote(
+            EW.at[zi, :, next_to(4, v, step)], YB.at[n - 2, zi], along_v(step), g_v_base + 4 * i + n
+        )
+
+    def expert_grads(i, carry):
+        zi = z_of(i)
         for ci in range(2):
-            grad = dot(XT[...], DIN[ci]).astype(BF)
+            grad = dot(XT[...], DIN[i, ci]).astype(BF)
             for b, (vi, ui) in enumerate(natural):
                 EW[zi, ci, vi, ui, :, 0:256] = grad[b * 32 : (b + 1) * 32, :]
         for ci in range(2):
-            grad = dot(GT[...], ACT[ci]).astype(BF)
+            grad = dot(GT[...], ACT[i, ci]).astype(BF)
             for b, (vi, ui) in enumerate(natural):
                 EW[zi, ci, vi, ui, :, 256:512] = grad[b * 32 : (b + 1) * 32, :]
-        for k in (1, 2, 3):
-            grad_copy(i, k).start()
         return carry
 
-    lax.fori_loop(0, 4, hidden_units, 0)
-    SB2[:, :, 0:512] = racc[...].astype(BF).reshape(4, SLOT, D)
-    SB2[:, :, 512:1024] = dxacc[...].astype(BF).reshape(4, SLOT, D)
-    b_u = [send(SB2.at[next_to(4, u, k)], RB2.at[u], along_u(k)) for k in (1, 2, 3)]
-    RB2[u] = SB2[u]
+    lax.fori_loop(0, 4, expert_grads, 0)
+    for i in range(4):
+        for n in (0, 1):
+            grad_copy(i, n).start()
 
     g_u, g_t = {}, []
+    XR = T1
+
+    def add_over_v(i):
+        zi = z_of(i)
+        for n in (0, 1):
+            grad_copy(i, n).wait_recv()
+            part = next_to(4, v, (1, 3)[n])
+            EW[zi, n, part] = (EW[zi, n, part].astype(F32) + YA[n, zi].astype(F32)).astype(BF)
+            grad_copy(i, n + 2).start()
 
     def sum_over_v(i):
         zi = z_of(i)
-        for k in (1, 2, 3):
-            grad_copy(i, k).wait_recv()
+        for n in (2, 3):
+            grad_copy(i, n).wait_recv()
         for ci in range(2):
-            s = EW[zi, ci, v].astype(F32)
-            for k in range(3):
-                s = s + YR[k, zi, ci].astype(F32)
-            YS[zi, ci] = s.astype(BF)
+            s = EW[zi, ci, v].astype(F32) + YB[0, zi, ci].astype(F32) + YB[1, zi, ci].astype(F32)
+            EW[zi, ci, v] = s.astype(BF)
+            XR[zi, ci, u] = EW[zi, ci, v, u]
         g_u[i] = [
-            send(YS.at[zi, :, next_to(4, u, k)], XR.at[zi, :, u], along_u(k)) for k in (1, 2, 3)
+            send(EW.at[zi, :, v, next_to(4, u, k)], XR.at[zi, :, u], along_u(k)) for k in (1, 2, 3)
         ]
-        for ci in range(2):
-            XR[zi, ci, u] = YS[zi, ci, u]
 
     def last_hop(i):
         zi = z_of(i)
@@ -443,68 +494,70 @@
             else:
                 g_t.append(send(XR.at[zi, ci], gexp.at[t], {"tensor": 2 * zi + ci}))
 
-    sum_over_v(0)
-    arrive(b_u)
-
-    res = RB2[:, :, 0:512].reshape(4 * SLOT, D)
-    back = RB2[:, :, 512:1024].reshape(4 * SLOT, D)
+    left(c_z + c_c + n_z + n_c)
+    r_c, r_z, o_c, o_z = {}, {}, {}, {}
+    arrive(b_r)
+    res = RBR[...].reshape(4 * SLOT, D)
+
+    def columns_of(i):
+        return pl.ds(pl.multiple_of(i * LQ, LQ), LQ)
+
+    def moe_rows(i):
+        hot = PM[:, columns_of(i)] * gates[:, 0:1].astype(BF)
+        CG[i, 0:LP, :] = dot_tn(hot, res)[0:LP].astype(BF)
+
+    for kz in (2, 1, 3, 0):
+        i = next_to(4, z, kz)
+        moe_rows(2 * i + oc)
+        o_c[kz] = send(CG.at[2 * i + oc, pl.ds(0, LP)], CRM.at[i], core)
+    for kz in (2, 1, 3, 0):
+        moe_rows(2 * next_to(4, z, kz) + c)
     d_gate = jnp.sum(res.astype(F32) * DS[...].astype(F32), -1, keepdims=True)
     d_gate = jnp.where(lane_e == row_e, d_gate, 0.0).astype(BF)
-
-    def columns_of(i):
-        return pl.ds(pl.multiple_of(i * LQ, LQ), LQ)
+    arrive(b_d)
+
+    back = RBD[...].reshape(4 * SLOT, D)
 
     def grad_rows(i):
         hot = PM[:, columns_of(i)]
-        CPD[i, 0:LP, :] = dot_tn(hot, back)[0:LP].astype(BF)
+        N2G[i, 0:LP, :] = dot_tn(hot, back)[0:LP].astype(BF)
         by_expert = dot_tn(d_gate, hot)[0:32].astype(BF)
-        CPD[i, LP : LP + 16, 0:256] = by_expert[0:16]
-        CPD[i, LP : LP + 16, 256:512] = by_expert[16:32]
-
-    r_c, r_z, o_c, o_z = {}, {}, {}, {}
+        N2G[i, LP : LP + 16, 0:256] = by_expert[0:16]
+        N2G[i, LP : LP + 16, 256:512] = by_expert[16:32]
+
     for kz in (2, 1, 3, 0):
         i = next_to(4, z, kz)
         grad_rows(2 * i + oc)
-        r_c[kz] = send(CPD.at[2 * i + oc], CRD.at[i], core)
+        r_c[kz] = send(N2G.at[2 * i + oc, pl.ds(0, LP + 16)], CRD.at[i], core)
     for kz in (2, 1, 3, 0):
         i = next_to(4, z, kz)
         grad_rows(2 * i + c)
         r_c[kz].wait_recv()
-        CSD[i] = (CPD[2 * i + c].astype(F32) + CRD[i].astype(F32)).astype(BF)
+        CSD[i] = (N2G[2 * i + c, 0 : LP + 16].astype(F32) + CRD[i].astype(F32)).astype(BF)
         if kz:
             r_z[kz] = send(CSD.at[i], ZRD.at[kz - 1], along_z(kz))
-
-    def moe_rows(i):
-        hot = PM[:, columns_of(i)] * gates[:, 0:1].astype(BF)
-        CPM[i] = dot_tn(hot, res)[0:LP].astype(BF)
-
+    add_over_v(0)
     for kz in (2, 1, 3, 0):
         i = next_to(4, z, kz)
-        moe_rows(2 * i + oc)
-        o_c[kz] = send(CPM.at[2 * i + oc], CRM.at[i], core)
-    for kz in (2, 1, 3, 0):
-        i = next_to(4, z, kz)
-        moe_rows(2 * i + c)
         o_c[kz].wait_recv()
-        CSM[i] = (CPM[2 * i + c].astype(F32) + CRM[i].astype(F32)).astype(BF)
-        if kz:
-            o_z[kz] = send(CSM.at[i], ZRM.at[kz - 1], along_z(kz))
-
+        CSM[i] = (CG[2 * i + c, 0:LP].astype(F32) + CRM[i].astype(F32)).astype(BF)
+
+    add_over_v(1)
+    add_over_v(2)
+    sum_over_v(0)
+    add_over_v(3)
     sum_over_v(1)
-    last_hop(0)
-    sum_over_v(2)
-    last_hop(1)
-    sum_over_v(3)
-    last_hop(2)
     for kz in (1, 3, 2):
         r_z[kz].wait_recv()
+    for kz in (2, 1, 3):
+        o_z[kz] = send(CSM.at[next_to(4, z, kz)], ZRM.at[kz - 1], along_z(kz))
     total = CSD[z].astype(F32)
     for k in range(3):
         total = total + ZRD[k].astype(F32)
     d_n2 = total[0:LP]
     d_router = jnp.concatenate([total[LP:, 0:256], total[LP:, 256:512], jnp.zeros((96, 256), F32)], 0)
     d_router = jnp.transpose(d_router)[0:LP]
-    n2_own = N2G[t, 0:LP, :]
+    n2_own = n2s[...]
     router = router_of(n2_own)
     d_logits = router * (d_router - jnp.sum(d_router * router, -1, keepdims=True))
     dl_high, dl_low = split_two(d_logits)
@@ -515,6 +568,13 @@
     resid_low = d_resid.astype(BF)
     router_part = dot_tn(n2_own, dl_high) + dot_tn(n2_own, dl_low)
     gain_two_part = jnp.sum(d_n2 * unit_two, 0, keepdims=True)
+    gains = jnp.transpose(jnp.concatenate([gain_two_part, jnp.zeros((127, D), F32)], 0))
+    lane_m = lax.broadcasted_iota(jnp.int32, (D, 128), 1)
+    merged = jnp.where(lane_m == 33, gains[:, 0:1], router_part)
+    for i, (vi, ui) in enumerate(natural):
+        MG[vi, ui] = merged[i * 32 : (i + 1) * 32]
+    p_u = [send(MG.at[:, next_to(4, u, k)], MXR.at[k - 1], along_u(k)) for k in (1, 2, 3)]
+    last_hop(0)
 
     n1_cols = jnp.transpose(n1s[...])
     resid_cols = jnp.transpose(resid_low)
@@ -543,10 +603,12 @@
                     b = (yi * 4 + xi) * 32
                     dW[1, hz, xi, yi] = grad[b : b + 32]
             a_c.append(send(dW.at[oc, hz], DWC.at[hz], core))
+    sum_over_v(2)
     d_n1 = jnp.zeros((LP, D), F32)
     for h in range(8):
         d_n1 = d_n1 + dot_nt(DQ[h, :, 0:192], weights_of(h)[:, 0:192])
-    last_hop(3)
+    last_hop(1)
+    sum_over_v(3)
 
     a_u = []
     for i in range(4):
@@ -557,23 +619,34 @@
         ]
     unit, inv = normalize(xs[...])
     gain_one_part = jnp.sum(d_n1 * unit, 0, keepdims=True)
-    gains = jnp.concatenate([gain_one_part, gain_two_part, jnp.zeros((126, D), F32)], 0)
-    gains = jnp.transpose(gains)
-    lane_m = lax.broadcasted_iota(jnp.int32, (D, 128), 1)
-    merged = jnp.where(lane_m == 32, gains[:, 0:1], jnp.where(lane_m == 33, gains[:, 1:2], router_part))
-    for i, (vi, ui) in enumerate(natural):
-        MG[vi, ui] = merged[i * 32 : (i + 1) * 32]
-    p_u = [send(MG.at[:, next_to(4, u, k)], MXR.at[k - 1], along_u(k)) for k in (1, 2, 3)]
-    tgs[...] = (d_resid + normalize_back(d_n1 * gain_one, unit, inv))[0:L, :]
-    store_tg = local(tgs, tg)
-
-
+    packed = [gain_one_part[:, 128 * i : 128 * (i + 1)] for i in range(4)]
+    GA[z, v] = jnp.concatenate(packed + [jnp.zeros((4, 128), F32)], 0)
+    q_1 = [send(GA.at[z, v], GA.at[z, v], along_vz(*k)) for k in VZ]
+    last_hop(2)
     arrive(p_u)
     s = MG[:, u]
     for k in range(3):
         s = s + MXR[k]
     MXS[...] = s
     p_v = [send(MXS.at[next_to(4, v, k)], MYR.at[k - 1], along_v(k)) for k in (1, 2, 3)]
+    tgs[...] = (d_resid + normalize_back(d_n1 * gain_one, unit, inv))[0:L, :]
+    store_tg = local(tgs, tg)
+
+
+    last_hop(3)
+    arrive(q_1)
+    s = jnp.zeros((8, 128), F32)
+    for i in range(4):
+        for j in range(4):
+            s = s + GA[i, j]
+    GB[u] = s
+    q_u = [send(GB.at[u], GB.at[u], along_u(k)) for k in (1, 2, 3)]
+    arrive(p_v)
+    s = MXS[v]
+    for k in range(3):
+        s = s + MYR[k]
+    MYS[t] = s
+    p_t = [send(MYS.at[t], MYS.at[t], along_t(k)) for k in range(1, 8)]
     arrive(a_u)
     s = DWS[:, :, u].astype(F32)
     for k in range(3):
@@ -583,12 +656,9 @@
         send(XS.at[next_to(4, z, kz), next_to(4, v, kv)], ZW.at[kz * 4 + kv], along_vz(kv, kz))
         for kv, kz in VZ
     ]
-    arrive(p_v)
-    s = MXS[v]
-    for k in range(3):
-        s = s + MYR[k]
-    MYS[t] = s
-    p_t = [send(MYS.at[t], MYS.at[t], along_t(k)) for k in range(1, 8)]
+    arrive(q_u)
+    GC[c] = GB[0] + GB[1] + GB[2] + GB[3]
+    q_c = send(GC.at[c], GC.at[c], core)
     for kz in (1, 3, 2):
         o_z[kz].wait_recv()
     moe = CSM[z].astype(F32)
@@ -605,7 +675,14 @@
     s = MYS[0]
     for k in range(1, 8):
         s = s + MYS[k]
-    gm[...] = s
+    q_c.wait_recv()
+    both = GC[0] + GC[1]
+    own_row = lax.broadcasted_iota(jnp.int32, (8, 128), 0) == lax.div(d, 4)
+    both = jnp.sum(jnp.where(own_row, both, 0.0), 0, keepdims=True)
+    at_r = lax.broadcasted_iota(jnp.int32, (32, 128), 0)
+    at_l = lax.broadcasted_iota(jnp.int32, (32, 128), 1)
+    both = jnp.sum(jnp.where(at_l == lax.rem(d, 4) * 32 + at_r, both, 0.0), -1, keepdims=True)
+    gm[...] = jnp.where(at_l == 32, both, s)
     arrive(g_t[1:])
     g_t[0].wait()
     store_tg.wait()
@@ -613,8 +690,8 @@
     for cp in sent:
         cp.wait_send()
     for i in range(4):
-        for k in (1, 2, 3):
-            grad_copy(i, k).wait_send()
+        for n in range(4):
+            grad_copy(i, n).wait_send()
 
 
 def finish(gexp, gw, gm, out_in, tg_in, out, tg, g_in, g_out, g_qkv, g_o, g_router, g_one, g_two):
@@ -649,24 +726,23 @@
         buf(N_IMG, LQ, D),
         buf(N_IMG, LQ, D),
         buf(4 * SLOT, ROWS),
-        buf(4, SLOT, 1024),
-        buf(4, SLOT, 1024),
-        buf(4, SLOT, 1024),
-        buf(4, SLOT, 1024),
+        buf(4, SLOT, D),
+        buf(4, SLOT, D),
+        buf(4, SLOT, D),
+        buf(4, SLOT, D),
+        buf(4, SLOT, D),
+        buf(4, SLOT, D),
         buf(4 * SLOT, D),
         buf(4 * SLOT, D, dtype=F32),
         buf(4 * SLOT, D, dtype=F32),
-        buf(2, 4 * SLOT, 256),
-        buf(2, 4 * SLOT, 256),
-        buf(2, 4 * SLOT, 256, dtype=F32),
+        buf(4, 2, 4 * SLOT, 256),
+        buf(4, 2, 4 * SLOT, 256),
+        buf(4, 2, 4 * SLOT, 256, dtype=F32),
         buf(2, 4 * SLOT, 256, dtype=F32),
         buf(D, 4 * SLOT),
         buf(D, 4 * SLOT),
-        buf(3, 4, 2, 4, 32, 512),
-        buf(4, 2, 4, 32, 512),
-        buf(4, 2, 4, 32, 512),
-        buf(N_IMG, LP + 16, D),
-        buf(N_IMG, LP, D),
+        buf(2, 4, 4, 32, 512),
+        buf(2, 4, 2, 4, 32, 512),
         buf(4, LP + 16, D),
         buf(4, LP, D),
         buf(4, LP + 16, D),
@@ -679,6 +755,7 @@
         buf(L, D, dtype=F32),
         buf(LP, D, dtype=F32),
         buf(LP, D, dtype=F32),
+        buf(LP, D),
         buf(LP, D),
         buf(8, LP, 256),
         buf(8, LP, LP, dtype=F32),
@@ -703,6 +780,9 @@
         buf(4, 32, 128, dtype=F32),
         buf(3, 32, 128, dtype=F32),
         buf(8, 32, 128, dtype=F32),
+        buf(4, 4, 8, 128, dtype=F32),
+        buf(4, 8, 128, dtype=F32),
+        buf(2, 8, 128, dtype=F32),
         pltpu.SemaphoreType.DMA((N_SEM,)),
         pltpu.SemaphoreType.DMA((N_SEM,)),
         pltpu.SemaphoreType.DMA((12,)),

time: 134 us -> 124 us (0.925); the launches traced: 134 us -> 122 us
  Pallas kernels: 133 us -> 121 us
    pallas_call x1, Pallas kernels: 130 us -> 117 us  [body(): pl.pallas_call(kernel, name='block', out_shape=[jax.ShapeDtypeStruct((L,...]
where the time goes in v4:
time: 124 us; the launch traced here: 122 us
  Pallas kernels  121 us (98%)
  between operations  1.3 us (1%)
    pallas_call x1, Pallas kernels, body(): pl.pallas_call(kernel, name='block', out_shape=[jax.ShapeDtypeStruct((L,...  117 us
    pallas_call x1, Pallas kernels, body(): pl.pallas_call(finish, name='finish', out_shape=[jax.ShapeDtypeStruct((L,...  3.05 us

profile of v4, /device:TPU:1, one launch (start us, length us, event | category | flops | bytes accessed | tf_op | source)
XLA Modules:
  0.0 121.8 jit_solution(633902680739397801)
XLA Ops:
  1.3 117.5 %block.1 = (bf16[197,512]{1,0:T(8,128)(2,1)}, f32[197,512]{1,0:T(8,128)}, f32[32,256]{1,0:T(8,128)}, f32[32,128]{1,0:T(8,128)}, bf16[8,4,32,512]{3,2,1,0:T(8,128)(2,1)}) custom-call(s32[1]{0:T(128)S(6)} %copy.20.cnt, bf16[197,512]{1,0:T(8,128)(2,1)} %tok.1, bf16[197,512]{1,0:T(8,128)(2,1)} %cot.1, s32[2,1576]{1,0:T(2,128)} %bitcast.12, ...), custom_call_target="tpu_custom_call" | custom-call | tf_op jit(solution)/shard_map/block/pallas_call | solution.py:790
  118.8 3.0 %finish.1 = (bf16[197,512]{1,0:T(8,128)(2,1)}, f32[197,512]{1,0:T(8,128)}, f32[32,32,256]{2,1,0:T(8,128)}, f32[32,32,256]{2,1,0:T(8,128)}, f32[32,192]{1,0:T(8,1...) custom-call(bf16[32,32,512]{2,1,0:T(8,128)(2,1)} %bitcast.10, ...), custom_call_target="tpu_custom_call" | custom-call | tf_op jit(solution)/shard_map/finish/pallas_call | solution.py:810

commit v5 on v4

--- a/solution.py
+++ b/solution.py
@@ -18,7 +18,7 @@
 MESH = pl.DeviceIdType.MESH
 BF = jnp.bfloat16
 F32 = jnp.float32
-N_SEM = 240
+N_SEM = 72
 
 
 def dot(a, b):
@@ -54,9 +54,9 @@
 def kernel(
     cnt, tok, cot, picks, qkv_in, out_in, router_in, gain_one_in, gain_two_in, ein, eout,
     out, tg, gw, gm, gexp,
-    W, M, T1, EW, CG, N2G, PM, SBX, SBG, RBX, RBG, RBR, RBD, DS, racc, dxacc, ACT, DIN, INN, DAC, XT, GT,
+    W, M, T1, EW, CG, N2G, PM, SBX, SBG, RBX, RBG, RBR, RBD, DS, racc, dxacc, ACT, DIN, INN, XT, GT,
     YA, YB, CRD, CRM, CSD, CSM, ZRD, ZRM,
-    toks, cots, outs, tgs, xs, cpad, n1s, n2s, QKV, PF, MX, DM, DSC, DQ, resid, xh2s, r2s, chs, pos, gates,
+    qkvs, outws, routers, gain_ones, gain_twos, pickss, toks, cots, outs, tgs, xs, cpad, n1s, n2s, n1t, rts, QKV, PF, MX, DM, DSC, DQ, resid, xh2s, r2s, chs, pos, gates,
     dW, DWC, DWS, XW, XS, ZW, MG, MXR, MXS, MYR, MYS, GA, GB, GC,
     send_sem, recv_sem, loc_sem,
 ):
@@ -113,6 +113,25 @@
         sent.append(cp)
         return cp
 
+    def wait_all(sem, i, like):
+        pltpu.make_async_copy(like, like, sem.at[i]).wait()
+
+    class Batch:
+        def __init__(self, like, copies=()):
+            self.like, self.i = like, take(1)
+            sent.append(self)
+            for src, dst, to in copies:
+                self.add(src, dst, to)
+
+        def add(self, src, dst, to):
+            remote(src, dst, to, self.i).start()
+
+        def wait_recv(self):
+            wait_all(recv_sem, self.i, self.like)
+
+        def wait_send(self):
+            wait_all(send_sem, self.i, self.like)
+
     def left(copies):
         for cp in copies:
             cp.wait_send()
@@ -125,12 +144,14 @@
         cp.start()
         return cp
 
-    def arrive(copies):
-        for cp in copies:
-            cp.wait_recv()
-
     VZ = [(kv, kz) for kz in range(4) for kv in range(4) if (kv, kz) != (0, 0)]
     ZORDER = (0, 1, 3, 2)
+
+    loads = [
+        local(qkv_in, qkvs), local(out_in, outws), local(router_in, routers),
+        local(gain_one_in, gain_ones), local(gain_two_in, gain_twos),
+    ]
+    load_tok, load_cot, load_picks = local(tok, toks), local(cot, cots), local(picks, pickss)
 
     bar = pltpu.get_barrier_semaphore()
     peers = [along_u(k) for k in (1, 2, 3)] + [along_vz(*k) for k in VZ]
@@ -138,58 +159,58 @@
     for p in peers:
         pl.semaphore_signal(bar, inc=1, device_id=p, device_id_type=MESH)
 
-    load_tok, load_cot = local(tok, toks), local(cot, cots)
     eye_r = lax.broadcasted_iota(jnp.int32, (32, 32), 0)
     eye_c = lax.broadcasted_iota(jnp.int32, (32, 32), 1)
 
     def column(row):
         return jnp.sum(jnp.where(eye_r == eye_c, row.astype(F32), 0.0), -1, keepdims=True)
 
-    W[c, z, v, u, :, 0:192] = qkv_in[...]
-    W[c, z, v, u, :, 192:256] = out_in[...]
+    for cp in loads:
+        cp.wait()
+    W[c, z, v, u, :, 0:192] = qkvs[...]
+    W[c, z, v, u, :, 192:256] = outws[...]
     M[v, u] = jnp.zeros((32, 128), BF)
-    M[v, u, :, 0:32] = router_in[...]
-    M[v, u, :, 32:33] = column(gain_one_in[...]).astype(BF)
-    M[v, u, :, 33:34] = column(gain_two_in[...]).astype(BF)
+    M[v, u, :, 0:32] = routers[...]
+    M[v, u, :, 32:33] = column(gain_ones[...]).astype(BF)
+    M[v, u, :, 33:34] = column(gain_twos[...]).astype(BF)
     pl.semaphore_wait(bar, len(peers))
 
-    w_1 = [send(W.at[c, z, v, u], W.at[c, z, v, u], along_vz(*k)) for k in VZ]
-    m_1 = [send(M.at[v, u], M.at[v, u], along_v(k)) for k in (1, 2, 3)]
-
-    e_1 = {}
-
-    def first_hop(kz, kc):
-        to_z = next_to(4, z, kz)
-        to_c = c + kc * (oc - c)
-        to_t = 2 * to_z + to_c
-        src = [ein.at[pl.ds(4 * to_t, 4)], eout.at[pl.ds(4 * to_t, 4)]]
-        dst = [T1.at[z, c, :, :, pl.ds(0, 256)], T1.at[z, c, :, :, pl.ds(256, 256)]]
-        if kz == 0 and kc == 0:
-            return [local(s, q) for s, q in zip(src, dst)]
-        return [send(s, q, {"tensor": to_t}) for s, q in zip(src, dst)]
-
+    fifteen = ZW.at[pl.ds(0, 15)]
+    w_1 = Batch(fifteen, [(W.at[c, z, v, u], W.at[c, z, v, u], along_vz(*k)) for k in VZ])
+    m_1 = Batch(M.at[pl.ds(0, 3), 0], [(M.at[v, u], M.at[v, u], along_v(k)) for k in (1, 2, 3)])
+
+    e_1, e_1_own = {}, []
     for kz in ZORDER:
+        e_1[kz] = Batch(T1.at[0] if kz else T1.at[0, 0])
         for kc in (0, 1):
-            e_1[kz, kc] = first_hop(kz, kc)
+            to_z = next_to(4, z, kz)
+            to_c = c + kc * (oc - c)
+            to_t = 2 * to_z + to_c
+            for source, lanes in ((ein, pl.ds(0, 256)), (eout, pl.ds(256, 256))):
+                src, dst = source.at[pl.ds(4 * to_t, 4)], T1.at[z, c, :, :, lanes]
+                if kz == 0 and kc == 0:
+                    e_1_own.append(local(src, dst))
+                else:
+                    e_1[kz].add(src, dst, {"tensor": to_t})
 
     def first_arrived(kz):
-        for kc in (0, 1):
-            for cp in e_1[kz, kc]:
-                if kz == 0 and kc == 0:
-                    cp.wait()
-                else:
-                    cp.wait_recv()
+        e_1[kz].wait_recv()
+        if kz == 0:
+            for cp in e_1_own:
+                cp.wait()
 
     e_2 = {}
 
     def second_hop(kz):
         zi = next_to(4, z, 4 - kz)
-        e_2[kz] = [
-            send(T1.at[zi, :, next_to(4, u, k)], EW.at[zi, :, v, u], along_u(k)) for k in (1, 2, 3)
+        moved = [
+            (T1.at[zi, :, next_to(4, u, k)], EW.at[zi, :, v, u], along_u(k)) for k in (1, 2, 3)
         ]
+        e_2[kz] = [Batch(EW.at[pl.ds(0, 3), :, 0, 0], moved)]
         e_2[kz].append(local(T1.at[zi, :, u], EW.at[zi, :, v, u]))
 
-    e_3_base = take(16)
+    e_3_base = take(6)
+    e_3_last = []
 
     def third_hop_copy(i, n, zi):
         step = (1, 3)[n % 2]
@@ -197,23 +218,33 @@
             part = EW.at[zi, :, v]
         else:
             part = EW.at[zi, n - 2, next_to(4, v, 4 - step)]
-        return remote(part, part, along_v(step), e_3_base + 4 * i + n)
+        return remote(part, part, along_v(step), e_3_base + 2 * i + n // 2)
+
+    like_3 = (EW.at[0, :, pl.ds(0, 2)], EW.at[0, :, 0])
 
     def third_hop(kz):
-        arrive(e_2[kz][:3])
-        e_2[kz][3].wait()
+        e_2[kz][0].wait_recv()
+        e_2[kz][1].wait()
         zi = next_to(4, z, 4 - kz)
-        for n in (0, 1):
-            third_hop_copy(ZORDER.index(kz), n, zi).start()
+        if kz == 2:
+            part = EW.at[zi, :, v]
+            e_3_last.append(
+                Batch(EW.at[pl.ds(0, 3), :, 0], [(part, part, along_v(k)) for k in (2, 1, 3)])
+            )
+        else:
+            for n in (0, 1):
+                third_hop_copy(ZORDER.index(kz), n, zi).start()
 
     def third_hop_on(kz):
         zi = next_to(4, z, 4 - kz)
-        for n in (0, 1):
-            third_hop_copy(ZORDER.index(kz), n, zi).wait_recv()
-            third_hop_copy(ZORDER.index(kz), n + 2, zi).start()
+        i = ZORDER.index(kz)
+        wait_all(recv_sem, e_3_base + 2 * i, like_3[0])
+        for n in (2, 3):
+            third_hop_copy(i, n, zi).start()
 
     load_tok.wait()
     load_cot.wait()
+    load_picks.wait()
     xs[...] = jnp.zeros((LP, D), F32)
     xs[0:L, :] = toks[...].astype(F32)
     cpad[...] = jnp.zeros((LP, D), F32)
@@ -225,7 +256,7 @@
 
     chs[...] = jnp.full((8, ROWS), -1, jnp.int32)
     for i in range(N_IMG):
-        held = picks[:, i * L : (i + 1) * L]
+        held = pickss[:, i * L : (i + 1) * L]
         live = jnp.full((2, L), cnt[0], jnp.int32) > i
         chs[0:2, i * LQ : i * LQ + L] = jnp.where(live, held, -1)
     sub8 = lax.broadcasted_iota(jnp.int32, (8, ROWS), 0)
@@ -247,14 +278,15 @@
     place = jnp.minimum(first, second)
     pos[0:4, :] = jnp.where(place < CAP, place, 999.0)
 
-    arrive(w_1)
+    w_1.wait_recv()
     w_u, w_c = [], []
     for i in range(4):
-        w_u.append([send(W.at[c, i, :, u], W.at[c, i, :, u], along_u(k)) for k in (1, 2, 3)])
-    arrive(m_1)
-    m_u = [send(M.at[:, u], M.at[:, u], along_u(k)) for k in (1, 2, 3)]
+        part = W.at[c, i, :, u]
+        w_u.append(Batch(W.at[0, pl.ds(0, 3), :, 0], [(part, part, along_u(k)) for k in (1, 2, 3)]))
+    m_1.wait_recv()
+    m_u = Batch(M.at[pl.ds(0, 3)], [(M.at[:, u], M.at[:, u], along_u(k)) for k in (1, 2, 3)])
     for i in range(4):
-        w_c.append([send(W.at[c, i, :, u], W.at[c, i, :, u], core)])
+        w_c.append(Batch(W.at[0, 0], [(W.at[c, i, :, u], W.at[c, i, :, u], core)]))
     first_arrived(0)
     second_hop(0)
     slot_ids = lax.broadcasted_iota(jnp.int32, (SLOT, ROWS), 0).astype(F32)
@@ -266,9 +298,10 @@
     first_arrived(3)
     second_hop(3)
     c_z = [send(CG.at[t, pl.ds(0, LP)], CG.at[t, pl.ds(0, LP)], along_z(k)) for k in (2, 1, 3)]
-    c_c = [send(CG.at[t, pl.ds(0, LP)], CG.at[t, pl.ds(0, LP)], core)]
-
-    arrive(m_u)
+    four = (pl.ds(0, 4), pl.ds(0, LP))
+    c_c = Batch(CG.at[four], [(CG.at[t, pl.ds(0, LP)], CG.at[t, pl.ds(0, LP)], core)])
+
+    m_u.wait_recv()
     natural = [place_uv(yi, xi) for yi in range(4) for xi in range(4)]
     small = jnp.concatenate([M[vi, ui] for vi, ui in natural], 0)
     small_rows = jnp.transpose(small.astype(F32))
@@ -284,13 +317,13 @@
         return jnp.concatenate([W[1, h // 2, xi, yi] for yi in range(4) for xi in range(4)], 0)
 
     def pass_on(i):
+        w_u[i].wait_recv()
         for k in (1, 2, 3):
-            w_u[i][k - 1].wait_recv()
             ui = next_to(4, u, 4 - k)
-            w_c[i].append(send(W.at[c, i, :, ui], W.at[c, i, :, ui], core))
+            w_c[i].add(W.at[c, i, :, ui], W.at[c, i, :, ui], core)
 
     def project(i):
-        arrive(w_c[i])
+        w_c[i].wait_recv()
         for h in (2 * i, 2 * i + 1):
             QKV[h] = dot(n1s[...], weights_of(h)).astype(BF)
 
@@ -328,14 +361,14 @@
     n2s[...] = jnp.where(real, unit_two * gain_two, 0.0).astype(BF)
     N2G[t, 0:LP, :] = n2s[...]
     n_z = [send(N2G.at[t, pl.ds(0, LP)], N2G.at[t, pl.ds(0, LP)], along_z(k)) for k in (2, 1, 3)]
-    n_c = [send(N2G.at[t, pl.ds(0, LP)], N2G.at[t, pl.ds(0, LP)], core)]
+    n_c = Batch(N2G.at[four], [(N2G.at[t, pl.ds(0, LP)], N2G.at[t, pl.ds(0, LP)], core)])
     third_hop(2)
     third_hop_on(0)
     for k, cp in sorted(zip((2, 1, 3), c_z), key=lambda kc: kc[0] % 2 == 0):
         cp.wait_recv()
         im = next_to(4, z, 4 - k) * 2 + c
-        c_c.append(send(CG.at[im, pl.ds(0, LP)], CG.at[im, pl.ds(0, LP)], core))
-    arrive(c_c)
+        c_c.add(CG.at[im, pl.ds(0, LP)], CG.at[im, pl.ds(0, LP)], core)
+    c_c.wait_recv()
     third_hop_on(1)
     cot_slots = dot(PM[...], CG[...].reshape(ROWS, D))
     DS[...] = cot_slots.astype(BF)
@@ -343,14 +376,20 @@
     for k, cp in sorted(zip((2, 1, 3), n_z), key=lambda kc: kc[0] % 2 == 0):
         cp.wait_recv()
         im = next_to(4, z, 4 - k) * 2 + c
-        n_c.append(send(N2G.at[im, pl.ds(0, LP)], N2G.at[im, pl.ds(0, LP)], core))
-    arrive(n_c)
+        n_c.add(N2G.at[im, pl.ds(0, LP)], N2G.at[im, pl.ds(0, LP)], core)
+    n_c.wait_recv()
+
+    def shuffle(source, target):
+        return Batch(
+            target.at[pl.ds(0, 3)],
+            [(source.at[next_to(4, u, k)], target.at[u], along_u(k)) for k in (2, 1, 3)],
+        )
 
     rows_x = dot(PM[...], N2G[...].reshape(ROWS, D)).astype(BF)
     SBX[...] = rows_x.reshape(4, SLOT, D)
     for kz in range(4):
-        left(e_2[kz][:3])
-    s_x = [send(SBX.at[next_to(4, u, k)], RBX.at[u], along_u(k)) for k in (2, 1, 3)]
+        left(e_2[kz][:1])
+    s_x = shuffle(SBX, RBX)
     RBX[u] = SBX[u]
     lane_e = lax.broadcasted_iota(jnp.int32, (4 * SLOT, 128), 1)
     row_e = 4 * t + lax.div(lax.broadcasted_iota(jnp.int32, (4 * SLOT, 128), 0), SLOT)
@@ -366,10 +405,9 @@
     gate = jnp.sum(jnp.where(lane_e == row_e, slot_router, 0.0), -1, keepdims=True)
     gates[...] = jnp.broadcast_to(gate, (4 * SLOT, 128))
     SBG[...] = (DS[...].astype(F32) * gate).astype(BF).reshape(4, SLOT, D)
-    s_g = [send(SBG.at[next_to(4, u, k)], RBG.at[u], along_u(k)) for k in (2, 1, 3)]
+    s_g = shuffle(SBG, RBG)
     RBG[u] = SBG[u]
-    third_hop_on(2)
-    arrive(s_x)
+    s_x.wait_recv()
 
     racc[...] = jnp.zeros((4 * SLOT, D), F32)
     dxacc[...] = jnp.zeros((4 * SLOT, D), F32)
@@ -383,9 +421,13 @@
 
     def forward_units(i, carry):
         zi = z_of(i)
-        for n in (0, 1):
-            third_hop_copy(i, n, zi).wait_send()
-            third_hop_copy(i, n + 2, zi).wait()
+        if isinstance(i, int):
+            e_3_last[0].wait_recv()
+            left(e_3_last)
+        else:
+            wait_all(send_sem, e_3_base + 2 * i, like_3[0])
+            wait_all(send_sem, e_3_base + 2 * i + 1, like_3[1])
+            wait_all(recv_sem, e_3_base + 2 * i + 1, like_3[1])
         rows_e = RBX[...].reshape(4 * SLOT, D)
         for ci in range(2):
             INN[i, ci] = dot(rows_e, tile_of(zi, ci, slice(0, 256)))
@@ -408,40 +450,40 @@
         zi = z_of(i)
         grad_e = RBG[...].reshape(4 * SLOT, D)
         for ci in range(2):
-            DAC[ci] = dot(grad_e, tile_of(zi, ci, slice(256, 512)))
-        for ci in range(2):
-            DIN[i, ci] = (DAC[ci] * INN[i, ci]).astype(BF)
+            d_act = dot(grad_e, tile_of(zi, ci, slice(256, 512)))
+            DIN[i, ci] = (d_act * INN[i, ci]).astype(BF)
         acc = dxacc[...]
         for ci in range(2):
             acc = acc + dot_nt(DIN[i, ci], tile_of(zi, ci, slice(0, 256)))
         dxacc[...] = acc
         return carry
 
-    lax.fori_loop(0, 4, forward_units, 0)
-    left(s_x)
+    lax.fori_loop(0, 3, forward_units, 0)
+    forward_units(3, 0)
+    left([s_x])
     SBX[...] = racc[...].astype(BF).reshape(4, SLOT, D)
-    b_r = [send(SBX.at[next_to(4, u, k)], RBR.at[u], along_u(k)) for k in (2, 1, 3)]
+    b_r = shuffle(SBX, RBR)
     RBR[u] = SBX[u]
-    arrive(s_g)
+    s_g.wait_recv()
     lax.fori_loop(0, 4, backward_units, 0)
-    left(s_g)
+    left([s_g])
     SBG[...] = dxacc[...].astype(BF).reshape(4, SLOT, D)
-    b_d = [send(SBG.at[next_to(4, u, k)], RBD.at[u], along_u(k)) for k in (2, 1, 3)]
+    b_d = shuffle(SBG, RBD)
     RBD[u] = SBG[u]
 
     XT[...] = jnp.transpose(RBX[...].reshape(4 * SLOT, D))
     GT[...] = jnp.transpose(RBG[...].reshape(4 * SLOT, D))
-    g_v_base = take(16)
+    g_v_base = take(8)
 
     def grad_copy(i, n):
         zi = z_of(i)
         step = (1, 3)[n % 2]
         if n < 2:
             return remote(
-                EW.at[zi, n, next_to(4, v, 2)], YA.at[n, zi], along_v(step), g_v_base + 4 * i + n
+                EW.at[zi, n, next_to(4, v, 2)], YA.at[n, zi], along_v(step), g_v_base + 2 * i
             )
         return remote(
-            EW.at[zi, :, next_to(4, v, step)], YB.at[n - 2, zi], along_v(step), g_v_base + 4 * i + n
+            EW.at[zi, :, next_to(4, v, step)], YB.at[n - 2, zi], along_v(step), g_v_base + 2 * i + 1
         )
 
     def expert_grads(i, carry):
@@ -461,42 +503,42 @@
         for n in (0, 1):
             grad_copy(i, n).start()
 
-    g_u, g_t = {}, []
+    g_u, g_t, g_t_own = {}, Batch(gexp.at[pl.ds(0, 7)]), []
     XR = T1
 
     def add_over_v(i):
         zi = z_of(i)
+        wait_all(recv_sem, g_v_base + 2 * i, YA.at[:, 0])
         for n in (0, 1):
-            grad_copy(i, n).wait_recv()
             part = next_to(4, v, (1, 3)[n])
             EW[zi, n, part] = (EW[zi, n, part].astype(F32) + YA[n, zi].astype(F32)).astype(BF)
             grad_copy(i, n + 2).start()
 
     def sum_over_v(i):
         zi = z_of(i)
-        for n in (2, 3):
-            grad_copy(i, n).wait_recv()
+        wait_all(recv_sem, g_v_base + 2 * i + 1, YB.at[:, 0])
         for ci in range(2):
             s = EW[zi, ci, v].astype(F32) + YB[0, zi, ci].astype(F32) + YB[1, zi, ci].astype(F32)
             EW[zi, ci, v] = s.astype(BF)
             XR[zi, ci, u] = EW[zi, ci, v, u]
-        g_u[i] = [
-            send(EW.at[zi, :, v, next_to(4, u, k)], XR.at[zi, :, u], along_u(k)) for k in (1, 2, 3)
+        moved = [
+            (EW.at[zi, :, v, next_to(4, u, k)], XR.at[zi, :, u], along_u(k)) for k in (1, 2, 3)
         ]
+        g_u[i] = Batch(XR.at[pl.ds(0, 3), :, 0], moved)
 
     def last_hop(i):
         zi = z_of(i)
-        arrive(g_u[i])
+        g_u[i].wait_recv()
         for kc in (0, 1):
             ci = c + kc * (oc - c)
             if i == 0 and kc == 0:
-                g_t.append(local(XR.at[zi, ci], gexp.at[t]))
+                g_t_own.append(local(XR.at[zi, ci], gexp.at[t]))
             else:
-                g_t.append(send(XR.at[zi, ci], gexp.at[t], {"tensor": 2 * zi + ci}))
-
-    left(c_z + c_c + n_z + n_c)
-    r_c, r_z, o_c, o_z = {}, {}, {}, {}
-    arrive(b_r)
+                g_t.add(XR.at[zi, ci], gexp.at[t], {"tensor": 2 * zi + ci})
+
+    left(c_z + [c_c] + n_z + [n_c])
+    r_c, r_z, o_c = {}, Batch(ZRD), Batch(CRM)
+    b_r.wait_recv()
     res = RBR[...].reshape(4 * SLOT, D)
 
     def columns_of(i):
@@ -509,12 +551,12 @@
     for kz in (2, 1, 3, 0):
         i = next_to(4, z, kz)
         moe_rows(2 * i + oc)
-        o_c[kz] = send(CG.at[2 * i + oc, pl.ds(0, LP)], CRM.at[i], core)
+        o_c.add(CG.at[2 * i + oc, pl.ds(0, LP)], CRM.at[i], core)
     for kz in (2, 1, 3, 0):
         moe_rows(2 * next_to(4, z, kz) + c)
     d_gate = jnp.sum(res.astype(F32) * DS[...].astype(F32), -1, keepdims=True)
     d_gate = jnp.where(lane_e == row_e, d_gate, 0.0).astype(BF)
-    arrive(b_d)
+    b_d.wait_recv()
 
     back = RBD[...].reshape(4 * SLOT, D)
 
@@ -535,11 +577,13 @@
         r_c[kz].wait_recv()
         CSD[i] = (N2G[2 * i + c, 0 : LP + 16].astype(F32) + CRD[i].astype(F32)).astype(BF)
         if kz:
-            r_z[kz] = send(CSD.at[i], ZRD.at[kz - 1], along_z(kz))
+            r_z.add(CSD.at[i], ZRD.at[kz - 1], along_z(kz))
+    n2_own = n2s[...]
+    rts[...] = router_of(n2_own)
+    n1t[...] = jnp.transpose(n1s[...])
     add_over_v(0)
-    for kz in (2, 1, 3, 0):
-        i = next_to(4, z, kz)
-        o_c[kz].wait_recv()
+    o_c.wait_recv()
+    for i in range(4):
         CSM[i] = (CG[2 * i + c, 0:LP].astype(F32) + CRM[i].astype(F32)).astype(BF)
 
     add_over_v(1)
@@ -547,18 +591,17 @@
     sum_over_v(0)
     add_over_v(3)
     sum_over_v(1)
-    for kz in (1, 3, 2):
-        r_z[kz].wait_recv()
-    for kz in (2, 1, 3):
-        o_z[kz] = send(CSM.at[next_to(4, z, kz)], ZRM.at[kz - 1], along_z(kz))
+    r_z.wait_recv()
+    o_z = Batch(
+        ZRM, [(CSM.at[next_to(4, z, k)], ZRM.at[k - 1], along_z(k)) for k in (2, 1, 3)]
+    )
     total = CSD[z].astype(F32)
     for k in range(3):
         total = total + ZRD[k].astype(F32)
     d_n2 = total[0:LP]
     d_router = jnp.concatenate([total[LP:, 0:256], total[LP:, 256:512], jnp.zeros((96, 256), F32)], 0)
     d_router = jnp.transpose(d_router)[0:LP]
-    n2_own = n2s[...]
-    router = router_of(n2_own)
+    router = rts[...]
     d_logits = router * (d_router - jnp.sum(d_router * router, -1, keepdims=True))
     dl_high, dl_low = split_two(d_logits)
     d_n2 = d_n2 + dot_nt(dl_high, small) + dot_nt(dl_low, small)
@@ -573,10 +616,12 @@
     merged = jnp.where(lane_m == 33, gains[:, 0:1], router_part)
     for i, (vi, ui) in enumerate(natural):
         MG[vi, ui] = merged[i * 32 : (i + 1) * 32]
-    p_u = [send(MG.at[:, next_to(4, u, k)], MXR.at[k - 1], along_u(k)) for k in (1, 2, 3)]
+    p_u = Batch(
+        MXR, [(MG.at[:, next_to(4, u, k)], MXR.at[k - 1], along_u(k)) for k in (1, 2, 3)]
+    )
     last_hop(0)
 
-    n1_cols = jnp.transpose(n1s[...])
+    n1_cols = n1t[...]
     resid_cols = jnp.transpose(resid_low)
     for h in range(8):
         DM[h] = dot(resid_low, weights_of(h)[:, 192:256]).astype(BF)
@@ -610,68 +655,67 @@
     last_hop(1)
     sum_over_v(3)
 
-    a_u = []
+    a_u = Batch(XW)
     for i in range(4):
         a_c[i].wait_recv()
         DWS[i] = (dW[c, i].astype(F32) + DWC[i].astype(F32)).astype(BF)
-        a_u += [
-            send(DWS.at[i, :, next_to(4, u, k)], XW.at[k - 1, i], along_u(k)) for k in (1, 2, 3)
-        ]
+        for k in (1, 2, 3):
+            a_u.add(DWS.at[i, :, next_to(4, u, k)], XW.at[k - 1, i], along_u(k))
     unit, inv = normalize(xs[...])
     gain_one_part = jnp.sum(d_n1 * unit, 0, keepdims=True)
     packed = [gain_one_part[:, 128 * i : 128 * (i + 1)] for i in range(4)]
-    GA[z, v] = jnp.concatenate(packed + [jnp.zeros((4, 128), F32)], 0)
-    q_1 = [send(GA.at[z, v], GA.at[z, v], along_vz(*k)) for k in VZ]
+    GA[4 * z + v] = jnp.concatenate(packed + [jnp.zeros((4, 128), F32)], 0)
+    own = GA.at[4 * z + v]
+    q_1 = Batch(GA.at[pl.ds(0, 15)], [(own, own, along_vz(*k)) for k in VZ])
     last_hop(2)
-    arrive(p_u)
+    p_u.wait_recv()
     s = MG[:, u]
     for k in range(3):
         s = s + MXR[k]
     MXS[...] = s
-    p_v = [send(MXS.at[next_to(4, v, k)], MYR.at[k - 1], along_v(k)) for k in (1, 2, 3)]
+    p_v = Batch(
+        MYR, [(MXS.at[next_to(4, v, k)], MYR.at[k - 1], along_v(k)) for k in (1, 2, 3)]
+    )
     tgs[...] = (d_resid + normalize_back(d_n1 * gain_one, unit, inv))[0:L, :]
     store_tg = local(tgs, tg)
-
-
     last_hop(3)
-    arrive(q_1)
+    q_1.wait_recv()
     s = jnp.zeros((8, 128), F32)
-    for i in range(4):
-        for j in range(4):
-            s = s + GA[i, j]
+    for i in range(16):
+        s = s + GA[i]
     GB[u] = s
-    q_u = [send(GB.at[u], GB.at[u], along_u(k)) for k in (1, 2, 3)]
-    arrive(p_v)
+    q_u = Batch(GB.at[pl.ds(0, 3)], [(GB.at[u], GB.at[u], along_u(k)) for k in (1, 2, 3)])
+    p_v.wait_recv()
     s = MXS[v]
     for k in range(3):
         s = s + MYR[k]
     MYS[t] = s
-    p_t = [send(MYS.at[t], MYS.at[t], along_t(k)) for k in range(1, 8)]
-    arrive(a_u)
+    p_t = Batch(MYS.at[pl.ds(0, 7)], [(MYS.at[t], MYS.at[t], along_t(k)) for k in range(1, 8)])
+    a_u.wait_recv()
     s = DWS[:, :, u].astype(F32)
     for k in range(3):
         s = s + XW[k].astype(F32)
     XS[...] = s.astype(BF)
-    a_2 = [
-        send(XS.at[next_to(4, z, kz), next_to(4, v, kv)], ZW.at[kz * 4 + kv], along_vz(kv, kz))
+    moved = [
+        (XS.at[next_to(4, z, kz), next_to(4, v, kv)], ZW.at[kz * 4 + kv], along_vz(kv, kz))
         for kv, kz in VZ
     ]
-    arrive(q_u)
+    a_2 = Batch(fifteen, moved)
+    q_u.wait_recv()
     GC[c] = GB[0] + GB[1] + GB[2] + GB[3]
     q_c = send(GC.at[c], GC.at[c], core)
-    for kz in (1, 3, 2):
-        o_z[kz].wait_recv()
+    o_z.wait_recv()
     moe = CSM[z].astype(F32)
     for k in range(3):
         moe = moe + ZRM[k].astype(F32)
     outs[...] = (((resid[...] + moe) * alive)[0:L, :]).astype(BF)
     store_out = local(outs, out)
-    arrive(a_2)
+    a_2.wait_recv()
     s = XS[z, v].astype(F32)
     for kv, kz in VZ:
         s = s + ZW[kz * 4 + kv].astype(F32)
     gw[...] = s
-    arrive(p_t)
+    p_t.wait_recv()
     s = MYS[0]
     for k in range(1, 8):
         s = s + MYS[k]
@@ -683,15 +727,15 @@
     at_l = lax.broadcasted_iota(jnp.int32, (32, 128), 1)
     both = jnp.sum(jnp.where(at_l == lax.rem(d, 4) * 32 + at_r, both, 0.0), -1, keepdims=True)
     gm[...] = jnp.where(at_l == 32, both, s)
-    arrive(g_t[1:])
-    g_t[0].wait()
+    g_t.wait_recv()
+    g_t_own[0].wait()
     store_tg.wait()
     store_out.wait()
     for cp in sent:
         cp.wait_send()
     for i in range(4):
-        for n in range(4):
-            grad_copy(i, n).wait_send()
+        wait_all(send_sem, g_v_base + 2 * i, YA.at[:, 0])
+        wait_all(send_sem, g_v_base + 2 * i + 1, YB.at[:, 0])
 
 
 def finish(gexp, gw, gm, out_in, tg_in, out, tg, g_in, g_out, g_qkv, g_o, g_router, g_one, g_two):
@@ -738,7 +782,6 @@
         buf(4, 2, 4 * SLOT, 256),
         buf(4, 2, 4 * SLOT, 256),
         buf(4, 2, 4 * SLOT, 256, dtype=F32),
-        buf(2, 4 * SLOT, 256, dtype=F32),
         buf(D, 4 * SLOT),
         buf(D, 4 * SLOT),
         buf(2, 4, 4, 32, 512),
@@ -749,6 +792,12 @@
         buf(4, LP, D),
         buf(3, LP + 16, D),
         buf(3, LP, D),
+        buf(32, 192),
+        buf(32, 64),
+        buf(32, 32),
+        buf(1, 32),
+        buf(1, 32),
+        buf(2, N_IMG * L, dtype=jnp.int32),
         buf(L, D),
         buf(L, D),
         buf(L, D),
@@ -757,6 +806,8 @@
         buf(LP, D, dtype=F32),
         buf(LP, D),
         buf(LP, D),
+        buf(D, LP),
+        buf(LP, 128, dtype=F32),
         buf(8, LP, 256),
         buf(8, LP, LP, dtype=F32),
         buf(8, LP, 64),
@@ -780,12 +831,12 @@
         buf(4, 32, 128, dtype=F32),
         buf(3, 32, 128, dtype=F32),
         buf(8, 32, 128, dtype=F32),
-        buf(4, 4, 8, 128, dtype=F32),
+        buf(16, 8, 128, dtype=F32),
         buf(4, 8, 128, dtype=F32),
         buf(2, 8, 128, dtype=F32),
         pltpu.SemaphoreType.DMA((N_SEM,)),
         pltpu.SemaphoreType.DMA((N_SEM,)),
-        pltpu.SemaphoreType.DMA((12,)),
+        pltpu.SemaphoreType.DMA((18,)),
     ]
     out, tg, gw, gm, gexp = pl.pallas_call(
         kernel,
@@ -797,7 +848,7 @@
             jax.ShapeDtypeStruct((32, 128), F32),
             jax.ShapeDtypeStruct((8, 4, 32, 512), BF),
         ],
-        in_specs=[sm, hbm, hbm] + [vm] * 6 + [hbm, hbm],
+        in_specs=[sm] + [hbm] * 10,
         out_specs=[hbm, hbm, vm, vm, hbm],
         scratch_shapes=scratch,
         compiler_params=pltpu.CompilerParams(

time: 124 us -> 118 us (0.952)
  Pallas kernels: 121 us -> 114 us
    pallas_call x1, Pallas kernels: 117 us -> 111 us  [body(): pl.pallas_call(kernel, name='block', out_shape=[jax.ShapeDtypeStruct((L,...]
where the time goes in v5:
time: 118 us; the launch traced here: 115 us
  Pallas kernels  114 us (97%)
  between operations  1.3 us (1%)
    pallas_call x1, Pallas kernels, body(): pl.pallas_call(kernel, name='block', out_shape=[jax.ShapeDtypeStruct((L,...  111 us
    pallas_call x1, Pallas kernels, body(): pl.pallas_call(finish, name='finish', out_shape=[jax.ShapeDtypeStruct((L,...  3.05 us

profile of v5, /device:TPU:1, one launch (start us, length us, event | category | flops | bytes accessed | tf_op | source)
XLA Modules:
  0.0 115.4 jit_solution(17590990794111630001)
XLA Ops:
  1.3 111.0 %block.1 = (bf16[197,512]{1,0:T(8,128)(2,1)}, f32[197,512]{1,0:T(8,128)}, f32[32,256]{1,0:T(8,128)}, f32[32,128]{1,0:T(8,128)}, bf16[8,4,32,512]{3,2,1,0:T(8,128)(2,1)}) custom-call(s32[1]{0:T(128)S(6)} %copy.20.cnt, bf16[197,512]{1,0:T(8,128)(2,1)} %tok.1, bf16[197,512]{1,0:T(8,128)(2,1)} %cot.1, s32[2,1576]{1,0:T(2,128)} %bitcast.12, ...), custom_call_target="tpu_custom_call" | custom-call | tf_op jit(solution)/shard_map/block/pallas_call | solution.py:841
  112.3 3.0 %finish.1 = (bf16[197,512]{1,0:T(8,128)(2,1)}, f32[197,512]{1,0:T(8,128)}, f32[32,32,256]{2,1,0:T(8,128)}, f32[32,32,256]{2,1,0:T(8,128)}, f32[32,192]{1,0:T(8,1...) custom-call(bf16[32,32,512]{2,1,0:T(8,128)(2,1)} %bitcast.10, ...), custom_call_target="tpu_custom_call" | custom-call | tf_op jit(solution)/shard_map/finish/pallas_call | solution.py:861

commit v6 on v5

--- a/solution.py
+++ b/solution.py
@@ -209,38 +209,15 @@
         e_2[kz] = [Batch(EW.at[pl.ds(0, 3), :, 0, 0], moved)]
         e_2[kz].append(local(T1.at[zi, :, u], EW.at[zi, :, v, u]))
 
-    e_3_base = take(6)
-    e_3_last = []
-
-    def third_hop_copy(i, n, zi):
-        step = (1, 3)[n % 2]
-        if n < 2:
-            part = EW.at[zi, :, v]
-        else:
-            part = EW.at[zi, n - 2, next_to(4, v, 4 - step)]
-        return remote(part, part, along_v(step), e_3_base + 2 * i + n // 2)
-
-    like_3 = (EW.at[0, :, pl.ds(0, 2)], EW.at[0, :, 0])
+    e_3_base = take(4)
+    like_3 = EW.at[pl.ds(0, 3), :, 0]
 
     def third_hop(kz):
         e_2[kz][0].wait_recv()
         e_2[kz][1].wait()
-        zi = next_to(4, z, 4 - kz)
-        if kz == 2:
-            part = EW.at[zi, :, v]
-            e_3_last.append(
-                Batch(EW.at[pl.ds(0, 3), :, 0], [(part, part, along_v(k)) for k in (2, 1, 3)])
-            )
-        else:
-            for n in (0, 1):
-                third_hop_copy(ZORDER.index(kz), n, zi).start()
-
-    def third_hop_on(kz):
-        zi = next_to(4, z, 4 - kz)
-        i = ZORDER.index(kz)
-        wait_all(recv_sem, e_3_base + 2 * i, like_3[0])
-        for n in (2, 3):
-            third_hop_copy(i, n, zi).start()
+        part = EW.at[next_to(4, z, 4 - kz), :, v]
+        for k in (2, 1, 3):
+            remote(part, part, along_v(k), e_3_base + ZORDER.index(kz)).start()
 
     load_tok.wait()
     load_cot.wait()
@@ -329,13 +306,13 @@
 
     pass_on(0)
     pass_on(1)
+    first_arrived(2)
+    second_hop(2)
     third_hop(0)
     project(0)
     pass_on(2)
     project(1)
     pass_on(3)
-    first_arrived(2)
-    second_hop(2)
     project(2)
     third_hop(1)
     project(3)
@@ -363,16 +340,13 @@
     n_z = [send(N2G.at[t, pl.ds(0, LP)], N2G.at[t, pl.ds(0, LP)], along_z(k)) for k in (2, 1, 3)]
     n_c = Batch(N2G.at[four], [(N2G.at[t, pl.ds(0, LP)], N2G.at[t, pl.ds(0, LP)], core)])
     third_hop(2)
-    third_hop_on(0)
     for k, cp in sorted(zip((2, 1, 3), c_z), key=lambda kc: kc[0] % 2 == 0):
         cp.wait_recv()
         im = next_to(4, z, 4 - k) * 2 + c
         c_c.add(CG.at[im, pl.ds(0, LP)], CG.at[im, pl.ds(0, LP)], core)
     c_c.wait_recv()
-    third_hop_on(1)
     cot_slots = dot(PM[...], CG[...].reshape(ROWS, D))
     DS[...] = cot_slots.astype(BF)
-    third_hop_on(3)
     for k, cp in sorted(zip((2, 1, 3), n_z), key=lambda kc: kc[0] % 2 == 0):
         cp.wait_recv()
         im = next_to(4, z, 4 - k) * 2 + c
@@ -421,13 +395,8 @@
 
     def forward_units(i, carry):
         zi = z_of(i)
-        if isinstance(i, int):
-            e_3_last[0].wait_recv()
-            left(e_3_last)
-        else:
-            wait_all(send_sem, e_3_base + 2 * i, like_3[0])
-            wait_all(send_sem, e_3_base + 2 * i + 1, like_3[1])
-            wait_all(recv_sem, e_3_base + 2 * i + 1, like_3[1])
+        wait_all(send_sem, e_3_base + i, like_3)
+        wait_all(recv_sem, e_3_base + i, like_3)
         rows_e = RBX[...].reshape(4 * SLOT, D)
         for ci in range(2):
             INN[i, ci] = dot(rows_e, tile_of(zi, ci, slice(0, 256)))
@@ -458,8 +427,7 @@
         dxacc[...] = acc
         return carry
 
-    lax.fori_loop(0, 3, forward_units, 0)
-    forward_units(3, 0)
+    lax.fori_loop(0, 4, forward_units, 0)
     left([s_x])
     SBX[...] = racc[...].astype(BF).reshape(4, SLOT, D)
     b_r = shuffle(SBX, RBR)

time: 118 us -> 117 us (level); the launches traced: 115 us -> 117 us
    pallas_call x1, Pallas kernels: 111 us -> 112 us  [body(): pl.pallas_call(kernel, name='block', out_shape=[jax.ShapeDtypeStruct((L,...]
where the time goes in v6:
time: 117 us
  Pallas kernels  115 us (98%)
  between operations  1.3 us (1%)
    pallas_call x1, Pallas kernels, body(): pl.pallas_call(kernel, name='block', out_shape=[jax.ShapeDtypeStruct((L,...  112 us
    pallas_call x1, Pallas kernels, body(): pl.pallas_call(finish, name='finish', out_shape=[jax.ShapeDtypeStruct((L,...  3.05 us

profile of v6, /device:TPU:1, one launch (start us, length us, event | category | flops | bytes accessed | tf_op | source)
XLA Modules:
  0.0 116.6 jit_solution(18441415928853641853)
XLA Ops:
  1.3 112.3 %block.1 = (bf16[197,512]{1,0:T(8,128)(2,1)}, f32[197,512]{1,0:T(8,128)}, f32[32,256]{1,0:T(8,128)}, f32[32,128]{1,0:T(8,128)}, bf16[8,4,32,512]{3,2,1,0:T(8,128)(2,1)}) custom-call(s32[1]{0:T(128)S(6)} %copy.20.cnt, bf16[197,512]{1,0:T(8,128)(2,1)} %tok.1, bf16[197,512]{1,0:T(8,128)(2,1)} %cot.1, s32[2,1576]{1,0:T(2,128)} %bitcast.12, ...), custom_call_target="tpu_custom_call" | custom-call | tf_op jit(solution)/shard_map/block/pallas_call | solution.py:809
  113.6 3.0 %finish.1 = (bf16[197,512]{1,0:T(8,128)(2,1)}, f32[197,512]{1,0:T(8,128)}, f32[32,32,256]{2,1,0:T(8,128)}, f32[32,32,256]{2,1,0:T(8,128)}, f32[32,192]{1,0:T(8,1...) custom-call(bf16[32,32,512]{2,1,0:T(8,128)(2,1)} %bitcast.10, ...), custom_call_target="tpu_custom_call" | custom-call | tf_op jit(solution)/shard_map/finish/pallas_call | solution.py:829

commit v7 on v6

--- a/solution.py
+++ b/solution.py
@@ -56,7 +56,7 @@
     out, tg, gw, gm, gexp,
     W, M, T1, EW, CG, N2G, PM, SBX, SBG, RBX, RBG, RBR, RBD, DS, racc, dxacc, ACT, DIN, INN, XT, GT,
     YA, YB, CRD, CRM, CSD, CSM, ZRD, ZRM,
-    qkvs, outws, routers, gain_ones, gain_twos, pickss, toks, cots, outs, tgs, xs, cpad, n1s, n2s, n1t, rts, QKV, PF, MX, DM, DSC, DQ, resid, xh2s, r2s, chs, pos, gates,
+    qkvs, outws, routers, gain_ones, gain_twos, pickss, toks, cots, outs, tgs, xs, cpad, n1s, n2s, n1t, rts, QKV, PF, MX, DM, DSC, DQ, resid, xh1s, r1s, xh2s, r2s, chs, pos, gates,
     dW, DWC, DWS, XW, XS, ZW, MG, MXR, MXS, MYR, MYS, GA, GB, GC,
     send_sem, recv_sem, loc_sem,
 ):
@@ -283,7 +283,9 @@
     small = jnp.concatenate([M[vi, ui] for vi, ui in natural], 0)
     small_rows = jnp.transpose(small.astype(F32))
     gain_one, gain_two = small_rows[32:33, :], small_rows[33:34, :]
-    unit, _ = normalize(xs[...])
+    unit, inv = normalize(xs[...])
+    xh1s[...] = unit
+    r1s[...] = jnp.broadcast_to(inv, (LP, 128))
     n1s[...] = (unit * gain_one).astype(BF)
 
     lane = lax.broadcasted_iota(jnp.int32, (LP, LP), 1)
@@ -381,10 +383,10 @@
     SBG[...] = (DS[...].astype(F32) * gate).astype(BF).reshape(4, SLOT, D)
     s_g = shuffle(SBG, RBG)
     RBG[u] = SBG[u]
-    s_x.wait_recv()
-
     racc[...] = jnp.zeros((4 * SLOT, D), F32)
     dxacc[...] = jnp.zeros((4 * SLOT, D), F32)
+    s_x.wait_recv()
+
 
     def z_of(i):
         kz = ZORDER[i] if isinstance(i, int) else jnp.where(i < 2, i, 5 - i)
@@ -620,8 +622,8 @@
     d_n1 = jnp.zeros((LP, D), F32)
     for h in range(8):
         d_n1 = d_n1 + dot_nt(DQ[h, :, 0:192], weights_of(h)[:, 0:192])
+    sum_over_v(3)
     last_hop(1)
-    sum_over_v(3)
 
     a_u = Batch(XW)
     for i in range(4):
@@ -629,7 +631,7 @@
         DWS[i] = (dW[c, i].astype(F32) + DWC[i].astype(F32)).astype(BF)
         for k in (1, 2, 3):
             a_u.add(DWS.at[i, :, next_to(4, u, k)], XW.at[k - 1, i], along_u(k))
-    unit, inv = normalize(xs[...])
+    unit, inv = xh1s[...], r1s[:, 0:1]
     gain_one_part = jnp.sum(d_n1 * unit, 0, keepdims=True)
     packed = [gain_one_part[:, 128 * i : 128 * (i + 1)] for i in range(4)]
     GA[4 * z + v] = jnp.concatenate(packed + [jnp.zeros((4, 128), F32)], 0)
@@ -785,6 +787,8 @@
         buf(LP, D, dtype=F32),
         buf(LP, D, dtype=F32),
         buf(LP, 128, dtype=F32),
+        buf(LP, D, dtype=F32),
+        buf(LP, 128, dtype=F32),
         buf(8, ROWS, dtype=jnp.int32),
         buf(8, ROWS, dtype=F32),
         buf(4 * SLOT, 128, dtype=F32),

time: 117 us -> 117 us (level)
  no operation moved by 1% of the time
where the time goes in v7:
time: 117 us
  Pallas kernels  115 us (98%)
  between operations  1.3 us (1%)
    pallas_call x1, Pallas kernels, body(): pl.pallas_call(kernel, name='block', out_shape=[jax.ShapeDtypeStruct((L,...  112 us
    pallas_call x1, Pallas kernels, body(): pl.pallas_call(finish, name='finish', out_shape=[jax.ShapeDtypeStruct((L,...  3.05 us

profile of v7, /device:TPU:1, one launch (start us, length us, event | category | flops | bytes accessed | tf_op | source)
XLA Modules:
  0.0 116.5 jit_solution(8251160068323517393)
XLA Ops:
  1.3 112.2 %block.1 = (bf16[197,512]{1,0:T(8,128)(2,1)}, f32[197,512]{1,0:T(8,128)}, f32[32,256]{1,0:T(8,128)}, f32[32,128]{1,0:T(8,128)}, bf16[8,4,32,512]{3,2,1,0:T(8,128)(2,1)}) custom-call(s32[1]{0:T(128)S(6)} %copy.20.cnt, bf16[197,512]{1,0:T(8,128)(2,1)} %tok.1, bf16[197,512]{1,0:T(8,128)(2,1)} %cot.1, s32[2,1576]{1,0:T(2,128)} %bitcast.12, ...), custom_call_target="tpu_custom_call" | custom-call | tf_op jit(solution)/shard_map/block/pallas_call | solution.py:813
  113.5 3.0 %finish.1 = (bf16[197,512]{1,0:T(8,128)(2,1)}, f32[197,512]{1,0:T(8,128)}, f32[32,32,256]{2,1,0:T(8,128)}, f32[32,32,256]{2,1,0:T(8,128)}, f32[32,192]{1,0:T(8,1...) custom-call(bf16[32,32,512]{2,1,0:T(8,128)(2,1)} %bitcast.10, ...), custom_call_target="tpu_custom_call" | custom-call | tf_op jit(solution)/shard_map/finish/pallas_call | solution.py:833

commit v8 on v6

--- a/solution.py
+++ b/solution.py
@@ -546,10 +546,10 @@
         CSD[i] = (N2G[2 * i + c, 0 : LP + 16].astype(F32) + CRD[i].astype(F32)).astype(BF)
         if kz:
             r_z.add(CSD.at[i], ZRD.at[kz - 1], along_z(kz))
+    add_over_v(0)
     n2_own = n2s[...]
     rts[...] = router_of(n2_own)
     n1t[...] = jnp.transpose(n1s[...])
-    add_over_v(0)
     o_c.wait_recv()
     for i in range(4):
         CSM[i] = (CG[2 * i + c, 0:LP].astype(F32) + CRM[i].astype(F32)).astype(BF)

time: 117 us -> 117 us (level)
  no operation moved by 1% of the time
where the time goes in v8:
time: 117 us; the launch traced here: 116 us
  Pallas kernels  115 us (98%)
  between operations  1.3 us (1%)
    pallas_call x1, Pallas kernels, body(): pl.pallas_call(kernel, name='block', out_shape=[jax.ShapeDtypeStruct((L,...  112 us
    pallas_call x1, Pallas kernels, body(): pl.pallas_call(finish, name='finish', out_shape=[jax.ShapeDtypeStruct((L,...  3.05 us

profile of v8, /device:TPU:1, one launch (start us, length us, event | category | flops | bytes accessed | tf_op | source)
XLA Modules:
  0.0 116.4 jit_solution(6608033806488416750)
XLA Ops:
  1.3 112.1 %block.1 = (bf16[197,512]{1,0:T(8,128)(2,1)}, f32[197,512]{1,0:T(8,128)}, f32[32,256]{1,0:T(8,128)}, f32[32,128]{1,0:T(8,128)}, bf16[8,4,32,512]{3,2,1,0:T(8,128)(2,1)}) custom-call(s32[1]{0:T(128)S(6)} %copy.20.cnt, bf16[197,512]{1,0:T(8,128)(2,1)} %tok.1, bf16[197,512]{1,0:T(8,128)(2,1)} %cot.1, s32[2,1576]{1,0:T(2,128)} %bitcast.12, ...), custom_call_target="tpu_custom_call" | custom-call | tf_op jit(solution)/shard_map/block/pallas_call | solution.py:809
  113.4 3.0 %finish.1 = (bf16[197,512]{1,0:T(8,128)(2,1)}, f32[197,512]{1,0:T(8,128)}, f32[32,32,256]{2,1,0:T(8,128)}, f32[32,32,256]{2,1,0:T(8,128)}, f32[32,192]{1,0:T(8,1...) custom-call(bf16[32,32,512]{2,1,0:T(8,128)(2,1)} %bitcast.10, ...), custom_call_target="tpu_custom_call" | custom-call | tf_op jit(solution)/shard_map/finish/pallas_call | solution.py:829
